TPU v7x, 128 devices: a whole 4x4x4 slice. The times are simulated.
128 devices in a mesh: pipe: 4 (over x), chan: 8 (over y_hi, z), dp: 4 (over y_lo, core).
Axes of the slice: x: 4, y: 4 (y_hi: 2, y_lo: 2; y = y_hi * 2 + y_lo), z: 4, core: 2. Of those that a mesh axis runs over, the one named last changes fastest.
Arguments:
- tokens: bfloat16 [2, 1152, 512], P(None, 'dp', 'chan'), may hold values from -6 to 6
- seq_lengths: int32 [2, 2], replicated, may hold values from 1 to 1151, as said below
- out_cot: bfloat16 [2, 1152, 512], P(None, 'dp', 'chan'), may hold values from -6 to 6
- s4_vectors: float32 [4, 4, 512], P('pipe', None, 'chan'), may hold values from -7 to 2, as said below
- s4_modes: float32 [4, 8, 512, 32], P('pipe', None, 'chan'), may hold values from -4 to 128, as said below
- glu_weight: bfloat16 [4, 512, 2, 512], P('pipe', None, None, 'chan'), may hold values from -0.5 to 0.5
- glu_bias: float32 [4, 2, 512], P('pipe', None, 'chan'), may hold values from -3 to 3
- ffn_vectors: float32 [4, 3, 512], P('pipe', None, 'chan'), may hold values from -1 to 2, as said below
- up_weight: bfloat16 [4, 512, 2048], P('pipe', None, 'chan'), may hold values from -0.25 to 0.25
- up_bias: bfloat16 [4, 2048], P('pipe', 'chan'), may hold values from -3 to 3
- down_weight: bfloat16 [4, 2048, 512], P('pipe', 'chan'), may hold values from -0.125 to 0.125
Outputs:
- hidden_states: bfloat16 [4, 2, 1152, 512], P('pipe', None, 'dp', 'chan')
- input_grads: bfloat16 [4, 2, 1152, 512], P('pipe', None, 'dp', 'chan')
- grad_s4_vectors: float32 [4, 4, 512], P('pipe', None, 'chan')
- grad_s4_modes: float32 [4, 8, 512, 32], P('pipe', None, 'chan')
- grad_glu_weight: float32 [4, 512, 2, 512], P('pipe', None, None, 'chan')
- grad_glu_bias: float32 [4, 2, 512], P('pipe', None, 'chan')
- grad_ffn_vectors: float32 [4, 3, 512], P('pipe', None, 'chan')
- grad_up_weight: float32 [4, 512, 2048], P('pipe', None, 'chan')
- grad_up_bias: float32 [4, 2048], P('pipe', 'chan')
- grad_down_weight: float32 [4, 2048, 512], P('pipe', 'chan')
Inputs may be any that keep to these rules, and one draw needn't show every extreme that they name: `seq_lengths`: the 2 lengths of each micro-batch sum to 1152; in each micro-batch one of the sequences has 1080 tokens or more, so it has tokens on every index of dp. `s4_vectors`: row 2 lies between log(0.001) and log(0.01); row 0 lies between 0.5 and 2. `s4_modes`: row 0 lies between 0.3 and 10, row 1 between 0 and pi * 32. `ffn_vectors`: row 0 lies between 0.5 and 2.
All inputs are finite; a program needn't handle non-finite values.
Results may differ from a plain program's by a relative error of at most 0.033.
Values may be sent and summed in bfloat16 or wider, within the bound.
A program may use at most 192 MiB of HBM per device.

v0:
```python
import math

import jax
import jax.numpy as jnp
from jax import lax
from jax.sharding import PartitionSpec as P

norm_eps = 1e-05
highest = lax.Precision.HIGHEST


def passed_along(x, axis, by):
    peers = lax.axis_size(axis)
    pairs = [(i, i + by) for i in range(peers) if 0 <= i + by < peers]
    return lax.ppermute(x, axis, pairs)


def complex_mul(left_real, left_imag, right_real, right_imag):
    return (
        left_real * right_real - left_imag * right_imag,
        left_real * right_imag + left_imag * right_real,
    )


def complex_div(left_real, left_imag, right_real, right_imag):
    modulus = right_real * right_real + right_imag * right_imag
    return (
        (left_real * right_real + left_imag * right_imag) / modulus,
        (left_imag * right_real - left_real * right_imag) / modulus,
    )


def cauchy_spectrum(steps_log, mode_values, length):
    step_size = jnp.exp(steps_log)[:, None, None]
    angles = 2.0 * math.pi / length * jnp.arange(length, dtype=jnp.float32)
    cosine = jnp.cos(angles)
    sine_vals = jnp.sin(angles)
    decays = mode_values[0][:, :, None]
    rotate = mode_values[1][:, :, None]
    rank_real, rank_imag = (mode_values[2][:, :, None], mode_values[3][:, :, None])
    input_real, input_imag = (mode_values[4][:, :, None], mode_values[5][:, :, None])
    output_real, output_imag = (mode_values[6][:, :, None], mode_values[7][:, :, None])
    coeffs = [
        complex_mul(output_real, output_imag, input_real, input_imag),
        complex_mul(output_real, output_imag, rank_real, rank_imag),
        complex_mul(rank_real, -rank_imag, input_real, input_imag),
        (rank_real * rank_real + rank_imag * rank_imag, jnp.zeros_like(rank_real)),
    ]
    sums_real = [0.0, 0.0, 0.0, 0.0]
    sums_imag = [0.0, 0.0, 0.0, 0.0]
    for conj_sign in (1.0, -1.0):
        imag_rate = conj_sign * rotate
        den_real = (
            2.0 / step_size * (1.0 - cosine) + (1.0 + cosine) * decays - sine_vals * imag_rate
        )
        den_imag = 2.0 / step_size * sine_vals - (1.0 + cosine) * imag_rate - sine_vals * decays
        for number in range(4):
            term_real, term_imag = complex_div(
                2.0 * coeffs[number][0], 2.0 * conj_sign * coeffs[number][1], den_real, den_imag
            )
            sums_real[number] = sums_real[number] + jnp.sum(term_real, axis=1)
            sums_imag[number] = sums_imag[number] + jnp.sum(term_imag, axis=1)
    half_real = (1.0 + cosine) / 2.0
    half_imag = -sine_vals / 2.0
    weight_real, weight_imag = complex_mul(half_real, half_imag, sums_real[3], sums_imag[3])
    cross_real, cross_imag = complex_mul(sums_real[1], sums_imag[1], sums_real[2], sums_imag[2])
    numer_real, numer_imag = complex_mul(half_real, half_imag, cross_real, cross_imag)
    fix_real, fix_imag = complex_div(numer_real, numer_imag, 1.0 + weight_real, weight_imag)
    return (sums_real[0] - fix_real, sums_imag[0] - fix_imag)


def fourier_tables(length):
    time_index = jnp.arange(length, dtype=jnp.int32)
    freq_index = jnp.arange(2 * length, dtype=jnp.int32)
    phases = time_index[:, None] * freq_index[None, :] % (2 * length)
    angles = phases.astype(jnp.float32) * (math.pi / length)
    forward_table = jnp.concatenate([jnp.cos(angles), -jnp.sin(angles)], axis=1)
    short_phases = time_index[:, None] * time_index[None, :] % length
    short_angles = short_phases.astype(jnp.float32) * (2.0 * math.pi / length)
    inverse_table = (
        jnp.concatenate([jnp.cos(short_angles), -jnp.sin(short_angles)], axis=0) / length
    )
    return (forward_table, inverse_table)


def kernel_spectrum(steps_log, mode_values, forward_table, inverse_table, block_size):
    length = inverse_table.shape[1]
    block_count = steps_log.shape[0] // block_size
    blocked_modes = jnp.moveaxis(
        mode_values.reshape(8, block_count, block_size, mode_values.shape[2]), 1, 0
    )

    def one_block(operands):
        spec_real, spec_imag = cauchy_spectrum(operands[0], operands[1], length)
        return jnp.dot(
            jnp.concatenate([spec_real, spec_imag], axis=1), inverse_table, precision=highest
        )

    kernels = lax.map(
        jax.checkpoint(one_block), (steps_log.reshape(block_count, block_size), blocked_modes)
    )
    return jnp.dot(
        kernels.reshape(block_count * block_size, length), forward_table, precision=highest
    )


def body(
    tokens,
    seq_lengths,
    out_cot,
    s4_vectors,
    s4_modes,
    glu_weight,
    glu_bias,
    ffn_vectors,
    up_weight,
    up_bias,
    down_weight,
):
    sections = lax.axis_size("pipe")
    groups = lax.axis_size("dp")
    section_index = lax.axis_index("pipe")
    data_index = lax.axis_index("dp")
    micro_count = tokens.shape[0]
    tok_rows = tokens.shape[1]
    chan_width = tokens.shape[2]
    model_width = glu_weight.shape[1]
    segments = seq_lengths.shape[1]
    length = tok_rows * groups
    offset = data_index * tok_rows
    forward_table, inverse_table = fourier_tables(length)
    local_table = lax.dynamic_slice_in_dim(forward_table, offset, tok_rows, 0)
    local_turn = local_table.T
    local_back = local_turn / (2.0 * length)
    vectors = s4_vectors[0]
    gain_one, bias_one, log_step, skip_gain = (vectors[0], vectors[1], vectors[2], vectors[3])
    modes = s4_modes[0]
    glu_matrix = glu_weight[0].reshape(model_width, 2 * chan_width)
    glu_offset = glu_bias[0].reshape(2 * chan_width)
    ffn_params = ffn_vectors[0]
    gain_two, bias_two, out_bias = (ffn_params[0], ffn_params[1], ffn_params[2])
    up_matrix = up_weight[0]
    up_offset = up_bias[0]
    down_matrix = down_weight[0]
    block_size = math.gcd(chan_width, 16)

    def spectrum_of(steps_log, mode_values):
        return kernel_spectrum(steps_log, mode_values, forward_table, inverse_table, block_size)

    kernel_freq = spectrum_of(log_step, modes)
    kernel_real = kernel_freq[:, : 2 * length]
    kernel_imag = kernel_freq[:, 2 * length :]
    ends = jnp.cumsum(seq_lengths, axis=1)
    begins = ends - seq_lengths
    positions = jnp.arange(length, dtype=jnp.int32)
    mask_table = (
        (positions[None, None, :] >= begins[:, :, None])
        & (positions[None, None, :] < ends[:, :, None])
    ).astype(jnp.float32)

    def row_sums(first_part, second_part):
        return lax.psum((first_part, second_part), "chan")

    def gather_features(values_low):
        return lax.all_gather(values_low, "chan", axis=1, tiled=True)

    def sum_features(partial_sum):
        return lax.psum_scatter(partial_sum, "chan", scatter_dimension=1, tiled=True)

    def norm_forward(values, gain_vec, bias_vec):
        totals, squares = row_sums(jnp.sum(values, axis=1), jnp.sum(values * values, axis=1))
        average = totals / model_width
        spread = squares / model_width - average * average
        inverse_std = lax.rsqrt(spread + norm_eps)
        normal_hat = (values - average[:, None]) * inverse_std[:, None]
        return (normal_hat * gain_vec + bias_vec, normal_hat, inverse_std)

    def norm_backward(grad_normed, normal_hat, inverse_std, gain_vec):
        grad_hat = grad_normed * gain_vec
        first_sum, second_sum = row_sums(
            jnp.sum(grad_hat, axis=1), jnp.sum(grad_hat * normal_hat, axis=1)
        )
        grad_in = inverse_std[:, None] * (
            grad_hat
            - first_sum[:, None] / model_width
            - normal_hat * second_sum[:, None] / model_width
        )
        return (grad_in, jnp.sum(grad_normed * normal_hat, axis=0), jnp.sum(grad_normed, axis=0))

    def sequence_conv(values_low, micro_masks, local_masks):
        cols_low = values_low.T
        whole_seq = lax.all_gather(cols_low, "dp", axis=1, tiled=True).astype(jnp.float32)
        pieces = (micro_masks[:, None, :] * whole_seq[None, :, :]).reshape(
            segments * chan_width, length
        )
        spectrum = jnp.dot(pieces, forward_table, precision=highest)
        spectrum = spectrum.reshape(segments, chan_width, 4 * length)
        prod_real, prod_imag = complex_mul(
            spectrum[..., : 2 * length], spectrum[..., 2 * length :], kernel_real, kernel_imag
        )
        inverse = jnp.dot(
            jnp.concatenate([prod_real, prod_imag], axis=2).reshape(
                segments * chan_width, 4 * length
            ),
            local_back,
            precision=highest,
        )
        inverse = inverse.reshape(segments, chan_width, tok_rows)
        return (jnp.sum(local_masks[:, None, :] * inverse, axis=0).T, spectrum)

    def layer_forward(residual, micro_idx, kept_conv):
        micro_masks = lax.dynamic_index_in_dim(mask_table, micro_idx, 0, keepdims=False)
        local_masks = lax.dynamic_slice_in_dim(micro_masks, offset, tok_rows, 1)
        normed, hat_one, inv_one = norm_forward(residual, gain_one, bias_one)
        conv_in = normed.astype(jnp.bfloat16)
        if kept_conv is None:
            conv_part, spectrum = sequence_conv(conv_in, micro_masks, local_masks)
        else:
            conv_part, spectrum = kept_conv
        conv_in_wide = conv_in.astype(jnp.float32)
        conv_out = conv_part + skip_gain * conv_in_wide
        gated = jax.nn.gelu(conv_out).astype(jnp.bfloat16)
        gated_full = gather_features(gated)
        glu_pre = jnp.dot(gated_full, glu_matrix, preferred_element_type=jnp.float32) + glu_offset
        residual_mid = residual + glu_pre[:, :chan_width] * jax.nn.sigmoid(glu_pre[:, chan_width:])
        normed_two, hat_two, inv_two = norm_forward(residual_mid, gain_two, bias_two)
        ffn_in = normed_two.astype(jnp.bfloat16)
        ffn_rows = gather_features(ffn_in)
        hidden = jnp.dot(
            ffn_rows, up_matrix, preferred_element_type=jnp.float32
        ) + up_offset.astype(jnp.float32)
        active = jax.nn.gelu(hidden).astype(jnp.bfloat16)
        branch = sum_features(jnp.dot(active, down_matrix, preferred_element_type=jnp.float32))
        layer_out = residual_mid + branch + out_bias
        saved = (
            micro_masks,
            local_masks,
            hat_one,
            inv_one,
            spectrum,
            conv_in_wide,
            conv_out,
            gated_full,
            glu_pre,
            hat_two,
            inv_two,
            ffn_rows,
            hidden,
            active,
            conv_part,
        )
        return (layer_out, saved)

    tick_count = micro_count + sections - 1
    hidden_store = jnp.zeros((micro_count, tok_rows, chan_width), jnp.bfloat16)
    kept_inputs = jnp.zeros((micro_count, tok_rows, chan_width), jnp.bfloat16)
    spectrum_store = jnp.zeros((micro_count, segments, chan_width, 4 * length), jnp.float32)
    conv_store = jnp.zeros((micro_count, tok_rows, chan_width), jnp.float32)
    outgoing = jnp.zeros((tok_rows, chan_width), jnp.bfloat16)
    for tick_num in range(tick_count):
        micro_idx = tick_num - section_index
        is_valid = (micro_idx >= 0) & (micro_idx < micro_count)
        slot_idx = jnp.clip(micro_idx, 0, micro_count - 1)
        own_input = lax.dynamic_index_in_dim(tokens, slot_idx, 0, keepdims=False)
        if tick_num > 0:
            arriving = passed_along(outgoing, "pipe", 1)
            current = jnp.where(section_index == 0, own_input, arriving)
        else:
            current = own_input
        kept_inputs = jnp.where(
            is_valid,
            lax.dynamic_update_index_in_dim(kept_inputs, current, slot_idx, 0),
            kept_inputs,
        )
        layer_out, saved = layer_forward(current.astype(jnp.float32), slot_idx, None)
        result = layer_out.astype(jnp.bfloat16)
        hidden_store = jnp.where(
            is_valid,
            lax.dynamic_update_index_in_dim(hidden_store, result, slot_idx, 0),
            hidden_store,
        )
        spectrum_store = jnp.where(
            is_valid,
            lax.dynamic_update_index_in_dim(spectrum_store, saved[4], slot_idx, 0),
            spectrum_store,
        )
        conv_store = jnp.where(
            is_valid,
            lax.dynamic_update_index_in_dim(conv_store, saved[14], slot_idx, 0),
            conv_store,
        )
        outgoing = result
    grad_store = jnp.zeros((micro_count, tok_rows, chan_width), jnp.bfloat16)
    returning = jnp.zeros((tok_rows, chan_width), jnp.bfloat16)
    totals = None
    for tick_num in range(tick_count):
        micro_idx = tick_num - (sections - 1 - section_index)
        is_valid = (micro_idx >= 0) & (micro_idx < micro_count)
        slot_idx = jnp.clip(micro_idx, 0, micro_count - 1)
        own_grad = lax.dynamic_index_in_dim(out_cot, slot_idx, 0, keepdims=False)
        if tick_num > 0:
            arriving = passed_along(returning, "pipe", -1)
            incoming = jnp.where(section_index == sections - 1, own_grad, arriving)
        else:
            incoming = own_grad
        current = lax.dynamic_index_in_dim(kept_inputs, slot_idx, 0, keepdims=False)
        kept_conv = (
            lax.dynamic_index_in_dim(conv_store, slot_idx, 0, keepdims=False),
            lax.dynamic_index_in_dim(spectrum_store, slot_idx, 0, keepdims=False),
        )
        layer_grad_out = incoming.astype(jnp.float32)
        unused, layer_saved = layer_forward(current.astype(jnp.float32), slot_idx, kept_conv)
        (
            layer_micro_masks,
            layer_local_masks,
            layer_hat_one,
            layer_inv_one,
            layer_spectrum,
            layer_conv_in_wide,
            layer_conv_out,
            layer_gated_full,
            layer_glu_pre,
            layer_hat_two,
            layer_inv_two,
            layer_ffn_rows,
            layer_hidden,
            layer_active,
            layer_conv_part,
        ) = layer_saved
        grad_out_bias = jnp.sum(layer_grad_out, axis=0)
        branch_grad = layer_grad_out.astype(jnp.bfloat16)
        grad_rows = gather_features(branch_grad)
        grad_active = jnp.einsum(
            "tj,ij->ti", grad_rows, down_matrix, preferred_element_type=jnp.float32
        )
        grad_down = jnp.einsum(
            "ti,tj->ij", layer_active, grad_rows, preferred_element_type=jnp.float32
        )
        grad_hidden = jax.vjp(jax.nn.gelu, layer_hidden)[1](grad_active)[0].astype(jnp.bfloat16)
        grad_up_off = jnp.sum(grad_hidden.astype(jnp.float32), axis=0)
        grad_up = jnp.einsum(
            "ti,tj->ij", layer_ffn_rows, grad_hidden, preferred_element_type=jnp.float32
        )
        grad_ffn_in = sum_features(
            jnp.einsum("tj,ij->ti", grad_hidden, up_matrix, preferred_element_type=jnp.float32)
        )
        back_two, grad_gain_two, grad_bias_two = norm_backward(
            grad_ffn_in, layer_hat_two, layer_inv_two, gain_two
        )
        grad_mid = layer_grad_out + back_two
        gate_sig = jax.nn.sigmoid(layer_glu_pre[:, chan_width:])
        value_part = layer_glu_pre[:, :chan_width]
        grad_pre = jnp.concatenate(
            [grad_mid * gate_sig, grad_mid * value_part * gate_sig * (1.0 - gate_sig)], axis=1
        ).astype(jnp.bfloat16)
        grad_glu_off = jnp.sum(grad_pre.astype(jnp.float32), axis=0)
        grad_glu = jnp.einsum(
            "ti,tj->ij", layer_gated_full, grad_pre, preferred_element_type=jnp.float32
        )
        grad_gated = sum_features(
            jnp.einsum("tj,ij->ti", grad_pre, glu_matrix, preferred_element_type=jnp.float32)
        )
        grad_conv = jax.vjp(jax.nn.gelu, layer_conv_out)[1](grad_gated)[0]
        grad_cols = grad_conv.T
        whole_grad = lax.all_gather(grad_cols, "dp", axis=1, tiled=True)
        sequence_pieces = (layer_micro_masks[:, None, :] * whole_grad[None, :, :]).reshape(
            segments * chan_width, length
        )
        grad_spec = jnp.dot(sequence_pieces, forward_table, precision=highest) / (2.0 * length)
        grad_spec = grad_spec.reshape(segments, chan_width, 4 * length)
        grad_real = grad_spec[..., : 2 * length]
        grad_imag = grad_spec[..., 2 * length :]
        spec_real = layer_spectrum[..., : 2 * length]
        spec_imag = layer_spectrum[..., 2 * length :]
        input_real = grad_real * kernel_real + grad_imag * kernel_imag
        input_imag = grad_imag * kernel_real - grad_real * kernel_imag
        kernel_grad_real = jnp.sum(grad_real * spec_real + grad_imag * spec_imag, axis=0)
        kernel_grad_imag = jnp.sum(grad_imag * spec_real - grad_real * spec_imag, axis=0)
        turned = jnp.dot(
            jnp.concatenate([input_real, input_imag], axis=2).reshape(
                segments * chan_width, 4 * length
            ),
            local_turn,
            precision=highest,
        )
        turned = turned.reshape(segments, chan_width, tok_rows)
        sequence_grad_in = jnp.sum(layer_local_masks[:, None, :] * turned, axis=0).T
        grad_kernel = jnp.concatenate([kernel_grad_real, kernel_grad_imag], axis=1)
        layer_grad_normed = sequence_grad_in + skip_gain * grad_conv
        grad_skip = jnp.sum(grad_conv * layer_conv_in_wide, axis=0)
        back_one, grad_gain_one, grad_bias_one = norm_backward(
            layer_grad_normed, layer_hat_one, layer_inv_one, gain_one
        )
        grad_residual = grad_mid + back_one
        grad_residual, grads_now = (
            grad_residual,
            (
                grad_gain_one,
                grad_bias_one,
                grad_skip,
                grad_glu,
                grad_glu_off,
                grad_gain_two,
                grad_bias_two,
                grad_out_bias,
                grad_up,
                grad_up_off,
                grad_down,
                grad_kernel,
            ),
        )
        grad_low = grad_residual.astype(jnp.bfloat16)
        grad_store = jnp.where(
            is_valid, lax.dynamic_update_index_in_dim(grad_store, grad_low, slot_idx, 0), grad_store
        )
        returning = grad_low
        masked = jax.tree.map(
            lambda member: jnp.where(is_valid, member, jnp.zeros_like(member)), grads_now
        )
        totals = masked if totals is None else jax.tree.map(jnp.add, totals, masked)
    (
        sum_gain_one,
        sum_bias_one,
        sum_skip,
        sum_glu,
        sum_glu_off,
        sum_gain_two,
        sum_bias_two,
        sum_out_bias,
        sum_up,
        sum_up_off,
        sum_down,
        sum_kernel,
    ) = totals
    reduced = lax.psum(
        (
            sum_gain_one,
            sum_bias_one,
            sum_skip,
            sum_glu,
            sum_glu_off,
            sum_gain_two,
            sum_bias_two,
            sum_out_bias,
            sum_up,
            sum_up_off,
            sum_down,
        ),
        "dp",
    )
    (
        red_gain_one,
        red_bias_one,
        red_skip,
        red_glu,
        red_glu_off,
        red_gain_two,
        red_bias_two,
        red_out_bias,
        red_up,
        red_up_off,
        red_down,
    ) = reduced
    step_grad, mode_grad = jax.vjp(spectrum_of, log_step, modes)[1](sum_kernel)
    grad_vectors = jnp.stack([red_gain_one, red_bias_one, step_grad, red_skip])[None]
    grad_glu_matrix = red_glu.reshape(model_width, 2, chan_width)[None]
    grad_glu_offset = red_glu_off.reshape(2, chan_width)[None]
    grad_ffn_params = jnp.stack([red_gain_two, red_bias_two, red_out_bias])[None]
    return (
        hidden_store[None],
        grad_store[None],
        grad_vectors,
        mode_grad[None],
        grad_glu_matrix,
        grad_glu_offset,
        grad_ffn_params,
        red_up[None],
        red_up_off[None],
        red_down[None],
    )


def solution(mesh):
    placed = (
        P(None, "dp", "chan"),
        P(),
        P(None, "dp", "chan"),
        P("pipe", None, "chan"),
        P("pipe", None, "chan", None),
        P("pipe", None, None, "chan"),
        P("pipe", None, "chan"),
        P("pipe", None, "chan"),
        P("pipe", None, "chan"),
        P("pipe", "chan"),
        P("pipe", "chan", None),
    )
    return jax.shard_map(
        body,
        mesh=mesh,
        in_specs=placed,
        out_specs=(
            P("pipe", None, "dp", "chan"),
            P("pipe", None, "dp", "chan"),
            P("pipe", None, "chan"),
            P("pipe", None, "chan", None),
            P("pipe", None, None, "chan"),
            P("pipe", None, "chan"),
            P("pipe", None, "chan"),
            P("pipe", None, "chan"),
            P("pipe", "chan"),
            P("pipe", "chan", None),
        ),
        check_vma=False,
    )
```

profile of v0, /device:TPU:1, one launch (start us, length us, event | category | flops | bytes accessed | tf_op | source)
XLA Modules:
  0.0 3430.0 jit_solution(17386039850456307260)
XLA Ops:
  31.8 44.7 %sine_negate_fusion = (f32[1152,2304]{1,0:T(8,128)}, f32[1152,2304]{1,0:T(8,128)}) fusion(), kind=kLoop, calls=%fused_computation.365 | loop fusion | flops 26542080 | bytes 21233664 | tf_op jit(solution)/shard_map/neg | solution.py:77
  120.2 101.9 %while.26 = (s32[]{:T(128)}, f32[4,16,1152]{2,1,0:T(8,128)S(1)}, f32[4,8,16,32]{3,2,1,0:T(8,128)S(1)}, f32[4,16]{1,0:T(4,128)S(1)}, f32[2304,1152]{1,0:T(8,128)}...) while((s32[]{:T(128)}, f32[4,16,1152]{2,1,0:T(8,128)S(1)}, ...), condition=%wide.region_22.23_spmd, body=%wide.region_5.22_spmd.sunk | while | flops 568709760 | bytes 14371789 | solution.py:99
  355.6 82.9 %reduce-scatter.46.cloned.1.call-done = f32[64,288]{1,0:T(8,128)} async-done(((f32[512,288]{1,0:T(8,128)}), f32[64,288]{1,0:T(8,128)}) %reduce-scatter.46.cloned.1.call-update) | async-done | bytes 73744
  584.2 30.3 all-gather
  618.7 47.9 %reduce-scatter.48.cloned.1.call-done = f32[64,288]{1,0:T(8,128)} async-done(((f32[512,288]{1,0:T(8,128)}), f32[64,288]{1,0:T(8,128)}) %reduce-scatter.48.cloned.1.call-update) | async-done | bytes 73744
  813.6 80.7 %reduce-scatter.50.cloned.1.call-done = f32[64,288]{1,0:T(8,128)} async-done(((f32[512,288]{1,0:T(8,128)}), f32[64,288]{1,0:T(8,128)}) %reduce-scatter.50.cloned.1.call-update) | async-done | bytes 73744
  1040.4 81.4 %reduce-scatter.52.cloned.1.call-done = f32[64,288]{1,0:T(8,128)} async-done(((f32[512,288]{1,0:T(8,128)}), f32[64,288]{1,0:T(8,128)}) %reduce-scatter.52.cloned.1.call-update) | async-done | bytes 73744
  1271.5 81.4 %reduce-scatter.56.cloned.1.call-done = f32[64,288]{1,0:T(8,128)} async-done(((f32[512,288]{1,0:T(8,128)}), f32[64,288]{1,0:T(8,128)}) %reduce-scatter.56.cloned.1.call-update) | async-done | bytes 73744
  1388.0 61.7 %reduce-scatter.58.cloned.1.call-done = f32[64,288]{1,0:T(8,128)} async-done(((f32[512,288]{1,0:T(8,128)}), f32[64,288]{1,0:T(8,128)}) %reduce-scatter.58.cloned.1.call-update) | async-done | bytes 73744
  1640.2 94.3 %reduce-scatter.60.cloned.1.call-done = f32[64,288]{1,0:T(8,128)} async-done(((f32[512,288]{1,0:T(8,128)}), f32[64,288]{1,0:T(8,128)}) %reduce-scatter.60.cloned.1.call-update) | async-done | bytes 73744
  1764.4 70.9 %reduce-scatter.62.cloned.1.call-done = f32[64,288]{1,0:T(8,128)} async-done(((f32[512,288]{1,0:T(8,128)}), f32[64,288]{1,0:T(8,128)}) %reduce-scatter.62.cloned.1.call-update) | async-done | bytes 73744
  1852.8 28.9 all_gather.128
  2017.4 90.9 %reduce-scatter.64.cloned.1.call-done = f32[64,288]{1,0:T(8,128)} async-done(((f32[512,288]{1,0:T(8,128)}), f32[64,288]{1,0:T(8,128)}) %reduce-scatter.64.cloned.1.call-update) | async-done | bytes 73744
  2138.4 71.2 %reduce-scatter.66.cloned.1.call-done = f32[64,288]{1,0:T(8,128)} async-done(((f32[512,288]{1,0:T(8,128)}), f32[64,288]{1,0:T(8,128)}) %reduce-scatter.66.cloned.1.call-update) | async-done | bytes 73744
  2227.0 28.8 all_gather.132
  2392.6 90.2 %reduce-scatter.68.cloned.1.call-done = f32[64,288]{1,0:T(8,128)} async-done(((f32[512,288]{1,0:T(8,128)}), f32[64,288]{1,0:T(8,128)}) %reduce-scatter.68.cloned.1.call-update) | async-done | bytes 73744
  2517.1 65.1 %reduce-scatter.70.cloned.1.call-done = f32[64,288]{1,0:T(8,128)} async-done(((f32[512,288]{1,0:T(8,128)}), f32[64,288]{1,0:T(8,128)}) %reduce-scatter.70.cloned.1.call-update) | async-done | bytes 73744
  2751.7 82.5 %reduce-scatter.72.cloned.1.call-done = f32[64,288]{1,0:T(8,128)} async-done(((f32[512,288]{1,0:T(8,128)}), f32[64,288]{1,0:T(8,128)}) %reduce-scatter.72.cloned.1.call-update) | async-done | bytes 73744
  2869.8 61.7 %reduce-scatter.74.cloned.1.call-done = f32[64,288]{1,0:T(8,128)} async-done(((f32[512,288]{1,0:T(8,128)}), f32[64,288]{1,0:T(8,128)}) %reduce-scatter.74.cloned.1.call-update) | async-done | bytes 73744
  3090.1 300.6 %while.27 = (s32[]{:T(128)}, f32[4,16]{1,0:T(4,128)S(1)}, f32[4,8,16,32]{3,2,1,0:T(8,128)S(1)}, f32[4,16]{1,0:T(4,128)}, f32[4,8,16,32]{3,2,1,0:T(8,128)}, /*ind...) while((s32[]{:T(128)}, f32[4,16]{1,0:T(4,128)S(1)}, ...), condition=%wide.region_243.244_spmd, body=%wide.region_186.243_spmd.sunk | while | flops 801195392 | bytes 19305156 | solution.py:99
  3135.5 29.6 multiply_reduce_fusion.75
  3210.5 29.6 multiply_reduce_fusion.75
  3285.6 29.6 multiply_reduce_fusion.75
  3360.7 29.6 multiply_reduce_fusion.75
  (1042 shorter events, 2098.2 us)
Async XLA Ops:
  7.2 431.2 %reduce-scatter.46.cloned.1.call-start = ((), (), s32[]{:S(2)}) async-start(), calls=%async_computation.15 | async-start | bytes 884736
  355.5 311.1 %reduce-scatter.48.cloned.1.call-start = ((), (), s32[]{:S(2)}) async-start(), calls=%async_computation.16 | async-start | bytes 884736
  439.5 4.5 collective-permute-start
  581.5 312.7 %reduce-scatter.50.cloned.1.call-start = ((), (), s32[]{:S(2)}) async-start(), calls=%async_computation.17 | async-start | bytes 884736
  667.7 4.5 collective-permute-start.1
  809.5 312.3 %reduce-scatter.52.cloned.1.call-start = ((), (), s32[]{:S(2)}) async-start(), calls=%async_computation.18 | async-start | bytes 884736
  895.3 4.5 collective-permute-start.2
  1037.1 315.8 %reduce-scatter.56.cloned.1.call-start = ((), (), s32[]{:S(2)}) async-start(), calls=%async_computation.20 | async-start | bytes 884736
  1122.9 4.5 collective-permute-start.3
  1268.2 181.5 %reduce-scatter.58.cloned.1.call-start = ((), (), s32[]{:S(2)}) async-start(), calls=%async_computation.21 | async-start | bytes 884736
  1375.7 358.8 %reduce-scatter.60.cloned.1.call-start = ((), (), s32[]{:S(2)}) async-start(), calls=%async_computation.22 | async-start | bytes 884736
  1570.9 32.4 collective-permute-start.4
  1640.1 195.2 %reduce-scatter.62.cloned.1.call-start = ((), (), s32[]{:S(2)}) async-start(), calls=%async_computation.23 | async-start | bytes 884736
  1761.3 347.0 %reduce-scatter.64.cloned.1.call-start = ((), (), s32[]{:S(2)}) async-start(), calls=%async_computation.24 | async-start | bytes 884736
  1948.4 32.2 collective-permute-start.5
  2017.3 192.2 %reduce-scatter.66.cloned.1.call-start = ((), (), s32[]{:S(2)}) async-start(), calls=%async_computation.25 | async-start | bytes 884736
  2135.5 347.3 %reduce-scatter.68.cloned.1.call-start = ((), (), s32[]{:S(2)}) async-start(), calls=%async_computation.26 | async-start | bytes 884736
  2322.7 32.2 collective-permute-start.6
  2391.8 190.4 %reduce-scatter.70.cloned.1.call-start = ((), (), s32[]{:S(2)}) async-start(), calls=%async_computation.27 | async-start | bytes 884736
  2508.2 326.0 %reduce-scatter.72.cloned.1.call-start = ((), (), s32[]{:S(2)}) async-start(), calls=%async_computation.28 | async-start | bytes 884736
  2679.1 30.6 collective-permute-start.7
  2743.7 187.7 %reduce-scatter.74.cloned.1.call-start = ((), (), s32[]{:S(2)}) async-start(), calls=%async_computation.29 | async-start | bytes 884736
  2857.5 558.6 %reduce-scatter.54.cloned.1.call-start = ((), (), s32[]{:S(2)}) async-start(), calls=%async_computation.19 | async-start | bytes 884736
  3054.5 363.4 %all-reduce.33.cloned.1.call-start = ((), (), s32[]{:S(2)}) async-start(), calls=%async_computation.30 | async-start | bytes 2621440 | tf_op jit(solution)/shard_map/psum | solution.py:435
  (194 other events, 17556.1 us)
Sparse Core Ops, SparseCore 0:
  355.6 82.7 reduce-scatter.45
  581.7 84.9 reduce-scatter.47
  809.6 84.5 reduce-scatter.49
  1037.2 84.5 reduce-scatter.51
  1268.3 84.5 reduce-scatter.55
  1375.8 73.8 reduce-scatter.57
  1640.2 94.2 reduce-scatter.59
  1761.4 73.8 reduce-scatter.61
  2017.5 90.7 reduce-scatter.63
  2135.6 73.8 reduce-scatter.65
  2391.9 90.7 reduce-scatter.67
  2508.3 73.8 reduce-scatter.69
  2743.8 90.3 reduce-scatter.71
  2857.6 73.8 reduce-scatter.73
  3054.6 83.3 reduce-scatter.53
  3141.9 46.0 all-reduce.32
where the time goes:
time: 3440 us; the launch traced here: 3430 us
  blocking collectives  1220 us (35%)
  waiting for transfers between devices  1070 us (31%)
  other arithmetic  528 us (15%)
  matrix products  466 us (14%)
  local copies, waits for them, and re-layouts  115 us (3%)
    unnamed x31, waiting for transfers between devices  1060 us
    all_gather x25, blocking collectives, gather_features(): return lax.all_gather(values_low, 'chan', axis=1, tiled=True)  714 us
    psum x21, blocking collectives, row_sums(): return lax.psum((first_part, second_part), 'chan')  376 us
    reduce_sum x4, other arithmetic, complex_div(): left_real * right_imag  118 us
    dot_general x5, matrix products, sequence_conv(): spectrum = jnp.dot(pieces, forward_table, precision=highest)  98.8 us
    dot_general x5, matrix products, body(): jnp.dot(sequence_pieces, forward_table, precision=highest) / (2.0 * length)  95.3 us
    reduce_sum x4, other arithmetic, cauchy_spectrum(): sums_imag[number] = sums_imag[number] + jnp.sum(term_imag, axis=1)  85.1 us
    dot_general x8, matrix products, one_block(): jnp.dot(jnp.concatenate([spec_real, spec_imag], axis=1), inverse_table, p...  73.8 us
  transfers between devices with their start and end apart: 24, of which 18 were waited for; matrix products, arithmetic and copies ran while one was open for 12% of the time, Pallas kernels for 0%

commit v1 on v0

v1 whole, which is shorter than its diff:
```python
import math

import jax
import jax.numpy as jnp
import numpy as np
from jax import lax
from jax.experimental import pallas as pl
from jax.experimental.pallas import tpu as pltpu
from jax.sharding import PartitionSpec as P

norm_eps = 1e-05
highest = lax.Precision.HIGHEST
f32 = jnp.float32
bf16 = jnp.bfloat16
LANES = 128


def fourier_table(length, padded):
    half = length // 2
    freq = np.arange(padded, dtype=np.int64)[:, None]
    time = np.arange(length, dtype=np.int64)[None, :]
    angle = (freq * (2 * time + 1) % (2 * length)) * (np.pi / length)
    weight = np.where(freq <= half, np.where((freq == 0) | (freq == half), 1.0, 2.0), 0.0) / length
    table = np.concatenate([np.cos(angle) * weight, -np.sin(angle) * weight], axis=0)
    return table.astype(np.float32)


def half_angles(length, padded):
    angle = np.minimum(np.arange(padded), length // 2) * (np.pi / length)
    cosine = np.cos(angle)
    cosine[length // 2 :] = 0.0
    return cosine.astype(np.float32), np.sin(angle).astype(np.float32)


def kernel_of(log_step, modes, length, padded):
    cosine, sine = half_angles(length, padded)
    cosine, sine = jnp.asarray(cosine), jnp.asarray(sine)
    decay, rate = modes[0], modes[1]
    rank_r, rank_i, in_r, in_i, out_r, out_i = (modes[i] for i in range(2, 8))
    vals = [
        (out_r * in_r - out_i * in_i, out_r * in_i + out_i * in_r),
        (out_r * rank_r - out_i * rank_i, out_r * rank_i + out_i * rank_r),
        (rank_r * in_r + rank_i * in_i, rank_r * in_i - rank_i * in_r),
        (rank_r * rank_r + rank_i * rank_i, jnp.zeros_like(rank_r)),
    ]
    rise = (2.0 * jnp.exp(-log_step))[:, None] * sine[None, :]
    square = cosine * cosine
    den_r = (decay * decay + rate * rate)[:, :, None] * square - (rise * rise)[:, None, :]
    den_i = 2.0 * decay[:, :, None] * (cosine * rise)[:, None, :]
    inverse = 1.0 / (den_r * den_r + den_i * den_i)
    den = jnp.concatenate([den_r * inverse, den_i * inverse], axis=2)
    alpha = jnp.stack([decay * v_r - rate * v_i for v_r, v_i in vals], axis=1)
    beta = jnp.stack([v_r for v_r, v_i in vals], axis=1)
    sums = jnp.einsum(
        "hvn,hnj->hvj", jnp.concatenate([alpha, beta], axis=1), den, precision=highest
    )
    parts = []
    for v in range(4):
        a_u, a_w = sums[:, v, :padded], sums[:, v, padded:]
        b_u, b_w = sums[:, 4 + v, :padded], sums[:, 4 + v, padded:]
        parts.append((2.0 * (cosine * a_u + rise * b_w), 2.0 * (rise * b_u - cosine * a_w)))
    (m0r, m0i), (m1r, m1i), (m2r, m2i), (m3r, m3i) = parts
    top_r = cosine * (m1r * m2r - m1i * m2i)
    top_i = cosine * (m1r * m2i + m1i * m2r)
    low_r = 1.0 + cosine * m3r
    low_i = cosine * m3i
    size = 1.0 / (low_r * low_r + low_i * low_i)
    spec_r = m0r - (top_r * low_r + top_i * low_i) * size
    spec_i = m0i - (top_i * low_r - top_r * low_i) * size
    table = jnp.asarray(fourier_table(length, padded))
    return jnp.dot(jnp.concatenate([spec_r, spec_i], axis=1), table, precision=highest)


def shifted(x, by):
    size = x.shape[-1]
    by = by % size
    if by == 0:
        return x
    return pltpu.roll(x, by, x.ndim - 1)


def toeplitz_kernel(blocks, kern_ref, near_ref, far_ref):
    channels = kern_ref.shape[0]
    wide = kern_ref.shape[1]

    def step(h, carry):
        row = kern_ref[pl.ds(h, 1), :]
        full = jnp.broadcast_to(row, (LANES, wide))
        full = pltpu.roll(full, 0, 1, stride=1, stride_axis=0)
        low = full.astype(bf16)
        far_ref[h] = low[:, : blocks * LANES]
        for d in range(blocks):
            near_ref[h, d * LANES : (d + 1) * LANES, :] = low[:, d * LANES : (d + 1) * LANES]
        return carry

    lax.fori_loop(0, channels, step, 0)


def lag_kernel(blocks, x_ref, g_ref, out_ref):
    channels, groups = 16, 4
    stride = channels
    rows = 40
    wide = (blocks + 1) * LANES

    def step(h, carry):
        x = x_ref[pl.ds((blocks - 1) * groups * stride + h, rows, stride=stride), :]
        parts = [
            g_ref[pl.ds(d * groups * stride + h, rows, stride=stride), :] for d in range(blocks)
        ]
        g = jnp.concatenate(parts, axis=1)
        prod = lax.dot_general(
            x.astype(bf16), g.astype(bf16), (((0,), (0,)), ((), ())), preferred_element_type=f32
        )
        prod = jnp.concatenate([prod, jnp.zeros((LANES, LANES), f32)], axis=1)
        size = LANES // 2
        while size >= 8:
            prod = prod[:size] + shifted(prod[size:], wide - size)
            size //= 2
        row = prod[0:1]
        for a in range(1, 8):
            row = row + shifted(prod[a : a + 1], wide - a)
        out_ref[pl.ds(h, 1), :] = row
        return carry

    lax.fori_loop(0, channels, step, 0)


def gelu(x):
    return 0.5 * x * (1.0 + jnp.tanh(math.sqrt(2.0 / math.pi) * (x + 0.044715 * x * x * x)))


def gelu_slope(x):
    scale = math.sqrt(2.0 / math.pi)
    t = jnp.tanh(scale * (x + 0.044715 * x * x * x))
    return 0.5 * (1.0 + t) + 0.5 * x * (1.0 - t * t) * scale * (1.0 + 3.0 * 0.044715 * x * x)


def dot(a, b):
    return lax.dot_general(a, b, (((1,), (0,)), ((), ())), preferred_element_type=f32)


def dot_nt(a, b):
    return lax.dot_general(a, b, (((1,), (1,)), ((), ())), preferred_element_type=f32)


def dot_tn(a, b):
    return lax.dot_general(a, b, (((0,), (0,)), ((), ())), preferred_element_type=f32)


class Sizes:
    def __init__(self, sections, peers, groups, tok_rows, chan_width, model_width, hidden):
        self.sections, self.peers, self.groups = sections, peers, groups
        self.micros = 2
        self.segments = 2
        self.quarters = peers // self.micros
        self.tok = tok_rows // self.quarters
        self.rows = -(-self.tok // 16) * 16
        self.length = tok_rows * groups
        self.blocks = self.length // LANES
        self.width = model_width
        self.cw = chan_width
        self.hid = hidden
        self.members = peers * groups
        self.ch = model_width // self.members
        self.slots = self.quarters * groups
        self.gr = self.micros * self.segments
        self.stack = (2 * self.blocks) * self.gr * self.ch


def main_kernel(z, *refs):
    (tok_tx, cot_tx, vec_tx, glu_loc, up_loc, down_loc, near, far, skip, masks) = refs[:10]
    (hid_out, ig_out, dglu, dup, ddown, vec_out, xs, gs) = refs[10:18]
    (
        vec_all, glu_all, up_all, down_all, tok_rx, cot_rx, res, gtop,
        tx1, rx1, tx2, rx2, tx3, rx3, tx4, rx4,
        conv_out, ys, hat1_s, inv1_s, hat2_s, inv2_s, val_s, sig_s, hidden_s,
        gated_s, ffn_s, act_s, gh_s, gp_s, lay_s, res_tx, ig_s, ig_tx, vg_s,
        ga, fi, ac, bg, gh, gp, vrx, send, recv,
    ) = refs[18:]
    pipe = lax.axis_index("pipe")
    chan = lax.axis_index("chan")
    data = lax.axis_index("dp")
    me = chan * z.groups + data
    slot_me = (chan // z.quarters) * z.slots + data * z.quarters + lax.rem(chan, z.quarters)
    rows, width, tok = z.rows, z.width, z.tok
    lane = lax.broadcasted_iota(jnp.int32, (1, LANES), 1)
    first_half = lane < (LANES // 2)
    row_ok = lax.broadcasted_iota(jnp.int32, (rows, 1), 0) < tok

    def slot_of(p):
        c, d = p // z.groups, lax.rem(p, z.groups)
        return (c // z.quarters) * z.slots + d * z.quarters + lax.rem(c, z.quarters)

    def member(p):
        return {"pipe": pipe, "chan": p // z.groups, "dp": lax.rem(p, z.groups)}

    def remote(src, dst, phase, where):
        return pltpu.make_async_remote_copy(
            src_ref=src,
            dst_ref=dst,
            send_sem=send.at[phase],
            recv_sem=recv.at[phase],
            device_id=where,
            device_id_type=pl.DeviceIdType.MESH,
        )

    def wait_bytes(ref, sem):
        pltpu.make_async_copy(ref, ref, sem).wait()

    def to_peers(src_of, dst, phase):
        def step(k, carry):
            c = lax.rem(chan + k, z.peers)
            remote(src_of(c), dst.at[chan], phase, {"pipe": pipe, "chan": c, "dp": data}).start()
            return carry

        lax.fori_loop(1, z.peers, step, 0)
        pltpu.make_async_copy(src_of(chan), dst.at[chan], recv.at[phase]).start()

    def to_members(src_of, dst, slot, phase):
        def step(k, carry):
            p = lax.rem(me + k, z.members)
            remote(src_of(p), dst.at[slot], phase, member(p)).start()
            return carry

        lax.fori_loop(1, z.members, step, 0)
        pltpu.make_async_copy(src_of(me), dst.at[slot], recv.at[phase]).start()

    (VEC, GLU, UP, DOWN, TOK, COT, A1, A2, A3, A4, RES, GTOP, HID, IG, GA, FI, AC, BG, GH, GP, VG) = range(21)

    barrier = pltpu.get_barrier_semaphore()

    def greet(k, carry):
        p = lax.rem(me + k, z.members)
        pl.semaphore_signal(
            barrier, inc=1, device_id=member(p), device_id_type=pl.DeviceIdType.MESH
        )
        return carry

    lax.fori_loop(1, z.members, greet, 0)
    later = {"pipe": lax.rem(pipe + 1, z.sections), "chan": chan, "dp": data}
    earlier = {"pipe": lax.rem(pipe + z.sections - 1, z.sections), "chan": chan, "dp": data}
    for neighbour in (later, earlier):
        pl.semaphore_signal(
            barrier, inc=1, device_id=neighbour, device_id_type=pl.DeviceIdType.MESH
        )
    pl.semaphore_wait(barrier, z.members - 1 + 2)

    to_peers(lambda c: vec_tx, vec_all, VEC)

    @pl.when(pipe == 0)
    def _():
        to_peers(lambda c: tok_tx.at[c], tok_rx, TOK)

    @pl.when(pipe == z.sections - 1)
    def _():
        to_peers(lambda c: cot_tx.at[c], cot_rx, COT)

    to_peers(lambda c: glu_loc, glu_all, GLU)
    to_peers(lambda c: up_loc, up_all, UP)
    to_peers(lambda c: down_loc, down_all, DOWN)

    pad_rows = (z.blocks - 1) * z.gr * z.ch
    data_rows = z.blocks * z.gr * z.ch
    xs[0:pad_rows, :] = jnp.zeros((pad_rows, LANES), f32)
    xs[pad_rows + data_rows : z.stack, :] = jnp.zeros(
        (z.stack - pad_rows - data_rows, LANES), f32
    )
    gs[data_rows : z.stack, :] = jnp.zeros((z.stack - data_rows, LANES), f32)

    wait_bytes(vec_all, recv.at[VEC])

    def full_row(r):
        tiles = [
            jnp.where(first_half, vec_all[2 * j, r : r + 1, :], vec_all[2 * j + 1, r : r + 1, :])
            for j in range(z.peers // 2)
        ]
        return jnp.concatenate(tiles, axis=1)

    gain1, bias1, gain2, bias2, out_bias = (full_row(r) for r in range(5))

    def norm_stats(v):
        mean = jnp.sum(v, axis=1, keepdims=True) * (1.0 / width)
        spread = jnp.sum(v * v, axis=1, keepdims=True) * (1.0 / width) - mean * mean
        inv = lax.rsqrt(spread + norm_eps)
        return (v - mean) * inv, inv

    def norm_back(e, hat, inv, gain):
        dh = e * gain
        first = jnp.sum(dh, axis=1, keepdims=True) * (1.0 / width)
        second = jnp.sum(dh * hat, axis=1, keepdims=True) * (1.0 / width)
        return inv * (dh - first - hat * second)

    def turn_out(v, ref):
        tall = jnp.concatenate([v, jnp.zeros((LANES - rows, width), f32)], axis=0)
        ref[...] = tall.T.astype(bf16).reshape(z.members, z.ch, LANES)

    def turn_in(ref):
        return ref[...].reshape(width, LANES).astype(f32).T[:rows]

    def lane_tiles(ref, m):
        tiles = []
        for i in range(z.blocks):
            lo, hi = i * LANES, (i + 1) * LANES
            tile = None
            for k in range(lo // tok, -(-hi // tok)):
                piece = shifted(ref[m * z.slots + k].astype(f32), k * tok - lo)
                first = max(0, k * tok - lo)
                if tile is None:
                    tile = piece
                else:
                    tile = jnp.where(lane >= first, piece, tile)
            tiles.append(tile)
        return tiles

    def lane_pieces(tiles, m, ref):
        for k in range(z.slots):
            i, off = divmod(k * tok, LANES)
            piece = shifted(tiles[i], LANES - off)
            if off + tok > LANES:
                piece = jnp.where(lane < LANES - off, piece, shifted(tiles[i + 1], LANES - off))
            ref[m * z.slots + k] = piece.astype(bf16)

    def row_at(i, g):
        return (i * z.gr + g) * z.ch

    def masked_store(ref, base, m, i, tile):
        for q in range(z.segments):
            g = m * z.segments + q
            at = base + row_at(i, g)
            ref[at : at + z.ch, :] = tile * masks[i * z.gr + g : i * z.gr + g + 1, :]

    def masked_sum(m, i):
        total = None
        for q in range(z.segments):
            g = m * z.segments + q
            at = row_at(i, g)
            part = ys[at : at + z.ch, :] * masks[i * z.gr + g : i * z.gr + g + 1, :]
            total = part if total is None else total + part
        return total

    conv_rows = -(-(z.blocks * z.gr) // 8) * 8

    @pl.when(pipe == 0)
    def _():
        wait_bytes(tok_rx, recv.at[TOK])
        for j in range(z.peers // 2):
            res[:, j * LANES : (j + 1) * LANES] = jnp.where(
                first_half, tok_rx[2 * j].astype(f32), tok_rx[2 * j + 1].astype(f32)
            ).astype(bf16)

    @pl.when(pipe > 0)
    def _():
        wait_bytes(res, recv.at[RES])

    hat1, inv1 = norm_stats(res[...].astype(f32))
    hat1_s[...] = hat1
    inv1_s[...] = jnp.broadcast_to(inv1, (rows, LANES))
    turn_out(hat1 * gain1 + bias1, tx1)
    to_members(lambda p: tx1.at[p], rx1, slot_me, A1)
    wait_bytes(rx1, recv.at[A1])
    for m in range(z.micros):
        for i, tile in enumerate(lane_tiles(rx1, m)):
            masked_store(xs, pad_rows, m, i, tile)

    def conv_step(h, carry):
        parts = [
            xs[pl.ds((z.blocks - 1 - d) * z.gr * z.ch + h, conv_rows, stride=z.ch), :]
            for d in range(z.blocks)
        ]
        windows = jnp.concatenate(parts, axis=1).astype(bf16)
        ys[pl.ds(h, conv_rows, stride=z.ch), :] = dot(windows, near[h])
        return carry

    lax.fori_loop(0, z.ch, conv_step, 0)
    for m in range(z.micros):
        tiles = []
        for i in range(z.blocks):
            own = None
            for q in range(z.segments):
                at = pad_rows + row_at(i, m * z.segments + q)
                own = xs[at : at + z.ch, :] if own is None else own + xs[at : at + z.ch, :]
            tile = masked_sum(m, i) + skip[...] * own
            conv_out[m * z.blocks + i] = tile
            tiles.append(gelu(tile))
        lane_pieces(tiles, m, tx2)
    to_members(lambda p: tx2.at[slot_of(p)], rx2, me, A2)
    wait_bytes(rx2, recv.at[A2])
    gated_s[...] = turn_in(rx2).astype(bf16)
    wait_bytes(glu_all, recv.at[GLU])
    gated = gated_s[...]
    values, gates = [], []
    for j in range(z.peers // 2):
        even = dot(gated, glu_all[2 * j]) + vec_all[2 * j, 5:6, :]
        odd = dot(gated, glu_all[2 * j + 1]) + vec_all[2 * j + 1, 5:6, :]
        values.append(jnp.where(first_half, even, odd))
        gates.append(shifted(jnp.where(first_half, odd, even), LANES // 2))
    value = jnp.concatenate(values, axis=1)
    sig = jax.nn.sigmoid(jnp.concatenate(gates, axis=1))
    val_s[...] = value
    sig_s[...] = sig
    mid = res[...].astype(f32) + value * sig
    hat2, inv2 = norm_stats(mid)
    hat2_s[...] = hat2
    inv2_s[...] = jnp.broadcast_to(inv2, (rows, LANES))
    ffn_s[...] = (hat2 * gain2 + bias2).astype(bf16)
    wait_bytes(up_all, recv.at[UP])
    wait_bytes(down_all, recv.at[DOWN])
    ffn_in = ffn_s[...]
    total = mid + out_bias
    per = z.hid // LANES
    for c in range(z.peers):
        offset = jnp.concatenate([vec_all[c, 6 + r : 7 + r, :] for r in range(per)], axis=1)
        hidden = dot(ffn_in, up_all[c]) + offset
        hidden_s[c] = hidden
        active = gelu(hidden).astype(bf16)
        act_s[c] = active
        total = total + dot(active, down_all[c])
    layer_out = jnp.where(row_ok, total, 0.0).astype(bf16)
    res_tx[...] = layer_out

    @pl.when(pipe < z.sections - 1)
    def _():
        remote(res_tx, res, RES, later).start()

    for j in range(z.peers // 2):
        lay_s[j] = layer_out[:, j * LANES : (j + 1) * LANES]
    to_peers(lambda c: lay_s.at[c // 2], hid_out, HID)
    to_peers(lambda c: gated_s, ga, GA)
    to_peers(lambda c: ffn_s, fi, FI)
    to_peers(lambda c: act_s.at[c], ac, AC)

    @pl.when(pipe == z.sections - 1)
    def _():
        wait_bytes(cot_rx, recv.at[COT])
        for j in range(z.peers // 2):
            gtop[:, j * LANES : (j + 1) * LANES] = jnp.where(
                first_half, cot_rx[2 * j].astype(f32), cot_rx[2 * j + 1].astype(f32)
            ).astype(bf16)

    @pl.when(pipe < z.sections - 1)
    def _():
        wait_bytes(gtop, recv.at[GTOP])

    grad_low = gtop[...]
    grad_top = grad_low.astype(f32)
    grad_ffn = None
    for c in range(z.peers):
        grad_active = dot_nt(grad_low, down_all[c])
        grad_hidden = (grad_active * gelu_slope(hidden_s[c])).astype(bf16)
        gh_s[c] = grad_hidden
        part = dot_nt(grad_hidden, up_all[c])
        grad_ffn = part if grad_ffn is None else grad_ffn + part
    hat2 = hat2_s[...]
    grad_mid = grad_top + norm_back(grad_ffn, hat2, inv2_s[:, 0:1], gain2)
    sig = sig_s[...]
    grad_value = grad_mid * sig
    grad_gate = grad_value * val_s[...] * (1.0 - sig)
    grad_gated = None
    for j in range(z.peers // 2):
        gv = grad_value[:, j * LANES : (j + 1) * LANES]
        gg = shifted(grad_gate[:, j * LANES : (j + 1) * LANES], LANES // 2)
        pair = (jnp.where(first_half, gv, gg), jnp.where(first_half, gg, gv))
        for half in range(2):
            low = pair[half].astype(bf16)
            gp_s[2 * j + half] = low
            part = dot_nt(low, glu_all[2 * j + half])
            grad_gated = part if grad_gated is None else grad_gated + part
    turn_out(grad_gated, tx3)
    to_members(lambda p: tx3.at[p], rx3, slot_me, A3)
    to_peers(lambda c: gtop, bg, BG)
    to_peers(lambda c: gh_s.at[c], gh, GH)
    to_peers(lambda c: gp_s.at[c], gp, GP)
    wait_bytes(rx3, recv.at[A3])
    for m in range(z.micros):
        for i, tile in enumerate(lane_tiles(rx3, m)):
            masked_store(gs, 0, m, i, tile * gelu_slope(conv_out[m * z.blocks + i]))

    def back_step(h, carry):
        parts = [
            gs[pl.ds(d * z.gr * z.ch + h, conv_rows, stride=z.ch), :] for d in range(z.blocks)
        ]
        windows = jnp.concatenate(parts, axis=1).astype(bf16)
        ys[pl.ds(h, conv_rows, stride=z.ch), :] = dot_nt(windows, far[h])
        return carry

    lax.fori_loop(0, z.ch, back_step, 0)
    for m in range(z.micros):
        tiles = []
        for i in range(z.blocks):
            own = None
            for q in range(z.segments):
                at = row_at(i, m * z.segments + q)
                own = gs[at : at + z.ch, :] if own is None else own + gs[at : at + z.ch, :]
            tiles.append(masked_sum(m, i) + skip[...] * own)
        lane_pieces(tiles, m, tx4)
    to_members(lambda p: tx4.at[slot_of(p)], rx4, me, A4)
    wait_bytes(rx4, recv.at[A4])
    grad_conv_in = jnp.where(row_ok, turn_in(rx4), 0.0)
    hat1 = hat1_s[...]
    grad_res = grad_mid + norm_back(grad_conv_in, hat1, inv1_s[:, 0:1], gain1)
    grad_res_low = grad_res.astype(bf16)
    ig_tx[...] = grad_res_low

    @pl.when(pipe > 0)
    def _():
        remote(ig_tx, gtop, GTOP, earlier).start()

    for j in range(z.peers // 2):
        ig_s[j] = grad_res_low[:, j * LANES : (j + 1) * LANES]
    to_peers(lambda c: ig_s.at[c // 2], ig_out, IG)

    rows_of = [
        jnp.sum(grad_conv_in * hat1, axis=0, keepdims=True),
        jnp.sum(grad_conv_in, axis=0, keepdims=True),
        jnp.sum(grad_ffn * hat2, axis=0, keepdims=True),
        jnp.sum(grad_ffn, axis=0, keepdims=True),
        jnp.sum(grad_top, axis=0, keepdims=True),
    ]
    for c in range(z.peers):
        j = c // 2
        for r, row in enumerate(rows_of):
            vg_s[c, r : r + 1, :] = row[:, j * LANES : (j + 1) * LANES]
        vg_s[c, 5:6, :] = jnp.sum(gp_s[c].astype(f32), axis=0, keepdims=True)
        up_row = jnp.sum(gh_s[c].astype(f32), axis=0, keepdims=True)
        for r in range(per):
            vg_s[c, 6 + r : 7 + r, :] = up_row[:, r * LANES : (r + 1) * LANES]
    to_peers(lambda c: vg_s.at[c], vrx, VG)
    wait_bytes(ga, recv.at[GA])
    wait_bytes(gp, recv.at[GP])
    many = z.peers * rows
    dglu[...] = dot_tn(ga[...].reshape(many, width), gp[...].reshape(many, 2 * z.cw))
    wait_bytes(fi, recv.at[FI])
    wait_bytes(gh, recv.at[GH])
    dup[...] = dot_tn(fi[...].reshape(many, width), gh[...].reshape(many, z.hid))
    wait_bytes(ac, recv.at[AC])
    wait_bytes(bg, recv.at[BG])
    ddown[...] = dot_tn(ac[...].reshape(many, z.hid), bg[...].reshape(many, width))
    wait_bytes(vrx, recv.at[VG])
    summed = vrx[0]
    for c in range(1, z.peers):
        summed = summed + vrx[c]
    vec_out[...] = summed
    wait_bytes(hid_out, recv.at[HID])
    wait_bytes(ig_out, recv.at[IG])

    for ref, phase in (
        (vec_all, VEC), (glu_all, GLU), (up_all, UP), (down_all, DOWN), (hid_out, HID),
        (ig_out, IG), (ga, GA), (fi, FI), (ac, AC), (bg, BG), (gh, GH), (gp, GP), (vrx, VG),
    ):
        wait_bytes(ref.at[pl.ds(0, z.peers - 1)], send.at[phase])
    for ref, phase in ((rx1, A1), (rx2, A2), (rx3, A3), (rx4, A4)):
        wait_bytes(ref.at[pl.ds(0, z.members - 1)], send.at[phase])

    @pl.when(pipe == 0)
    def _():
        wait_bytes(tok_rx.at[pl.ds(0, z.peers - 1)], send.at[TOK])

    @pl.when(pipe == z.sections - 1)
    def _():
        wait_bytes(cot_rx.at[pl.ds(0, z.peers - 1)], send.at[COT])

    @pl.when(pipe < z.sections - 1)
    def _():
        wait_bytes(res_tx, send.at[RES])

    @pl.when(pipe > 0)
    def _():
        wait_bytes(ig_tx, send.at[GTOP])


def body(
    tokens,
    seq_lengths,
    out_cot,
    s4_vectors,
    s4_modes,
    glu_weight,
    glu_bias,
    ffn_vectors,
    up_weight,
    up_bias,
    down_weight,
):
    chan = lax.axis_index("chan")
    data = lax.axis_index("dp")
    micros, tok_rows, chan_width = tokens.shape
    width = glu_weight.shape[1]
    hidden = up_weight.shape[2]
    z = Sizes(
        lax.axis_size("pipe"), lax.axis_size("chan"), lax.axis_size("dp"),
        tok_rows, chan_width, width, hidden,
    )
    odd = lax.rem(chan, 2) == 1
    length = z.length
    padded = -(-(length // 2 + 1) // LANES) * LANES
    vectors = s4_vectors[0]
    own_vectors = lax.dynamic_slice_in_dim(vectors, data * z.ch, z.ch, 1)
    own_modes = lax.dynamic_slice_in_dim(s4_modes[0], data * z.ch, z.ch, 1)

    def spectrum_of(log_step, modes):
        return kernel_of(log_step, modes, length, padded)

    kern, pull = jax.vjp(spectrum_of, own_vectors[2], own_modes)
    kern_wide = jnp.pad(kern, ((0, 0), (0, LANES)))
    near, far = pl.pallas_call(
        lambda *refs: toeplitz_kernel(z.blocks, *refs),
        out_shape=(
            jax.ShapeDtypeStruct((z.ch, length, LANES), bf16),
            jax.ShapeDtypeStruct((z.ch, LANES, length), bf16),
        ),
        in_specs=[pl.BlockSpec(memory_space=pltpu.VMEM)],
        out_specs=[pl.BlockSpec(memory_space=pltpu.VMEM)] * 2,
        compiler_params=pltpu.CompilerParams(vmem_limit_bytes=40 * 2**20),
        name="toeplitz",
    )(kern_wide)

    def blocks_of(x):
        x = x.reshape(z.peers, z.tok, chan_width)
        x = jnp.pad(x, ((0, 0), (0, z.rows - z.tok), (0, 0)))
        return jnp.concatenate([x, x], axis=2)

    def swap(value, gate):
        return jnp.where(
            odd, jnp.concatenate([gate, value], -1), jnp.concatenate([value, gate], -1)
        )

    ffn = ffn_vectors[0]
    twice = jnp.stack([vectors[0], vectors[1], ffn[0], ffn[1], ffn[2]])
    vec = jnp.concatenate(
        [
            jnp.concatenate([twice, twice], axis=1),
            swap(glu_bias[0, 0], glu_bias[0, 1])[None],
            up_bias[0].astype(f32).reshape(hidden // LANES, LANES),
        ],
        axis=0,
    )
    glu_loc = swap(glu_weight[0, :, 0, :], glu_weight[0, :, 1, :])
    ends = jnp.cumsum(seq_lengths, axis=1)
    begins = ends - seq_lengths
    positions = jnp.arange(length, dtype=jnp.int32)
    masks = (
        (positions[None, None, :] >= begins[:, :, None])
        & (positions[None, None, :] < ends[:, :, None])
    ).astype(f32)
    masks = masks.reshape(z.gr, z.blocks, LANES).transpose(1, 0, 2).reshape(-1, LANES)
    skip = jnp.broadcast_to(own_vectors[3][:, None], (z.ch, LANES))

    vmem = pl.BlockSpec(memory_space=pltpu.VMEM)
    n, r, w = z.peers, z.rows, width

    def s(shape, kind=bf16):
        return jax.ShapeDtypeStruct(shape, kind)

    def v(shape, kind=bf16):
        return pltpu.VMEM(shape, kind)

    exchange = (z.members, z.ch, LANES)
    hid_blocks, ig_blocks, dglu, dup, ddown, vec_sum, xs, gs = pl.pallas_call(
        lambda *refs: main_kernel(z, *refs),
        out_shape=(
            s((n, r, LANES)), s((n, r, LANES)), s((w, 2 * chan_width), f32), s((w, hidden), f32),
            s((hidden, w), f32), s((8, LANES), f32), s((z.stack, LANES), f32),
            s((z.stack, LANES), f32),
        ),
        in_specs=[vmem] * 10,
        out_specs=[vmem] * 8,
        scratch_shapes=[
            v((n, 8, LANES), f32), v((n, w, 2 * chan_width)), v((n, w, hidden)),
            v((n, hidden, w)), v((n, r, LANES)), v((n, r, LANES)), v((r, w)), v((r, w)),
        ]
        + [v(exchange)] * 8
        + [
            v((z.micros * z.blocks, z.ch, LANES), f32),
            v((-(-(z.blocks * z.gr) // 8) * 8 * z.ch, LANES), f32),
            v((r, w), f32), v((r, LANES), f32), v((r, w), f32), v((r, LANES), f32),
            v((r, w), f32), v((r, w), f32), v((n, r, hidden), f32),
            v((r, w)), v((r, w)), v((n, r, hidden)), v((n, r, hidden)), v((n, r, LANES)),
            v((n // 2, r, LANES)), v((r, w)), v((n // 2, r, LANES)), v((r, w)),
            v((n, 8, LANES), f32),
            v((n, r, w)), v((n, r, w)), v((n, r, hidden)), v((n, r, w)), v((n, r, hidden)),
            v((n, r, LANES)), v((n, 8, LANES), f32),
            pltpu.SemaphoreType.DMA((21,)), pltpu.SemaphoreType.DMA((21,)),
        ],
        compiler_params=pltpu.CompilerParams(
            collective_id=0, has_side_effects=True, vmem_limit_bytes=60 * 2**20
        ),
        name="layers",
    )(
        blocks_of(tokens), blocks_of(out_cot), vec, glu_loc, up_weight[0], down_weight[0],
        near, far, skip, masks,
    )

    lags = pl.pallas_call(
        lambda *refs: lag_kernel(z.blocks, *refs),
        out_shape=s((z.ch, (z.blocks + 1) * LANES), f32),
        in_specs=[vmem] * 2,
        out_specs=vmem,
        name="lags",
    )(xs, gs)
    grad_kern = lags[:, :length]
    step_grad, mode_grad = pull(grad_kern)

    def whole(blocks):
        x = jnp.where(odd, blocks[:, : z.tok, chan_width:], blocks[:, : z.tok, :chan_width])
        return x.reshape(1, micros, tok_rows, chan_width)

    reduced = lax.psum((dglu, dup, ddown, vec_sum), "dp")
    red_glu, red_up, red_down, red_vec = reduced
    extra = jnp.stack([step_grad, grad_kern[:, 0]])
    packed = jnp.concatenate([mode_grad.transpose(1, 0, 2).reshape(z.ch, -1), extra.T], axis=1)
    gathered = lax.all_gather(packed, "dp", axis=0, tiled=True)
    split = gathered.shape[1] - 2
    mode_full = gathered[:, :split].reshape(chan_width, 8, -1).transpose(1, 0, 2)
    first, second = red_vec[:, :chan_width], red_vec[:, chan_width:]
    mine = jnp.where(odd, second, first)
    other = jnp.where(odd, first, second)
    grad_vectors = jnp.stack([mine[0], mine[1], gathered[:, split], gathered[:, split + 1]])[None]
    glu_first, glu_second = red_glu[:, :chan_width], red_glu[:, chan_width:]
    grad_glu = jnp.stack(
        [jnp.where(odd, glu_second, glu_first), jnp.where(odd, glu_first, glu_second)], axis=1
    )
    return (
        whole(hid_blocks),
        whole(ig_blocks),
        grad_vectors,
        mode_full[None],
        grad_glu[None],
        jnp.stack([mine[5], other[5]])[None],
        mine[2:5][None],
        red_up[None],
        red_vec[6:].reshape(1, hidden),
        red_down[None],
    )


def solution(mesh):
    placed = (
        P(None, "dp", "chan"),
        P(),
        P(None, "dp", "chan"),
        P("pipe", None, "chan"),
        P("pipe", None, "chan", None),
        P("pipe", None, None, "chan"),
        P("pipe", None, "chan"),
        P("pipe", None, "chan"),
        P("pipe", None, "chan"),
        P("pipe", "chan"),
        P("pipe", "chan", None),
    )
    return jax.shard_map(
        body,
        mesh=mesh,
        in_specs=placed,
        out_specs=(
            P("pipe", None, "dp", "chan"),
            P("pipe", None, "dp", "chan"),
            P("pipe", None, "chan"),
            P("pipe", None, "chan", None),
            P("pipe", None, None, "chan"),
            P("pipe", None, "chan"),
            P("pipe", None, "chan"),
            P("pipe", None, "chan"),
            P("pipe", "chan"),
            P("pipe", "chan", None),
        ),
        check_vma=False,
    )
```

time: 3440 us -> 405 us (0.12)
  blocking collectives: 1220 us -> 12.1 us
  waiting for transfers between devices: 1070 us -> 0.02 us
  other arithmetic: 528 us -> 16.5 us
  matrix products: 466 us -> 17.5 us
  Pallas kernels: 0 us -> 315 us
  local copies, waits for them, and re-layouts: 115 us -> 28.4 us
    unnamed x31 -> x1, waiting for transfers between devices: 1060 us -> 0.02 us
    all_gather x35 -> x1, blocking collectives: 817 us -> 5.8 us  [body(): gathered = lax.all_gather(packed, 'dp', axis=0, tiled=True)]
    dot_general x65 -> x6, matrix products: 443 us -> 17.5 us  [the longest x3 10.6 us: kernel_of(): jnp.dot(jnp.concatenate([spec_r, spec_i], axis=1), table, precision=highest)]
    psum x22 -> x1, blocking collectives: 398 us -> 6.26 us  [body(): reduced = lax.psum((dglu, dup, ddown, vec_sum), 'dp')]
    reduce_sum x69 -> x2, other arithmetic: 372 us -> 2.71 us  [the longest x1 1.74 us: kernel_of(): den_i = 2.0 * decay[:, :, None] * (cosine * rise)[:, None, :]]
    pallas_call x0 -> x3, Pallas kernels: none -> 315 us  [the longest x1 299 us: body(): pl.pallas_call(lambda *refs: main_kernel(z, *refs), out_shape=(s((n, r, L...]
    neg x2 -> x1, other arithmetic: 67.7 us -> 0.69 us  [kernel_of(): rise = (2.0 * jnp.exp(-log_step))[:, None] * sine[None, :]]
    unnamed x430 -> x148, local copies, waits for them, and re-layouts: 58.6 us -> 12 us
  transfers between devices with their start and end apart: 24 -> 1, of which waited for: 18 -> 0; matrix products, arithmetic and copies ran while one was open for 12% -> 7% of each run, Pallas kernels for 0% -> 3%
where the time goes in v1:
time: 405 us; the launch traced here: 404 us
  Pallas kernels  315 us (78%)
  local copies, waits for them, and re-layouts  28.4 us (7%)
  matrix products  17.5 us (4%)
  other arithmetic  16.5 us (4%)
  between operations  14.9 us (4%)
  blocking collectives  12.1 us (3%)
    pallas_call x1, Pallas kernels, body(): pl.pallas_call(lambda *refs: main_kernel(z, *refs), out_shape=(s((n, r, L...  299 us
    pallas_call x1, Pallas kernels, body(): pl.pallas_call(lambda *refs: lag_kernel(z.blocks, *refs), out_shape=s((z....  13.3 us
    unnamed x148, local copies, waits for them, and re-layouts  12 us
    dot_general x3, matrix products, kernel_of(): jnp.dot(jnp.concatenate([spec_r, spec_i], axis=1), table, precision=highest)  10.6 us
  transfers between devices with their start and end apart: 1, of which 0 were waited for; matrix products, arithmetic and copies ran while one was open for 7% of the time, Pallas kernels for 3%

profile of v1, /device:TPU:1, one launch (start us, length us, event | category | flops | bytes accessed | tf_op | source)
XLA Modules:
  0.0 404.3 jit_solution(425923415674382333)
XLA Ops:
  8.9 1.3 slice_bitcast_fusion.7
  10.9 0.9 constant_dynamic-slice_fusion.8
  12.6 1.2 convert_element_type.21
  13.9 1.3 slice_bitcast_fusion.3
  15.1 1.2 slice_bitcast_fusion.4
  22.7 1.4 fusion.1
  25.5 1.5 fusion.55
  27.4 1.5 convolution_add_fusion
  28.9 2.6 toeplitz.1
  31.6 2.2 copy-done
  33.7 2.2 copy-done.1
  38.2 1.4 and_convert_fusion.refs_9_
  39.6 1.2 broadcast_in_dim.56.refs_8_
  40.8 299.0 %layers.1 = (bf16[8,80,128]{2,1,0:T(8,128)(2,1)}, bf16[8,80,128]{2,1,0:T(8,128)(2,1)}, f32[512,128]{1,0:T(8,128)}, f32[512,256]{1,0:T(8,128)}, f32[256,512]{1,0:...) custom-call(bf16[8,80,128]{2,1,0:T(8,128)(2,1)} %pad_maximum_fusion.3.refs_0_, ...), custom_call_target="tpu_custom_call" | custom-call | tf_op jit(solution)/shard_map/layers/pallas_call | solution.py:658
  340.5 6.3 %psum.28 = f32[8,128]{1,0:T(8,128)S(1)} all-reduce(f32[8,128]{1,0:T(8,128)S(1)} %copy-done.58), channel_id=1, replica_groups=mesh['pipe'=4,'chan'=8,'dp'=4] {'dp'}, use_global_device_ids=true, to_apply=%region_1.2 | all-reduce | flops 1024 | bytes 8192 | tf_op jit(solution)/shard_map/psum | solution.py:707
  349.7 13.3 %lags.1 = f32[16,1280]{1,0:T(8,128)} custom-call(f32[1152,128]{1,0:T(8,128)} %get-tuple-element.25.refs_0_, f32[1152,128]{1,0:T(8,128)} %get-tuple-element.26.refs_1_), custom_call_target="tpu_custom_call" | custom-call | tf_op jit(solution)/shard_map/lags/pallas_call | solution.py:693
  363.0 7.5 %fusion.11 = f32[16,1280]{1,0:T(8,128)S(1)} fusion(f32[1280,1152]{1,0:T(8,128)} %constant.49.clone, f32[16,1280]{1,0:T(8,128)} %lags.1), kind=kOutput, calls=%fused_computation.51 | convolution fusion | flops 283115520 | bytes 6053888 | tf_op jit(solution)/shard_map/transpose(jvp())/dot_general | solution.py:71
  370.9 3.2 fusion
  374.1 2.3 fusion.8
  378.2 1.2 slice.250
  381.1 1.7 multiply_reduce_fusion.1
  384.0 1.0 fusion.17
  385.8 5.8 %all_gather.3 = f32[64,258]{1,0:T(8,128)S(1)} all-gather(f32[16,258]{1,0:T(8,128)S(1)} %pad_maximum_fusion.5), channel_id=1, replica_groups=mesh['pipe'=4,'chan'=8,'dp'=4] {'dp'}, dimensions={0}, use_global_device_ids=true | all-gather | bytes 82560 | tf_op jit(solution)/shard_map/all_gather | solution.py:711
  393.7 1.2 select_bitcast_fusion.1
  (212 shorter events, 26.8 us)
Async XLA Ops:
  7.2 12.7 %copy-start.45 = (bf16[2,288,64]{1,2,0:T(8,128)(2,1)S(1)}, bf16[2,288,64]{1,2,0:T(8,128)(2,1)}, u32[]{:S(2)}) copy-start(bf16[2,288,64]{1,2,0:T(8,128)(2,1)} %param.14) | copy-start | bytes 221188
  7.2 13.7 %copy-start.46 = (bf16[2,288,64]{1,2,0:T(8,128)(2,1)S(1)}, bf16[2,288,64]{1,2,0:T(8,128)(2,1)}, u32[]{:S(2)}) copy-start(bf16[2,288,64]{1,2,0:T(8,128)(2,1)} %param.16) | copy-start | bytes 221188
  7.2 386.5 %all-reduce.30.cloned.1.call-start = ((), (), s32[]{:S(2)}) async-start(), calls=%async_computation | async-start | bytes 2621440 | tf_op jit(solution)/shard_map/psum | solution.py:707
  12.1 9.8 %copy-start.26 = (f32[1,1,16,32]{3,2,1,0:T(8,128)}, f32[1,1,16,32]{3,2,1,0:T(8,128)S(1)}, u32[]{:S(2)}) copy-start(f32[1,1,16,32]{3,2,1,0:T(8,128)S(1)} %copy.208) | copy-start | bytes 6148
  12.2 9.7 %copy-start.28 = (f32[1,1,16,32]{3,2,1,0:T(8,128)}, f32[1,1,16,32]{3,2,1,0:T(8,128)S(1)}, u32[]{:S(2)}) copy-start(f32[1,1,16,32]{3,2,1,0:T(8,128)S(1)} %copy.207) | copy-start | bytes 6148
  12.3 9.6 %copy-start.30 = (f32[1,1,16,32]{3,2,1,0:T(8,128)}, f32[1,1,16,32]{3,2,1,0:T(8,128)S(1)}, u32[]{:S(2)}) copy-start(f32[1,1,16,32]{3,2,1,0:T(8,128)S(1)} %copy.205) | copy-start | bytes 6148
  12.4 9.5 %copy-start.24 = (f32[1,1,16,32]{3,2,1,0:T(8,128)}, f32[1,1,16,32]{3,2,1,0:T(8,128)S(1)}, u32[]{:S(2)}) copy-start(f32[1,1,16,32]{3,2,1,0:T(8,128)S(1)} %copy.204) | copy-start | bytes 6148
  12.4 9.6 %copy-start.41 = (f32[16,32]{1,0:T(8,128)}, f32[16,32]{1,0:T(8,128)S(1)}, u32[]{:S(2)}) copy-start(f32[16,32]{1,0:T(8,128)S(1)} %get-tuple-element.184) | copy-start | bytes 6148
  12.5 9.6 %copy-start.43 = (f32[16,32]{1,0:T(8,128)}, f32[16,32]{1,0:T(8,128)S(1)}, u32[]{:S(2)}) copy-start(f32[16,32]{1,0:T(8,128)S(1)} %get-tuple-element.185) | copy-start | bytes 6148
  12.5 9.4 %copy-start.32 = (f32[640]{0:T(1024)S(1)}, f32[640]{0:T(1024)}, u32[]{:S(2)}) copy-start(f32[640]{0:T(1024)} %constant.47.clone) | copy-start | bytes 7684
  12.5 9.4 %copy-start.37 = (f32[640]{0:T(1024)S(1)}, f32[640]{0:T(1024)}, u32[]{:S(2)}) copy-start(f32[640]{0:T(1024)} %constant.48.clone) | copy-start | bytes 7684
  27.4 8.6 %copy-start.61 = (f32[1,64]{1,0:T(1,128)S(1)}, f32[1,64]{1,0:T(1,128)}, u32[]{:S(2)}) copy-start(f32[1,64]{1,0:T(1,128)} %get-tuple-element.205) | copy-start | bytes 772
  27.4 8.6 %copy-start.62 = (f32[1,64]{1,0:T(1,128)S(1)}, f32[1,64]{1,0:T(1,128)}, u32[]{:S(2)}) copy-start(f32[1,64]{1,0:T(1,128)} %get-tuple-element.206) | copy-start | bytes 772
  27.4 10.1 %copy-start.57 = (f32[1,256]{1,0:T(1,128)S(1)}, f32[1,256]{1,0:T(1,128)}, u32[]{:S(2)}) copy-start(f32[1,256]{1,0:T(1,128)} %convert_element_type.21) | copy-start | bytes 3076
  27.4 10.8 %copy-start.60 = (s32[36]{0:T(128)S(1)}, s32[36]{0:T(128)}, u32[]{:S(2)}) copy-start(s32[36]{0:T(128)} %ge.45) | copy-start | bytes 436
  362.9 7.6 %copy-start.34 = (f32[640]{0:T(1024)S(1)}, f32[640]{0:T(1024)}, u32[]{:S(2)}) copy-start(f32[640]{0:T(1024)} %constant.47.clone) | copy-start | bytes 7684
  362.9 7.6 %copy-start.39 = (f32[640]{0:T(1024)S(1)}, f32[640]{0:T(1024)}, u32[]{:S(2)}) copy-start(f32[640]{0:T(1024)} %constant.48.clone) | copy-start | bytes 7684
  362.9 7.6 %copy-start.52 = (f32[16]{0:T(128)S(1)}, f32[16]{0:T(128)}, u32[]{:S(2)}) copy-start(f32[16]{0:T(128)} %copy-done.50) | copy-start | bytes 196
  362.9 7.8 %copy-start.17 = (f32[16,640]{1,0:T(8,128)S(1)}, f32[16,640]{1,0:T(8,128)}, u32[]{:S(2)}) copy-start(f32[16,640]{1,0:T(8,128)} %copy-done.16) | copy-start | bytes 122884
  362.9 7.8 %copy-start.19 = (f32[16,640]{1,0:T(8,128)S(1)}, f32[16,640]{1,0:T(8,128)}, u32[]{:S(2)}) copy-start(f32[16,640]{1,0:T(8,128)} %copy-done.18) | copy-start | bytes 122884
  363.0 7.8 %copy-start.54 = (f32[640]{0:T(1024)S(1)}, f32[640]{0:T(1024)}, u32[]{:S(2)}) copy-start(f32[640]{0:T(1024)} %constant.113) | copy-start | bytes 7684
  382.8 9.5 %copy-start.63 = (f32[1,64]{1,0:T(1,128)S(1)}, f32[1,64]{1,0:T(1,128)}, u32[]{:S(2)}) copy-start(f32[1,64]{1,0:T(1,128)} %slice.249) | copy-start | bytes 772
  382.8 9.5 %copy-start.64 = (f32[1,64]{1,0:T(1,128)S(1)}, f32[1,64]{1,0:T(1,128)}, u32[]{:S(2)}) copy-start(f32[1,64]{1,0:T(1,128)} %slice.250) | copy-start | bytes 772
  382.8 10.3 %copy-start.59 = (f32[2,64]{1,0:T(2,128)S(1)}, f32[2,64]{1,0:T(2,128)}, u32[]{:S(2)}) copy-start(f32[2,64]{1,0:T(2,128)} %slice.241) | copy-start | bytes 1540
  (42 other events, 102.2 us)
Sparse Core Ops, SparseCore 0:
  340.0 43.4 all-reduce.29

commit v2 on v1

--- a/solution.py
+++ b/solution.py
@@ -2,6 +2,7 @@
 
 import jax
 import jax.numpy as jnp
+import ml_dtypes
 import numpy as np
 from jax import lax
 from jax.experimental import pallas as pl
@@ -9,7 +10,6 @@
 from jax.sharding import PartitionSpec as P
 
 norm_eps = 1e-05
-highest = lax.Precision.HIGHEST
 f32 = jnp.float32
 bf16 = jnp.bfloat16
 LANES = 128
@@ -27,48 +27,10 @@
 
 def half_angles(length, padded):
     angle = np.minimum(np.arange(padded), length // 2) * (np.pi / length)
-    cosine = np.cos(angle)
-    cosine[length // 2 :] = 0.0
-    return cosine.astype(np.float32), np.sin(angle).astype(np.float32)
-
-
-def kernel_of(log_step, modes, length, padded):
-    cosine, sine = half_angles(length, padded)
-    cosine, sine = jnp.asarray(cosine), jnp.asarray(sine)
-    decay, rate = modes[0], modes[1]
-    rank_r, rank_i, in_r, in_i, out_r, out_i = (modes[i] for i in range(2, 8))
-    vals = [
-        (out_r * in_r - out_i * in_i, out_r * in_i + out_i * in_r),
-        (out_r * rank_r - out_i * rank_i, out_r * rank_i + out_i * rank_r),
-        (rank_r * in_r + rank_i * in_i, rank_r * in_i - rank_i * in_r),
-        (rank_r * rank_r + rank_i * rank_i, jnp.zeros_like(rank_r)),
-    ]
-    rise = (2.0 * jnp.exp(-log_step))[:, None] * sine[None, :]
-    square = cosine * cosine
-    den_r = (decay * decay + rate * rate)[:, :, None] * square - (rise * rise)[:, None, :]
-    den_i = 2.0 * decay[:, :, None] * (cosine * rise)[:, None, :]
-    inverse = 1.0 / (den_r * den_r + den_i * den_i)
-    den = jnp.concatenate([den_r * inverse, den_i * inverse], axis=2)
-    alpha = jnp.stack([decay * v_r - rate * v_i for v_r, v_i in vals], axis=1)
-    beta = jnp.stack([v_r for v_r, v_i in vals], axis=1)
-    sums = jnp.einsum(
-        "hvn,hnj->hvj", jnp.concatenate([alpha, beta], axis=1), den, precision=highest
-    )
-    parts = []
-    for v in range(4):
-        a_u, a_w = sums[:, v, :padded], sums[:, v, padded:]
-        b_u, b_w = sums[:, 4 + v, :padded], sums[:, 4 + v, padded:]
-        parts.append((2.0 * (cosine * a_u + rise * b_w), 2.0 * (rise * b_u - cosine * a_w)))
-    (m0r, m0i), (m1r, m1i), (m2r, m2i), (m3r, m3i) = parts
-    top_r = cosine * (m1r * m2r - m1i * m2i)
-    top_i = cosine * (m1r * m2i + m1i * m2r)
-    low_r = 1.0 + cosine * m3r
-    low_i = cosine * m3i
-    size = 1.0 / (low_r * low_r + low_i * low_i)
-    spec_r = m0r - (top_r * low_r + top_i * low_i) * size
-    spec_i = m0i - (top_i * low_r - top_r * low_i) * size
-    table = jnp.asarray(fourier_table(length, padded))
-    return jnp.dot(jnp.concatenate([spec_r, spec_i], axis=1), table, precision=highest)
+    rows = np.zeros((8, padded), np.float32)
+    rows[0] = np.where(np.arange(padded) < length // 2, np.cos(angle), 0.0)
+    rows[1] = np.sin(angle)
+    return rows
 
 
 def shifted(x, by):
@@ -77,52 +39,6 @@
     if by == 0:
         return x
     return pltpu.roll(x, by, x.ndim - 1)
-
-
-def toeplitz_kernel(blocks, kern_ref, near_ref, far_ref):
-    channels = kern_ref.shape[0]
-    wide = kern_ref.shape[1]
-
-    def step(h, carry):
-        row = kern_ref[pl.ds(h, 1), :]
-        full = jnp.broadcast_to(row, (LANES, wide))
-        full = pltpu.roll(full, 0, 1, stride=1, stride_axis=0)
-        low = full.astype(bf16)
-        far_ref[h] = low[:, : blocks * LANES]
-        for d in range(blocks):
-            near_ref[h, d * LANES : (d + 1) * LANES, :] = low[:, d * LANES : (d + 1) * LANES]
-        return carry
-
-    lax.fori_loop(0, channels, step, 0)
-
-
-def lag_kernel(blocks, x_ref, g_ref, out_ref):
-    channels, groups = 16, 4
-    stride = channels
-    rows = 40
-    wide = (blocks + 1) * LANES
-
-    def step(h, carry):
-        x = x_ref[pl.ds((blocks - 1) * groups * stride + h, rows, stride=stride), :]
-        parts = [
-            g_ref[pl.ds(d * groups * stride + h, rows, stride=stride), :] for d in range(blocks)
-        ]
-        g = jnp.concatenate(parts, axis=1)
-        prod = lax.dot_general(
-            x.astype(bf16), g.astype(bf16), (((0,), (0,)), ((), ())), preferred_element_type=f32
-        )
-        prod = jnp.concatenate([prod, jnp.zeros((LANES, LANES), f32)], axis=1)
-        size = LANES // 2
-        while size >= 8:
-            prod = prod[:size] + shifted(prod[size:], wide - size)
-            size //= 2
-        row = prod[0:1]
-        for a in range(1, 8):
-            row = row + shifted(prod[a : a + 1], wide - a)
-        out_ref[pl.ds(h, 1), :] = row
-        return carry
-
-    lax.fori_loop(0, channels, step, 0)
 
 
 def gelu(x):
@@ -168,15 +84,24 @@
 
 
 def main_kernel(z, *refs):
-    (tok_tx, cot_tx, vec_tx, glu_loc, up_loc, down_loc, near, far, skip, masks) = refs[:10]
-    (hid_out, ig_out, dglu, dup, ddown, vec_out, xs, gs) = refs[10:18]
     (
+        lengths, tokens, out_cot, vectors, modes, glu_loc, glu_bias, ffn_vec, up_loc, up_bias,
+        down_loc, angles, table_in,
+    ) = refs[:13]
+    (
+        hid_out, ig_out, vec_out, modes_out, dglu, glub_out, ffn_out, dup, upb_out, ddown,
+    ) = refs[13:23]
+    (
+        tok_tx, cot_tx, vec_tx, near, far, skip, masks, hid_rx, ig_rx, xs, gs,
+        table, turn_s, cols, rise_s, sums_s, gsum_s, slope_s, kern_s, lag_s, gcol_s, gstep_s,
+        modes_tx, modes_rx, pglu, pup, pdown, kglu, kup, kdown, sglu, sup, sdown,
+        lglu, lup, ldown,
         vec_all, glu_all, up_all, down_all, tok_rx, cot_rx, res, gtop,
         tx1, rx1, tx2, rx2, tx3, rx3, tx4, rx4,
         conv_out, ys, hat1_s, inv1_s, hat2_s, inv2_s, val_s, sig_s, hidden_s,
         gated_s, ffn_s, act_s, gh_s, gp_s, lay_s, res_tx, ig_s, ig_tx, vg_s,
         ga, fi, ac, bg, gh, gp, vrx, send, recv,
-    ) = refs[18:]
+    ) = refs[23:]
     pipe = lax.axis_index("pipe")
     chan = lax.axis_index("chan")
     data = lax.axis_index("dp")
@@ -225,7 +150,73 @@
         lax.fori_loop(1, z.members, step, 0)
         pltpu.make_async_copy(src_of(me), dst.at[slot], recv.at[phase]).start()
 
-    (VEC, GLU, UP, DOWN, TOK, COT, A1, A2, A3, A4, RES, GTOP, HID, IG, GA, FI, AC, BG, GH, GP, VG) = range(21)
+    (VEC, TOK, COT, A1, A2, A3, A4, RES, GTOP, HID, IG, GA, FI, AC, BG, GH, GP, VG) = range(18)
+    GLU, UP, DOWN = 18, 24, 30
+    TABLE, MODES, GRADS = 36, 37, 38
+
+    high, deep = chan // z.quarters, lax.rem(chan, z.quarters)
+    low, core = data // 2, lax.rem(data, 2)
+    weight_of = {GLU: (glu_loc, glu_all), UP: (up_loc, up_all), DOWN: (down_loc, down_all)}
+    own_side, far_side = high * z.quarters, (1 - high) * z.quarters
+
+    def place(c, d):
+        return {"pipe": pipe, "chan": c, "dp": d}
+
+    def weights_ring(t):
+        loc, whole = weight_of[t]
+        half = loc.shape[0] // 2
+        part = pl.ds(pl.multiple_of(core * half, half), half)
+        for k in range(1, z.quarters):
+            c = own_side + lax.rem(deep + k, z.quarters)
+            remote(loc.at[part], whole.at[chan, part], t, place(c, data)).start()
+        pltpu.make_async_copy(loc, whole.at[chan], recv.at[t + 5]).start()
+
+    def weights_across(t):
+        loc, whole = weight_of[t]
+        half = loc.shape[0] // 2
+        fourth = half // 2
+        wait_bytes(whole.at[pl.ds(0, z.quarters - 1), pl.ds(0, half)], recv.at[t])
+        wait_bytes(loc, recv.at[t + 5])
+        quarter = pl.ds(pl.multiple_of(core * half + low * fourth, fourth), fourth)
+        piece = whole.at[pl.ds(own_side, z.quarters), quarter]
+        remote(piece, piece, t + 1, place(far_side + deep, (1 - low) * 2 + core)).start()
+        part = pl.ds(pl.multiple_of(core * half, half), half)
+        for k in range(1, z.quarters):
+            piece = whole.at[own_side + lax.rem(deep + k, z.quarters), part]
+            remote(piece, piece, t + 3, place(chan, low * 2 + 1 - core)).start()
+
+    def weights_beside(t):
+        loc, whole = weight_of[t]
+        half = loc.shape[0] // 2
+        fourth = half // 2
+        wait_bytes(whole.at[pl.ds(0, z.quarters), pl.ds(0, fourth)], recv.at[t + 1])
+        quarter = pl.ds(pl.multiple_of(core * half + (1 - low) * fourth, fourth), fourth)
+        piece = whole.at[pl.ds(far_side, z.quarters), quarter]
+        remote(piece, piece, t + 2, place(chan, (1 - low) * 2 + core)).start()
+
+    def weights_core(t):
+        loc, whole = weight_of[t]
+        half = loc.shape[0] // 2
+        fourth = half // 2
+        wait_bytes(whole.at[pl.ds(0, z.quarters), pl.ds(0, fourth)], recv.at[t + 2])
+        part = pl.ds(pl.multiple_of(core * half, half), half)
+        piece = whole.at[pl.ds(far_side, z.quarters), part]
+        remote(piece, piece, t + 4, place(chan, low * 2 + 1 - core)).start()
+
+    def weights_here(t):
+        loc, whole = weight_of[t]
+        half = loc.shape[0] // 2
+        wait_bytes(whole.at[pl.ds(0, z.quarters - 1), pl.ds(0, half)], recv.at[t + 3])
+        wait_bytes(whole.at[pl.ds(0, z.quarters), pl.ds(0, half)], recv.at[t + 4])
+
+    def weights_sent(t):
+        loc, whole = weight_of[t]
+        half = loc.shape[0] // 2
+        for stage, count, size in (
+            (0, z.quarters - 1, half), (1, z.quarters, half // 2), (2, z.quarters, half // 2),
+            (3, z.quarters - 1, half), (4, z.quarters, half),
+        ):
+            wait_bytes(whole.at[pl.ds(0, count), pl.ds(0, size)], send.at[t + stage])
 
     barrier = pltpu.get_barrier_semaphore()
 
@@ -243,6 +234,30 @@
         pl.semaphore_signal(
             barrier, inc=1, device_id=neighbour, device_id_type=pl.DeviceIdType.MESH
         )
+    pltpu.make_async_copy(table_in, table, recv.at[TABLE]).start()
+    odd = lax.rem(chan, 2)
+
+    def fill_blocks(source, target):
+        for m in range(z.micros):
+            x = source[m].astype(f32)
+            x = jnp.concatenate([x, x], axis=1)
+            for q in range(z.quarters):
+                block = x[q * tok : (q + 1) * tok]
+                block = jnp.concatenate([block, jnp.zeros((rows - tok, LANES), f32)], axis=0)
+                target[m * z.quarters + q] = block.astype(bf16)
+
+    def own_half(x):
+        return pltpu.roll(x, odd * (LANES // 2), x.ndim - 1)
+
+    per = z.hid // LANES
+    vec_rows = [vectors[0:1, :], vectors[1:2, :]] + [ffn_vec[r : r + 1, :] for r in range(3)]
+    for r, row in enumerate(vec_rows):
+        vec_tx[r : r + 1, :] = jnp.concatenate([row, row], axis=1)
+    vec_tx[5:6, :] = own_half(jnp.concatenate([glu_bias[0:1, :], glu_bias[1:2, :]], axis=1))
+    for r in range(per):
+        vec_tx[6 + r : 7 + r, :] = up_bias[:, r * LANES : (r + 1) * LANES].astype(f32)
+    pl.when(pipe == 0)(lambda: fill_blocks(tokens, tok_tx))
+    pl.when(pipe == z.sections - 1)(lambda: fill_blocks(out_cot, cot_tx))
     pl.semaphore_wait(barrier, z.members - 1 + 2)
 
     to_peers(lambda c: vec_tx, vec_all, VEC)
@@ -255,9 +270,8 @@
     def _():
         to_peers(lambda c: cot_tx.at[c], cot_rx, COT)
 
-    to_peers(lambda c: glu_loc, glu_all, GLU)
-    to_peers(lambda c: up_loc, up_all, UP)
-    to_peers(lambda c: down_loc, down_all, DOWN)
+    for t in (GLU, UP, DOWN):
+        weights_ring(t)
 
     pad_rows = (z.blocks - 1) * z.gr * z.ch
     data_rows = z.blocks * z.gr * z.ch
@@ -266,6 +280,119 @@
         (z.stack - pad_rows - data_rows, LANES), f32
     )
     gs[data_rows : z.stack, :] = jnp.zeros((z.stack - data_rows, LANES), f32)
+
+    spot = lax.broadcasted_iota(jnp.int32, (1, LANES), 1)
+    masks[z.blocks * z.gr :, :] = jnp.zeros((masks.shape[0] - z.blocks * z.gr, LANES), f32)
+    for m in range(z.micros):
+        first_len, second_len = lengths[m, 0], lengths[m, 1]
+        for i in range(z.blocks):
+            at = i * z.gr + m * z.segments
+            where = spot + i * LANES
+            masks[at : at + 1, :] = jnp.where(where < first_len, 1.0, 0.0)
+            inside = jnp.where(where < first_len + second_len, 1.0, 0.0)
+            masks[at + 1 : at + 2, :] = jnp.where(where >= first_len, inside, 0.0)
+
+    ch, nh = z.ch, modes.shape[2]
+    mine = pl.ds(pl.multiple_of(data * ch, ch), ch)
+    decay, rate, rank_r, rank_i, in_r, in_i, out_r, out_i = (modes[p, mine, :] for p in range(8))
+    pairs = [
+        (out_r * in_r - out_i * in_i, out_r * in_i + out_i * in_r),
+        (out_r * rank_r - out_i * rank_i, out_r * rank_i + out_i * rank_r),
+        (rank_r * in_r + rank_i * in_i, rank_r * in_i - rank_i * in_r),
+        (rank_r * rank_r + rank_i * rank_i, None),
+    ]
+    turn_s[...] = jnp.zeros(turn_s.shape, f32)
+    for v, (v_r, v_i) in enumerate(pairs):
+        alpha = decay * v_r if v_i is None else decay * v_r - rate * v_i
+        turn_s[0, v * ch : (v + 1) * ch, 0:nh] = alpha
+        turn_s[0, (4 + v) * ch : (5 + v) * ch, 0:nh] = v_r
+    turn_s[1, 0:ch, 0:nh] = decay * decay + rate * rate
+    turn_s[1, ch : 2 * ch, 0:nh] = 2.0 * decay
+    turn_s[1, 2 * ch : 2 * ch + 4, 0 : z.cw] = vectors[...]
+    cols[0] = turn_s[0].T[0:nh]
+    turned = turn_s[1].T
+    cols[1] = turned[0:nh]
+    turn_s[1] = turned
+    side = turn_s[1, mine, 2 * ch : 2 * ch + 4]
+    rise_s[...] = jnp.broadcast_to(2.0 * jnp.exp(-side[:, 2:3]), (ch, LANES))
+    skip[...] = jnp.broadcast_to(side[:, 3:4], (ch, LANES))
+    cosine, sine = angles[0:1, :], angles[1:2, :]
+    padded = angles.shape[1]
+
+    def column_of(k, h):
+        return pltpu.roll(cols[k], lax.rem(LANES - h, LANES), 1)
+
+    def modes_at(h):
+        two = column_of(1, h)
+        square, double = two[:, 0:1], two[:, ch : ch + 1]
+        y = rise_s[pl.ds(h, 1), 0:1] * sine
+        cy = cosine * y
+        den_r = square * (cosine * cosine) - y * y
+        den_i = double * cy
+        inverse = 1.0 / (den_r * den_r + den_i * den_i)
+        return double, y, cy, den_r * inverse, den_i * inverse
+
+    def cauchy_step(h, carry):
+        _, _, _, u, w = modes_at(h)
+        column = column_of(0, h)
+        for v in range(4):
+            a = column[:, v * ch : v * ch + 1]
+            b = column[:, (4 + v) * ch : (4 + v) * ch + 1]
+            sums_s[v, pl.ds(h, 1), :] = jnp.sum(a * u, axis=0, keepdims=True)
+            sums_s[4 + v, pl.ds(h, 1), :] = jnp.sum(a * w, axis=0, keepdims=True)
+            sums_s[8 + v, pl.ds(h, 1), :] = jnp.sum(b * u, axis=0, keepdims=True)
+            sums_s[12 + v, pl.ds(h, 1), :] = jnp.sum(b * w, axis=0, keepdims=True)
+        return carry
+
+    def times(a, b):
+        return a[0] * b[0] - a[1] * b[1], a[0] * b[1] + a[1] * b[0]
+
+    def conj(a):
+        return a[0], -a[1]
+
+    def moments():
+        y_all = rise_s[:, 0:1] * sine
+        ms = [
+            (
+                2.0 * (cosine * sums_s[v] + y_all * sums_s[12 + v]),
+                2.0 * (y_all * sums_s[8 + v] - cosine * sums_s[4 + v]),
+            )
+            for v in range(4)
+        ]
+        low_r, low_i = 1.0 + cosine * ms[3][0], cosine * ms[3][1]
+        size = 1.0 / (low_r * low_r + low_i * low_i)
+        return y_all, ms, times(ms[1], ms[2]), (low_r * size, -low_i * size)
+
+    def high_low(x):
+        high_part = x.astype(bf16)
+        low_part = (x - high_part.astype(f32)).astype(bf16)
+        return jnp.concatenate([high_part, low_part], axis=0)
+
+    lax.fori_loop(0, ch, cauchy_step, 0)
+    weights_across(GLU)
+    y_all, ms, cross, over = moments()
+    fix = times(cross, over)
+    spec = jnp.concatenate([ms[0][0] - cosine * fix[0], ms[0][1] - cosine * fix[1]], axis=1)
+    wait_bytes(table, recv.at[TABLE])
+    both = dot(high_low(spec), table[...])
+    wide = (z.blocks + 1) * LANES
+    kern_s[:, 0 : z.length] = both[0:ch] + both[ch : 2 * ch]
+    kern_s[:, z.length : wide] = jnp.zeros((ch, wide - z.length), f32)
+    weights_across(UP)
+    weights_beside(GLU)
+
+    def toeplitz_step(h, carry):
+        full = jnp.broadcast_to(kern_s[pl.ds(h, 1), :], (LANES, wide))
+        full = pltpu.roll(full, 0, 1, stride=1, stride_axis=0).astype(bf16)
+        far[h] = full[:, : z.length]
+        for d in range(z.blocks):
+            near[h, d * LANES : (d + 1) * LANES, :] = full[:, d * LANES : (d + 1) * LANES]
+        return carry
+
+    lax.fori_loop(0, ch, toeplitz_step, 0)
+    weights_across(DOWN)
+    weights_core(GLU)
+    weights_beside(UP)
 
     wait_bytes(vec_all, recv.at[VEC])
 
@@ -357,6 +484,8 @@
     inv1_s[...] = jnp.broadcast_to(inv1, (rows, LANES))
     turn_out(hat1 * gain1 + bias1, tx1)
     to_members(lambda p: tx1.at[p], rx1, slot_me, A1)
+    weights_beside(DOWN)
+    weights_core(UP)
     wait_bytes(rx1, recv.at[A1])
     for m in range(z.micros):
         for i, tile in enumerate(lane_tiles(rx1, m)):
@@ -384,16 +513,17 @@
             tiles.append(gelu(tile))
         lane_pieces(tiles, m, tx2)
     to_members(lambda p: tx2.at[slot_of(p)], rx2, me, A2)
+    weights_core(DOWN)
     wait_bytes(rx2, recv.at[A2])
     gated_s[...] = turn_in(rx2).astype(bf16)
-    wait_bytes(glu_all, recv.at[GLU])
+    weights_here(GLU)
     gated = gated_s[...]
     values, gates = [], []
     for j in range(z.peers // 2):
-        even = dot(gated, glu_all[2 * j]) + vec_all[2 * j, 5:6, :]
-        odd = dot(gated, glu_all[2 * j + 1]) + vec_all[2 * j + 1, 5:6, :]
-        values.append(jnp.where(first_half, even, odd))
-        gates.append(shifted(jnp.where(first_half, odd, even), LANES // 2))
+        lead = dot(gated, glu_all[2 * j]) + vec_all[2 * j, 5:6, :]
+        tail = dot(gated, glu_all[2 * j + 1]) + vec_all[2 * j + 1, 5:6, :]
+        values.append(jnp.where(first_half, lead, tail))
+        gates.append(shifted(jnp.where(first_half, tail, lead), LANES // 2))
     value = jnp.concatenate(values, axis=1)
     sig = jax.nn.sigmoid(jnp.concatenate(gates, axis=1))
     val_s[...] = value
@@ -403,11 +533,10 @@
     hat2_s[...] = hat2
     inv2_s[...] = jnp.broadcast_to(inv2, (rows, LANES))
     ffn_s[...] = (hat2 * gain2 + bias2).astype(bf16)
-    wait_bytes(up_all, recv.at[UP])
-    wait_bytes(down_all, recv.at[DOWN])
+    weights_here(UP)
+    weights_here(DOWN)
     ffn_in = ffn_s[...]
     total = mid + out_bias
-    per = z.hid // LANES
     for c in range(z.peers):
         offset = jnp.concatenate([vec_all[c, 6 + r : 7 + r, :] for r in range(per)], axis=1)
         hidden = dot(ffn_in, up_all[c]) + offset
@@ -424,10 +553,19 @@
 
     for j in range(z.peers // 2):
         lay_s[j] = layer_out[:, j * LANES : (j + 1) * LANES]
-    to_peers(lambda c: lay_s.at[c // 2], hid_out, HID)
-    to_peers(lambda c: gated_s, ga, GA)
-    to_peers(lambda c: ffn_s, fi, FI)
-    to_peers(lambda c: act_s.at[c], ac, AC)
+    to_peers(lambda c: lay_s.at[c // 2], hid_rx, HID)
+
+    def forward_rows():
+        to_peers(lambda c: gated_s, ga, GA)
+        to_peers(lambda c: ffn_s, fi, FI)
+        to_peers(lambda c: act_s.at[c], ac, AC)
+
+    def backward_rows():
+        to_peers(lambda c: gtop, bg, BG)
+        to_peers(lambda c: gh_s.at[c], gh, GH)
+        to_peers(lambda c: gp_s.at[c], gp, GP)
+
+    pl.when(pipe < z.sections - 1)(forward_rows)
 
     @pl.when(pipe == z.sections - 1)
     def _():
@@ -461,15 +599,13 @@
         gg = shifted(grad_gate[:, j * LANES : (j + 1) * LANES], LANES // 2)
         pair = (jnp.where(first_half, gv, gg), jnp.where(first_half, gg, gv))
         for half in range(2):
-            low = pair[half].astype(bf16)
-            gp_s[2 * j + half] = low
-            part = dot_nt(low, glu_all[2 * j + half])
+            narrow = pair[half].astype(bf16)
+            gp_s[2 * j + half] = narrow
+            part = dot_nt(narrow, glu_all[2 * j + half])
             grad_gated = part if grad_gated is None else grad_gated + part
     turn_out(grad_gated, tx3)
     to_members(lambda p: tx3.at[p], rx3, slot_me, A3)
-    to_peers(lambda c: gtop, bg, BG)
-    to_peers(lambda c: gh_s.at[c], gh, GH)
-    to_peers(lambda c: gp_s.at[c], gp, GP)
+    pl.when(pipe == 0)(backward_rows)
     wait_bytes(rx3, recv.at[A3])
     for m in range(z.micros):
         for i, tile in enumerate(lane_tiles(rx3, m)):
@@ -494,6 +630,28 @@
             tiles.append(masked_sum(m, i) + skip[...] * own)
         lane_pieces(tiles, m, tx4)
     to_members(lambda p: tx4.at[slot_of(p)], rx4, me, A4)
+
+    def lag_step(h, carry):
+        x = xs[pl.ds(pad_rows + h, conv_rows, stride=z.ch), :]
+        parts = [
+            gs[pl.ds(d * z.gr * z.ch + h, conv_rows, stride=z.ch), :] for d in range(z.blocks)
+        ]
+        prod = dot_tn(x.astype(bf16), jnp.concatenate(parts, axis=1).astype(bf16))
+        prod = jnp.concatenate([prod, jnp.zeros((LANES, LANES), f32)], axis=1)
+        size = LANES // 2
+        while size >= 8:
+            prod = prod[:size] + shifted(prod[size:], wide - size)
+            size //= 2
+        row = prod[0:1]
+        for a in range(1, 8):
+            row = row + shifted(prod[a : a + 1], wide - a)
+        lag_s[pl.ds(h, 1), :] = row
+        return carry
+
+    def lags():
+        lax.fori_loop(0, ch, lag_step, 0)
+
+    pl.when(pipe == 0)(lags)
     wait_bytes(rx4, recv.at[A4])
     grad_conv_in = jnp.where(row_ok, turn_in(rx4), 0.0)
     hat1 = hat1_s[...]
@@ -504,10 +662,13 @@
     @pl.when(pipe > 0)
     def _():
         remote(ig_tx, gtop, GTOP, earlier).start()
+        backward_rows()
+
+    pl.when(pipe == z.sections - 1)(forward_rows)
 
     for j in range(z.peers // 2):
         ig_s[j] = grad_res_low[:, j * LANES : (j + 1) * LANES]
-    to_peers(lambda c: ig_s.at[c // 2], ig_out, IG)
+    to_peers(lambda c: ig_s.at[c // 2], ig_rx, IG)
 
     rows_of = [
         jnp.sum(grad_conv_in * hat1, axis=0, keepdims=True),
@@ -524,32 +685,174 @@
         up_row = jnp.sum(gh_s[c].astype(f32), axis=0, keepdims=True)
         for r in range(per):
             vg_s[c, 6 + r : 7 + r, :] = up_row[:, r * LANES : (r + 1) * LANES]
-    to_peers(lambda c: vg_s.at[c], vrx, VG)
-    wait_bytes(ga, recv.at[GA])
-    wait_bytes(gp, recv.at[GP])
+    to_members(lambda p: vg_s.at[p // z.groups], vrx, me, VG)
     many = z.peers * rows
-    dglu[...] = dot_tn(ga[...].reshape(many, width), gp[...].reshape(many, 2 * z.cw))
-    wait_bytes(fi, recv.at[FI])
-    wait_bytes(gh, recv.at[GH])
-    dup[...] = dot_tn(fi[...].reshape(many, width), gh[...].reshape(many, z.hid))
-    wait_bytes(ac, recv.at[AC])
-    wait_bytes(bg, recv.at[BG])
-    ddown[...] = dot_tn(ac[...].reshape(many, z.hid), bg[...].reshape(many, width))
+    grads = (
+        (ac, AC, bg, BG, z.hid, width, pdown, kdown, sdown, ldown, ddown),
+        (fi, FI, gh, GH, width, z.hid, pup, kup, sup, lup, dup),
+        (ga, GA, gp, GP, width, 2 * z.cw, pglu, kglu, sglu, lglu, dglu),
+    )
+    sibling, across = place(chan, low * 2 + 1 - core), place(chan, (1 - low) * 2 + core)
+    for t, (left, lp, right, rp, n_left, n_right, part, krx, *_) in enumerate(grads):
+        wait_bytes(left, recv.at[lp])
+        wait_bytes(right, recv.at[rp])
+        part[...] = dot_tn(left[...].reshape(many, n_left), right[...].reshape(many, n_right))
+        half = n_left // 2
+        other = pl.ds(pl.multiple_of((1 - core) * half, half), half)
+        remote(part.at[other], krx, GRADS + 3 * t, sibling).start()
+    pl.when(pipe > 0)(lags)
+    for t, (_, _, _, _, n_left, _, part, krx, lsend, lrx, _) in enumerate(grads):
+        half = n_left // 2
+        own = pl.ds(pl.multiple_of(core * half, half), half)
+        wait_bytes(krx, recv.at[GRADS + 3 * t])
+        lsend[...] = (part[own, :] + krx[...]).astype(bf16)
+        remote(lsend, lrx, GRADS + 3 * t + 1, across).start()
+
+    lag_low = high_low(lag_s[:, 0 : z.length])
+    both = dot_nt(lag_low, table[...])
+    grad_spec = both[0:ch] + both[ch : 2 * ch]
+    gk = (grad_spec[:, 0:padded], grad_spec[:, padded : 2 * padded])
+    y_all, ms, cross, over = moments()
+    g_top = times(conj(over), gk)
+    g_top = (-cosine * g_top[0], -cosine * g_top[1])
+    g_low = times(conj(times(times(cross, over), over)), gk)
+    g_three = (cosine * cosine * g_low[0], cosine * cosine * g_low[1])
+    g_ms = [gk, times(conj(ms[2]), g_top), times(conj(ms[1]), g_top), g_three]
+    g_rise = None
+    for v, (g_r, g_i) in enumerate(g_ms):
+        gsum_s[v] = 2.0 * cosine * g_r
+        gsum_s[4 + v] = -2.0 * cosine * g_i
+        gsum_s[8 + v] = 2.0 * y_all * g_i
+        gsum_s[12 + v] = 2.0 * y_all * g_r
+        part = 2.0 * (sums_s[12 + v] * g_r + sums_s[8 + v] * g_i)
+        g_rise = part if g_rise is None else g_rise + part
+    slope_s[...] = g_rise
+    gcol_s[...] = jnp.zeros(gcol_s.shape, f32)
+
+    def mode_step(h, carry):
+        double, y, cy, u, w = modes_at(h)
+        column = column_of(0, h)
+        gu, gw = 0.0, 0.0
+        acc = gcol_s[0, 0:nh, :]
+        for v in range(4):
+            a = column[:, v * ch : v * ch + 1]
+            b = column[:, (4 + v) * ch : (4 + v) * ch + 1]
+            au, aw = gsum_s[v, pl.ds(h, 1), :], gsum_s[4 + v, pl.ds(h, 1), :]
+            bu, bw = gsum_s[8 + v, pl.ds(h, 1), :], gsum_s[12 + v, pl.ds(h, 1), :]
+            gu = gu + a * au + b * bu
+            gw = gw + a * aw + b * bw
+            ga_col = jnp.sum(u * au + w * aw, axis=1, keepdims=True)
+            gb_col = jnp.sum(u * bu + w * bw, axis=1, keepdims=True)
+            acc = jnp.where(spot == v * ch + h, ga_col, acc)
+            acc = jnp.where(spot == (4 + v) * ch + h, gb_col, acc)
+        gcol_s[0, 0:nh, :] = acc
+        even, cross_uw = u * u - w * w, 2.0 * u * w
+        g_den_r = -(even * gu + cross_uw * gw)
+        g_den_i = even * gw - cross_uw * gu
+        acc = gcol_s[1, 0:nh, :]
+        ge = jnp.sum(cosine * cosine * g_den_r, axis=1, keepdims=True)
+        gf = jnp.sum(cy * g_den_i, axis=1, keepdims=True)
+        acc = jnp.where(spot == h, ge, acc)
+        gcol_s[1, 0:nh, :] = jnp.where(spot == ch + h, gf, acc)
+        gy = slope_s[pl.ds(h, 1), :] + jnp.sum(
+            double * cosine * g_den_i - 2.0 * y * g_den_r, axis=0, keepdims=True
+        )
+        total_y = jnp.sum(y * gy, axis=1, keepdims=True)
+        gstep_s[pl.ds(h, 1), :] = jnp.broadcast_to(-total_y, (1, LANES))
+        return carry
+
+    lax.fori_loop(0, ch, mode_step, 0)
+    back = gcol_s[0].T[:, 0:nh]
+    g_alpha = [back[v * ch : (v + 1) * ch] for v in range(4)]
+    g_beta = [back[(4 + v) * ch : (5 + v) * ch] for v in range(4)]
+    back = gcol_s[1].T[:, 0:nh]
+    g_square, g_double = back[0:ch], back[ch : 2 * ch]
+    g_decay = 2.0 * decay * g_square + 2.0 * g_double
+    g_rate = 2.0 * rate * g_square
+    g_pairs = []
+    for v, (v_r, v_i) in enumerate(pairs):
+        g_decay = g_decay + g_alpha[v] * v_r
+        if v_i is not None:
+            g_rate = g_rate - g_alpha[v] * v_i
+        g_pairs.append((decay * g_alpha[v] + g_beta[v], -rate * g_alpha[v]))
+    c_b, c_p, p_b = g_pairs[0], g_pairs[1], g_pairs[2]
+    p_p = g_pairs[3][0]
+    rank, into, out = (rank_r, rank_i), (in_r, in_i), (out_r, out_i)
+
+    def plus(*terms):
+        return sum(t[0] for t in terms), sum(t[1] for t in terms)
+
+    g_out = plus(times(conj(into), c_b), times(conj(rank), c_p))
+    g_in = plus(times(conj(out), c_b), times(rank, p_b))
+    g_rank = plus(
+        times(conj(out), c_p),
+        times(into, conj(p_b)),
+        (2.0 * rank_r * p_p, 2.0 * rank_i * p_p),
+    )
+    for p, value in enumerate((g_decay, g_rate, *g_rank, *g_in, *g_out)):
+        modes_tx[p, :, 0:nh] = value
+    modes_tx[8] = jnp.where(spot == 0, gstep_s[...], lag_s[:, 0:LANES])
+    modes_tx[9] = lag_s[:, 0:LANES]
+    for k in range(1, z.groups):
+        remote(modes_tx, modes_rx.at[data], MODES, place(chan, lax.rem(data + k, z.groups))).start()
+    pltpu.make_async_copy(modes_tx, modes_rx.at[data], recv.at[MODES]).start()
+
+    for t, (_, _, _, _, n_left, _, _, _, lsend, lrx, final) in enumerate(grads):
+        half = n_left // 2
+        own = pl.ds(pl.multiple_of(core * half, half), half)
+        wait_bytes(lrx, recv.at[GRADS + 3 * t + 1])
+        final[own, :] = lsend[...].astype(f32) + lrx[...].astype(f32)
+        remote(final.at[own], final.at[own], GRADS + 3 * t + 2, sibling).start()
+
+    def collect(source, target):
+        for m in range(z.micros):
+            parts = [
+                own_half(source[m * z.quarters + q].astype(f32))[0:tok] for q in range(z.quarters)
+            ]
+            target[m] = jnp.concatenate(parts, axis=0)[:, 0 : z.cw].astype(bf16)
+
+    wait_bytes(hid_rx, recv.at[HID])
+    collect(hid_rx, hid_out)
+    wait_bytes(ig_rx, recv.at[IG])
+    collect(ig_rx, ig_out)
     wait_bytes(vrx, recv.at[VG])
     summed = vrx[0]
-    for c in range(1, z.peers):
-        summed = summed + vrx[c]
-    vec_out[...] = summed
-    wait_bytes(hid_out, recv.at[HID])
-    wait_bytes(ig_out, recv.at[IG])
-
+    for p in range(1, z.members):
+        summed = summed + vrx[p]
+    upb_out[...] = jnp.concatenate([summed[6 + r : 7 + r, :] for r in range(per)], axis=1)
+    summed = own_half(summed)
+    ffn_out[...] = summed[2:5, 0 : z.cw]
+    glub_out[0:1, :] = summed[5:6, 0 : z.cw]
+    glub_out[1:2, :] = shifted(summed[5:6], LANES // 2)[:, 0 : z.cw]
+    vec_out[0:2, :] = summed[0:2, 0 : z.cw]
+    wait_bytes(modes_rx, recv.at[MODES])
+    for p in range(8):
+        for d in range(z.groups):
+            modes_out[p, d * ch : (d + 1) * ch, :] = modes_rx[d, p, :, 0:nh]
+    for d in range(z.groups):
+        turn_s[0, d * ch : (d + 1) * ch, :] = modes_rx[d, 8]
+        turn_s[1, d * ch : (d + 1) * ch, :] = modes_rx[d, 9]
+    vec_out[2:3, :] = turn_s[0].T[0:1, 0 : z.cw]
+    vec_out[3:4, :] = turn_s[1].T[0:1, 0 : z.cw]
+    for t, (_, _, _, _, n_left, _, _, _, _, _, final) in enumerate(grads):
+        half = n_left // 2
+        other = pl.ds(pl.multiple_of((1 - core) * half, half), half)
+        wait_bytes(final.at[other], recv.at[GRADS + 3 * t + 2])
+
+    for t in (GLU, UP, DOWN):
+        weights_sent(t)
     for ref, phase in (
-        (vec_all, VEC), (glu_all, GLU), (up_all, UP), (down_all, DOWN), (hid_out, HID),
-        (ig_out, IG), (ga, GA), (fi, FI), (ac, AC), (bg, BG), (gh, GH), (gp, GP), (vrx, VG),
+        (vec_all, VEC), (hid_rx, HID),
+        (ig_rx, IG), (ga, GA), (fi, FI), (ac, AC), (bg, BG), (gh, GH), (gp, GP),
     ):
         wait_bytes(ref.at[pl.ds(0, z.peers - 1)], send.at[phase])
-    for ref, phase in ((rx1, A1), (rx2, A2), (rx3, A3), (rx4, A4)):
+    for ref, phase in ((rx1, A1), (rx2, A2), (rx3, A3), (rx4, A4), (vrx, VG)):
         wait_bytes(ref.at[pl.ds(0, z.members - 1)], send.at[phase])
+    wait_bytes(modes_rx.at[pl.ds(0, z.groups - 1)], send.at[MODES])
+    for t, (_, _, _, _, n_left, _, _, krx, lsend, _, final) in enumerate(grads):
+        wait_bytes(krx, send.at[GRADS + 3 * t])
+        wait_bytes(lsend, send.at[GRADS + 3 * t + 1])
+        wait_bytes(final.at[pl.ds(0, n_left // 2)], send.at[GRADS + 3 * t + 2])
 
     @pl.when(pipe == 0)
     def _():
@@ -582,7 +885,6 @@
     down_weight,
 ):
     chan = lax.axis_index("chan")
-    data = lax.axis_index("dp")
     micros, tok_rows, chan_width = tokens.shape
     width = glu_weight.shape[1]
     hidden = up_weight.shape[2]
@@ -593,143 +895,85 @@
     odd = lax.rem(chan, 2) == 1
     length = z.length
     padded = -(-(length // 2 + 1) // LANES) * LANES
-    vectors = s4_vectors[0]
-    own_vectors = lax.dynamic_slice_in_dim(vectors, data * z.ch, z.ch, 1)
-    own_modes = lax.dynamic_slice_in_dim(s4_modes[0], data * z.ch, z.ch, 1)
-
-    def spectrum_of(log_step, modes):
-        return kernel_of(log_step, modes, length, padded)
-
-    kern, pull = jax.vjp(spectrum_of, own_vectors[2], own_modes)
-    kern_wide = jnp.pad(kern, ((0, 0), (0, LANES)))
-    near, far = pl.pallas_call(
-        lambda *refs: toeplitz_kernel(z.blocks, *refs),
-        out_shape=(
-            jax.ShapeDtypeStruct((z.ch, length, LANES), bf16),
-            jax.ShapeDtypeStruct((z.ch, LANES, length), bf16),
-        ),
-        in_specs=[pl.BlockSpec(memory_space=pltpu.VMEM)],
-        out_specs=[pl.BlockSpec(memory_space=pltpu.VMEM)] * 2,
-        compiler_params=pltpu.CompilerParams(vmem_limit_bytes=40 * 2**20),
-        name="toeplitz",
-    )(kern_wide)
-
-    def blocks_of(x):
-        x = x.reshape(z.peers, z.tok, chan_width)
-        x = jnp.pad(x, ((0, 0), (0, z.rows - z.tok), (0, 0)))
-        return jnp.concatenate([x, x], axis=2)
+    nh = s4_modes.shape[3]
 
     def swap(value, gate):
         return jnp.where(
             odd, jnp.concatenate([gate, value], -1), jnp.concatenate([value, gate], -1)
         )
 
-    ffn = ffn_vectors[0]
-    twice = jnp.stack([vectors[0], vectors[1], ffn[0], ffn[1], ffn[2]])
-    vec = jnp.concatenate(
-        [
-            jnp.concatenate([twice, twice], axis=1),
-            swap(glu_bias[0, 0], glu_bias[0, 1])[None],
-            up_bias[0].astype(f32).reshape(hidden // LANES, LANES),
-        ],
-        axis=0,
-    )
     glu_loc = swap(glu_weight[0, :, 0, :], glu_weight[0, :, 1, :])
-    ends = jnp.cumsum(seq_lengths, axis=1)
-    begins = ends - seq_lengths
-    positions = jnp.arange(length, dtype=jnp.int32)
-    masks = (
-        (positions[None, None, :] >= begins[:, :, None])
-        & (positions[None, None, :] < ends[:, :, None])
-    ).astype(f32)
-    masks = masks.reshape(z.gr, z.blocks, LANES).transpose(1, 0, 2).reshape(-1, LANES)
-    skip = jnp.broadcast_to(own_vectors[3][:, None], (z.ch, LANES))
+    table = jnp.asarray(fourier_table(length, padded).astype(ml_dtypes.bfloat16))
+    angles = jnp.asarray(half_angles(length, padded))
 
     vmem = pl.BlockSpec(memory_space=pltpu.VMEM)
-    n, r, w = z.peers, z.rows, width
-
-    def s(shape, kind=bf16):
+    smem = pl.BlockSpec(memory_space=pltpu.SMEM)
+    anywhere = pl.BlockSpec(memory_space=pl.ANY)
+    n, r, w, ch = z.peers, z.rows, width, z.ch
+
+    def s(shape, kind=f32):
         return jax.ShapeDtypeStruct(shape, kind)
 
     def v(shape, kind=bf16):
         return pltpu.VMEM(shape, kind)
 
     exchange = (z.members, z.ch, LANES)
-    hid_blocks, ig_blocks, dglu, dup, ddown, vec_sum, xs, gs = pl.pallas_call(
+    conv_rows = -(-(z.blocks * z.gr) // 8) * 8
+    wide = (z.blocks + 1) * LANES
+    hid, ig, vec, modes, dglu, glub, ffn, dup, upb, ddown = pl.pallas_call(
         lambda *refs: main_kernel(z, *refs),
         out_shape=(
-            s((n, r, LANES)), s((n, r, LANES)), s((w, 2 * chan_width), f32), s((w, hidden), f32),
-            s((hidden, w), f32), s((8, LANES), f32), s((z.stack, LANES), f32),
-            s((z.stack, LANES), f32),
+            s((micros, tok_rows, chan_width), bf16), s((micros, tok_rows, chan_width), bf16),
+            s((4, chan_width)), s((8, chan_width, nh)), s((w, 2 * chan_width)),
+            s((2, chan_width)), s((3, chan_width)), s((w, hidden)), s((1, hidden)),
+            s((hidden, w)),
         ),
-        in_specs=[vmem] * 10,
-        out_specs=[vmem] * 8,
+        in_specs=[smem] + [vmem] * 11 + [anywhere],
+        out_specs=[vmem] * 10,
         scratch_shapes=[
+            v((n, r, LANES)), v((n, r, LANES)), v((8, LANES), f32), v((ch, length, LANES)),
+            v((ch, LANES, length)), v((ch, LANES), f32), v((conv_rows, LANES), f32),
+            v((n, r, LANES)), v((n, r, LANES)), v((z.stack, LANES), f32),
+            v((z.stack, LANES), f32),
+            v((2 * padded, length)), v((2, LANES, LANES), f32), v((2, nh, LANES), f32),
+            v((ch, LANES), f32), v((16, ch, padded), f32), v((16, ch, padded), f32),
+            v((ch, padded), f32), v((ch, wide), f32), v((ch, wide), f32),
+            v((2, LANES, LANES), f32), v((ch, LANES), f32),
+            v((10, ch, LANES), f32), v((z.groups, 10, ch, LANES), f32),
+            v((w, 2 * chan_width), f32), v((w, hidden), f32), v((hidden, w), f32),
+            v((w // 2, 2 * chan_width), f32), v((w // 2, hidden), f32), v((hidden // 2, w), f32),
+            v((w // 2, 2 * chan_width)), v((w // 2, hidden)), v((hidden // 2, w)),
+            v((w // 2, 2 * chan_width)), v((w // 2, hidden)), v((hidden // 2, w)),
             v((n, 8, LANES), f32), v((n, w, 2 * chan_width)), v((n, w, hidden)),
             v((n, hidden, w)), v((n, r, LANES)), v((n, r, LANES)), v((r, w)), v((r, w)),
         ]
         + [v(exchange)] * 8
         + [
-            v((z.micros * z.blocks, z.ch, LANES), f32),
-            v((-(-(z.blocks * z.gr) // 8) * 8 * z.ch, LANES), f32),
+            v((z.micros * z.blocks, z.ch, LANES), f32), v((conv_rows * z.ch, LANES), f32),
             v((r, w), f32), v((r, LANES), f32), v((r, w), f32), v((r, LANES), f32),
             v((r, w), f32), v((r, w), f32), v((n, r, hidden), f32),
             v((r, w)), v((r, w)), v((n, r, hidden)), v((n, r, hidden)), v((n, r, LANES)),
             v((n // 2, r, LANES)), v((r, w)), v((n // 2, r, LANES)), v((r, w)),
             v((n, 8, LANES), f32),
             v((n, r, w)), v((n, r, w)), v((n, r, hidden)), v((n, r, w)), v((n, r, hidden)),
-            v((n, r, LANES)), v((n, 8, LANES), f32),
-            pltpu.SemaphoreType.DMA((21,)), pltpu.SemaphoreType.DMA((21,)),
+            v((n, r, LANES)), v((z.members, 8, LANES), f32),
+            pltpu.SemaphoreType.DMA((48,)), pltpu.SemaphoreType.DMA((48,)),
         ],
         compiler_params=pltpu.CompilerParams(
             collective_id=0, has_side_effects=True, vmem_limit_bytes=60 * 2**20
         ),
         name="layers",
     )(
-        blocks_of(tokens), blocks_of(out_cot), vec, glu_loc, up_weight[0], down_weight[0],
-        near, far, skip, masks,
+        seq_lengths, tokens, out_cot, s4_vectors[0], s4_modes[0], glu_loc, glu_bias[0],
+        ffn_vectors[0], up_weight[0], up_bias, down_weight[0], angles, table,
     )
-
-    lags = pl.pallas_call(
-        lambda *refs: lag_kernel(z.blocks, *refs),
-        out_shape=s((z.ch, (z.blocks + 1) * LANES), f32),
-        in_specs=[vmem] * 2,
-        out_specs=vmem,
-        name="lags",
-    )(xs, gs)
-    grad_kern = lags[:, :length]
-    step_grad, mode_grad = pull(grad_kern)
-
-    def whole(blocks):
-        x = jnp.where(odd, blocks[:, : z.tok, chan_width:], blocks[:, : z.tok, :chan_width])
-        return x.reshape(1, micros, tok_rows, chan_width)
-
-    reduced = lax.psum((dglu, dup, ddown, vec_sum), "dp")
-    red_glu, red_up, red_down, red_vec = reduced
-    extra = jnp.stack([step_grad, grad_kern[:, 0]])
-    packed = jnp.concatenate([mode_grad.transpose(1, 0, 2).reshape(z.ch, -1), extra.T], axis=1)
-    gathered = lax.all_gather(packed, "dp", axis=0, tiled=True)
-    split = gathered.shape[1] - 2
-    mode_full = gathered[:, :split].reshape(chan_width, 8, -1).transpose(1, 0, 2)
-    first, second = red_vec[:, :chan_width], red_vec[:, chan_width:]
-    mine = jnp.where(odd, second, first)
-    other = jnp.where(odd, first, second)
-    grad_vectors = jnp.stack([mine[0], mine[1], gathered[:, split], gathered[:, split + 1]])[None]
-    glu_first, glu_second = red_glu[:, :chan_width], red_glu[:, chan_width:]
+    glu_first, glu_second = dglu[:, :chan_width], dglu[:, chan_width:]
     grad_glu = jnp.stack(
         [jnp.where(odd, glu_second, glu_first), jnp.where(odd, glu_first, glu_second)], axis=1
     )
     return (
-        whole(hid_blocks),
-        whole(ig_blocks),
-        grad_vectors,
-        mode_full[None],
-        grad_glu[None],
-        jnp.stack([mine[5], other[5]])[None],
-        mine[2:5][None],
-        red_up[None],
-        red_vec[6:].reshape(1, hidden),
-        red_down[None],
+        hid[None], ig[None], vec[None], modes[None], grad_glu[None], glub[None], ffn[None],
+        dup[None], upb, ddown[None],
     )
 
 

time: 405 us -> 246 us (0.61)
  Pallas kernels: 315 us -> 221 us
  matrix products: 17.5 us -> 0 us
  other arithmetic: 16.5 us -> 2.01 us
  between operations: 14.9 us -> 0.74 us
  blocking collectives: 12.1 us -> 0 us
  local copies, waits for them, and re-layouts: 28.4 us -> 18.1 us
    pallas_call x3 -> x1, Pallas kernels: 315 us -> 221 us  [body(): pl.pallas_call(lambda *refs: main_kernel(z, *refs), out_shape=(s((micros,...]
    dot_general x6 -> x0, matrix products: 17.5 us -> none  [the longest x3 10.6 us: kernel_of(): jnp.dot(jnp.concatenate([spec_r, spec_i], axis=1), table, precision=highest)]
    slice x12 -> x0, local copies, waits for them, and re-layouts: 8.49 us -> none  [the longest x2 2.51 us: body(): twice = jnp.stack([vectors[0], vectors[1], ffn[0], ffn[1], ffn[2]])]
    psum x1 -> x0, blocking collectives: 6.26 us -> none  [body(): reduced = lax.psum((dglu, dup, ddown, vec_sum), 'dp')]
    all_gather x1 -> x0, blocking collectives: 5.8 us -> none  [body(): gathered = lax.all_gather(packed, 'dp', axis=0, tiled=True)]
    unnamed x148 -> x26, local copies, waits for them, and re-layouts: 12 us -> 17.2 us
  transfers between devices with their start and end apart: 1 -> 0, of which waited for: 0 -> 0; matrix products, arithmetic and copies ran while one was open for 7% -> 0% of each run, Pallas kernels for 3% -> 0%
where the time goes in v2:
time: 246 us; the launch traced here: 242 us
  Pallas kernels  221 us (90%)
  local copies, waits for them, and re-layouts  18.1 us (7%)
    pallas_call x1, Pallas kernels, body(): pl.pallas_call(lambda *refs: main_kernel(z, *refs), out_shape=(s((micros,...  221 us
    unnamed x26, local copies, waits for them, and re-layouts  17.2 us

profile of v2, /device:TPU:1, one launch (start us, length us, event | category | flops | bytes accessed | tf_op | source)
XLA Modules:
  0.0 241.5 jit_solution(3846944863407339639)
XLA Ops:
  0.6 1.3 copy.37
  1.9 0.9 fusion
  2.8 0.1 copy.34
  2.9 0.1 copy.35
  3.0 0.8 maximum_select_fusion.refs_5_
  3.9 1.7 copy.26.refs_1_
  5.5 1.7 copy.27.refs_2_
  7.2 1.7 copy.23
  9.0 220.7 %layers.1 = (bf16[2,288,64]{2,1,0:T(8,128)(2,1)}, bf16[2,288,64]{2,1,0:T(8,128)(2,1)}, f32[4,64]{1,0:T(4,128)}, f32[8,64,32]{2,1,0:T(8,128)}, f32[512,128]{1,0:T...) custom-call(s32[2,2]{1,0:T(2,128)} %refs_0_.1, ...), custom_call_target="tpu_custom_call" | custom-call | tf_op jit(solution)/shard_map/layers/pallas_call | solution.py:923
  229.7 0.0 copy-start.2
  229.7 0.0 copy-start.4
  229.7 0.0 copy-start.1
  229.7 0.0 copy-start.3
  229.7 1.8 copy.28
  231.5 1.7 copy.29
  233.1 1.2 copy.32
  234.4 1.7 copy.30
  236.1 1.2 select_bitcast_fusion.1
  237.3 0.9 copy.31
  238.2 0.6 copy.43
  238.8 0.6 copy.44
  239.4 0.8 copy.45
  240.2 0.6 copy.46
  240.7 0.8 copy.47
  (7 shorter events, 0.1 us)
Async XLA Ops:
  229.7 8.5 %copy-start.2 = (f32[4,64]{1,0:T(4,128)S(1)}, f32[4,64]{1,0:T(4,128)}, u32[]{:S(2)}) copy-start(f32[4,64]{1,0:T(4,128)} %get-tuple-element.22) | copy-start | bytes 3076
  229.7 9.1 %copy-start.4 = (f32[2,64]{1,0:T(2,128)S(1)}, f32[2,64]{1,0:T(2,128)}, u32[]{:S(2)}) copy-start(f32[2,64]{1,0:T(2,128)} %get-tuple-element.25) | copy-start | bytes 1540
  229.7 9.7 %copy-start.1 = (f32[512,256]{1,0:T(8,128)S(1)}, f32[512,256]{1,0:T(8,128)}, u32[]{:S(2)}) copy-start(f32[512,256]{1,0:T(8,128)} %get-tuple-element.27) | copy-start | bytes 1572868
  229.7 10.5 %copy-start.3 = (f32[1,256]{1,0:T(1,128)S(1)}, f32[1,256]{1,0:T(1,128)}, u32[]{:S(2)}) copy-start(f32[1,256]{1,0:T(1,128)} %get-tuple-element.62) | copy-start | bytes 3076
  229.7 11.0 %copy-start = (f32[256,512]{1,0:T(8,128)S(1)}, f32[256,512]{1,0:T(8,128)}, u32[]{:S(2)}) copy-start(f32[256,512]{1,0:T(8,128)} %get-tuple-element.29) | copy-start | bytes 1572868

commit v3 on v2

v3 whole, which is shorter than its diff:
```python
import math

import jax
import jax.numpy as jnp
import ml_dtypes
import numpy as np
from jax import lax
from jax.experimental import pallas as pl
from jax.experimental.pallas import tpu as pltpu
from jax.sharding import PartitionSpec as P

norm_eps = 1e-05
f32 = jnp.float32
bf16 = jnp.bfloat16
LANES = 128


def fourier_table(length, padded):
    half = length // 2
    freq = np.arange(padded, dtype=np.int64)[:, None]
    time = np.arange(length, dtype=np.int64)[None, :]
    angle = (freq * (2 * time + 1) % (2 * length)) * (np.pi / length)
    weight = np.where(freq <= half, np.where((freq == 0) | (freq == half), 1.0, 2.0), 0.0) / length
    table = np.concatenate([np.cos(angle) * weight, -np.sin(angle) * weight], axis=0)
    return table.astype(np.float32)


def half_angles(length, padded):
    angle = np.minimum(np.arange(padded), length // 2) * (np.pi / length)
    rows = np.zeros((8, padded), np.float32)
    rows[0] = np.where(np.arange(padded) < length // 2, np.cos(angle), 0.0)
    rows[1] = np.sin(angle)
    return rows


def shifted(x, by):
    size = x.shape[-1]
    by = by % size
    if by == 0:
        return x
    return pltpu.roll(x, by, x.ndim - 1)


def gelu(x):
    return 0.5 * x * (1.0 + jnp.tanh(math.sqrt(2.0 / math.pi) * (x + 0.044715 * x * x * x)))


def gelu_slope(x):
    scale = math.sqrt(2.0 / math.pi)
    t = jnp.tanh(scale * (x + 0.044715 * x * x * x))
    return 0.5 * (1.0 + t) + 0.5 * x * (1.0 - t * t) * scale * (1.0 + 3.0 * 0.044715 * x * x)


def dot(a, b):
    return lax.dot_general(a, b, (((1,), (0,)), ((), ())), preferred_element_type=f32)


def dot_nt(a, b):
    return lax.dot_general(a, b, (((1,), (1,)), ((), ())), preferred_element_type=f32)


def dot_tn(a, b):
    return lax.dot_general(a, b, (((0,), (0,)), ((), ())), preferred_element_type=f32)


class Sizes:
    def __init__(self, sections, peers, groups, tok_rows, chan_width, model_width, hidden):
        self.sections, self.peers, self.groups = sections, peers, groups
        self.micros = 2
        self.segments = 2
        self.quarters = peers // self.micros
        self.tok = tok_rows // self.quarters
        self.rows = -(-self.tok // 16) * 16
        self.length = tok_rows * groups
        self.blocks = self.length // LANES
        self.width = model_width
        self.cw = chan_width
        self.hid = hidden
        self.members = peers * groups
        self.ch = model_width // self.members
        self.slots = self.quarters * groups
        self.gr = self.micros * self.segments
        self.stack = (2 * self.blocks) * self.gr * self.ch


def main_kernel(z, *refs):
    (
        lengths, tokens, out_cot, vectors, modes, glu_loc, glu_bias, ffn_vec, up_loc, up_bias,
        down_loc, angles, table_in,
    ) = refs[:13]
    (
        hid_out, ig_out, vec_out, modes_out, glu_out, glub_out, ffn_out, dup, upb_out, ddown,
    ) = refs[13:23]
    (
        tok_tx, cot_tx, vec_tx, near, far, skip, masks, hid_rx, ig_rx, xs, gs,
        table, cols, rise_s, sums_s, gsum_s, slope_s, kern_s, lag_s, gcol_s, gstep_s,
        modes_tx, modes_rx, pglu, pup, pdown, kglu, kup, kdown, sglu, sup, sdown,
        lglu, lup, ldown, dglu,
        vec_all, vec_next, glu_all, up_all, down_all, tok_rx, cot_rx, res, gtop,
        tx1, tx1n, rx1, tx2, rx2, tx3, rx3, tx4, rx4, rx4n,
        conv_out, ys, hat1_s, inv1_s, hatn_s, invn_s, hat2_s, inv2_s, val_s, sig_s, hidden_s,
        gated_s, ffn_s, act_s, gh_s, gp_s, lay_s, lay_t, ig_t, ign_t, mid_s, mid_rx,
        vg_s, vgn_s, vg0_s, ga, fi, ac, bg, gh, gp, vrx, vnrx, send, recv,
    ) = refs[23:]
    pipe = lax.axis_index("pipe")
    chan = lax.axis_index("chan")
    data = lax.axis_index("dp")
    last = z.sections - 1
    me = chan * z.groups + data
    slot_me = (chan // z.quarters) * z.slots + data * z.quarters + lax.rem(chan, z.quarters)
    rows, width, tok = z.rows, z.width, z.tok
    spot = lax.broadcasted_iota(jnp.int32, (1, LANES), 1)
    first_half = spot < (LANES // 2)
    row_ok = lax.broadcasted_iota(jnp.int32, (rows, 1), 0) < tok
    odd = lax.rem(chan, 2)
    per = z.hid // LANES

    def slot_of(p):
        c, d = p // z.groups, lax.rem(p, z.groups)
        return (c // z.quarters) * z.slots + d * z.quarters + lax.rem(c, z.quarters)

    def place(c, d, section=None):
        return {"pipe": pipe if section is None else section, "chan": c, "dp": d}

    def member(p, section=None):
        return place(p // z.groups, lax.rem(p, z.groups), section)

    def remote(src, dst, phase, where):
        return pltpu.make_async_remote_copy(
            src_ref=src,
            dst_ref=dst,
            send_sem=send.at[phase],
            recv_sem=recv.at[phase],
            device_id=where,
            device_id_type=pl.DeviceIdType.MESH,
        )

    def wait_bytes(ref, sem):
        pltpu.make_async_copy(ref, ref, sem).wait()

    def to_peers(src_of, dst, phase):
        def step(k, carry):
            c = lax.rem(chan + k, z.peers)
            remote(src_of(c), dst.at[chan], phase, place(c, data)).start()
            return carry

        lax.fori_loop(1, z.peers, step, 0)
        pltpu.make_async_copy(src_of(chan), dst.at[chan], recv.at[phase]).start()

    def to_members(src_of, dst, slot, phase):
        def step(k, carry):
            p = lax.rem(me + k, z.members)
            remote(src_of(p), dst.at[slot], phase, member(p)).start()
            return carry

        lax.fori_loop(1, z.members, step, 0)
        pltpu.make_async_copy(src_of(me), dst.at[slot], recv.at[phase]).start()

    def to_section(src_of, dst, slot, phase, section):
        def step(k, carry):
            p = lax.rem(me + k, z.members)
            remote(src_of(p), dst.at[slot], phase, member(p, section)).start()
            return carry

        lax.fori_loop(0, z.members, step, 0)

    def to_section_peers(src_of, dst, phase, section):
        def step(k, carry):
            c = lax.rem(chan + k, z.peers)
            remote(src_of(c), dst.at[chan], phase, place(c, data, section)).start()
            return carry

        lax.fori_loop(0, z.peers, step, 0)

    (
        VEC, VECN, TOK, COT, A1, A2, A3, A4, A4N, RES, MID, HID, IG, GA, FI, AC, BG, GH, GP, VG,
        VGN, TABLE, MODES,
    ) = range(23)
    GLU, UP, DOWN, GRADS = 23, 29, 35, 41

    high, deep = chan // z.quarters, lax.rem(chan, z.quarters)
    side, core = data // 2, lax.rem(data, 2)
    own_side, far_side = high * z.quarters, (1 - high) * z.quarters
    sibling, across = place(chan, side * 2 + 1 - core), place(chan, (1 - side) * 2 + core)

    def piece_of(t, c, count, part=None):
        if t == GLU:
            if part is None:
                return glu_all.at[core, pl.ds(c, count)]
            fourth = z.cw // 2
            start = pl.multiple_of(part * fourth, fourth)
            return glu_all.at[core, pl.ds(c, count), pl.ds(start, fourth)]
        loc, whole = (up_loc, up_all) if t == UP else (down_loc, down_all)
        half = loc.shape[0] // 2
        fourth = half // 2
        if part is None:
            return whole.at[pl.ds(c, count), pl.ds(pl.multiple_of(core * half, half), half)]
        start = pl.multiple_of(core * half + part * fourth, fourth)
        return whole.at[pl.ds(c, count), pl.ds(start, fourth)]

    def weights_ring(t):
        if t == GLU:
            loc, whole, mine = glu_loc, glu_all.at[:, chan], glu_loc.at[core]
        else:
            loc, whole = (up_loc, up_all) if t == UP else (down_loc, down_all)
            half = loc.shape[0] // 2
            whole, mine = whole.at[chan], loc.at[pl.ds(pl.multiple_of(core * half, half), half)]
        pltpu.make_async_copy(loc, whole, recv.at[t + 5]).start()
        for k in range(1, z.quarters):
            c = own_side + lax.rem(deep + k, z.quarters)
            there = piece_of(t, chan, 1).at[0]
            remote(mine, there, t, place(c, data)).start()

    def weights_across(t):
        loc = {GLU: glu_loc, UP: up_loc, DOWN: down_loc}[t]
        wait_bytes(piece_of(t, 0, z.quarters - 1), recv.at[t])
        wait_bytes(loc, recv.at[t + 5])
        piece = piece_of(t, own_side, z.quarters, side)
        where = place(far_side + deep, (1 - side) * 2 + core)
        remote(piece, piece, t + 1, where).start()
        for k in range(1, z.quarters):
            piece = piece_of(t, own_side + lax.rem(deep + k, z.quarters), 1)
            remote(piece, piece, t + 3, sibling).start()

    def weights_beside(t):
        wait_bytes(piece_of(t, 0, z.quarters, 0), recv.at[t + 1])
        piece = piece_of(t, far_side, z.quarters, 1 - side)
        remote(piece, piece, t + 2, across).start()

    def weights_core(t):
        wait_bytes(piece_of(t, 0, z.quarters, 0), recv.at[t + 2])
        piece = piece_of(t, far_side, z.quarters)
        remote(piece, piece, t + 4, sibling).start()

    def weights_here(t):
        wait_bytes(piece_of(t, 0, z.quarters - 1), recv.at[t + 3])
        wait_bytes(piece_of(t, 0, z.quarters), recv.at[t + 4])

    def weights_sent(t):
        for stage, count, part in (
            (0, z.quarters - 1, None), (1, z.quarters, 0), (2, z.quarters, 0),
            (3, z.quarters - 1, None), (4, z.quarters, None),
        ):
            wait_bytes(piece_of(t, 0, count, part), send.at[t + stage])

    barrier = pltpu.get_barrier_semaphore()

    def greet(p, section):
        pl.semaphore_signal(
            barrier, inc=1, device_id=member(p, section), device_id_type=pl.DeviceIdType.MESH
        )

    def greet_own(k, carry):
        greet(lax.rem(me + k, z.members), None)
        return carry

    def greet_next(k, carry):
        greet(lax.rem(me + k, z.members), pipe + 1)
        return carry

    def greet_before(k, carry):
        greet(lax.rem(me + k, z.members), pipe - 1)
        return carry

    lax.fori_loop(1, z.members, greet_own, 0)

    @pl.when(pipe < last)
    def _():
        lax.fori_loop(0, z.members, greet_next, 0)

    @pl.when(pipe > 0)
    def _():
        lax.fori_loop(0, z.members, greet_before, 0)

    pltpu.make_async_copy(table_in, table, recv.at[TABLE]).start()

    def own_half(x):
        return pltpu.roll(x, odd * (LANES // 2), x.ndim - 1)

    def fill_blocks(source, target):
        count = z.tok * z.quarters
        over = -(-count // LANES) * LANES
        for m in range(z.micros):
            x = source[m].astype(f32)
            x = jnp.concatenate([x, jnp.zeros((z.cw, over - count), f32)], axis=1)
            for q in range(z.quarters):
                target[m * z.quarters + q] = shifted(x, over - q * tok)[:, 0:LANES].astype(bf16)

    vec_rows = [vectors[0:1, :], vectors[1:2, :]] + [ffn_vec[r] for r in range(3)]
    vec_rows += [glu_bias[0:1, :], glu_bias[1:2, :]]
    for r, row in enumerate(vec_rows):
        vec_tx[r : r + 1, :] = jnp.concatenate([row, row], axis=1)
    for r in range(per):
        vec_tx[7 + r : 8 + r, :] = up_bias[:, r * LANES : (r + 1) * LANES].astype(f32)
    pl.when(pipe == 0)(lambda: fill_blocks(tokens, tok_tx))
    pl.when(pipe == last)(lambda: fill_blocks(out_cot, cot_tx))

    ch, nh = z.ch, modes.shape[1]

    def own_lanes(x):
        x = jnp.concatenate([x, jnp.zeros((x.shape[0], LANES - z.cw), f32)], axis=1)
        return pltpu.roll(x, lax.rem(LANES - data * ch, LANES), 1)

    def packed(items):
        total = items[0]
        for i, item in enumerate(items[1:], 1):
            total = jnp.where(spot // ch == i, shifted(item, i * ch), total)
        return total

    decay, rate, rank_r, rank_i, in_r, in_i, out_r, out_i = (own_lanes(modes[p]) for p in range(8))
    pairs = [
        (out_r * in_r - out_i * in_i, out_r * in_i + out_i * in_r),
        (out_r * rank_r - out_i * rank_i, out_r * rank_i + out_i * rank_r),
        (rank_r * in_r + rank_i * in_i, rank_r * in_i - rank_i * in_r),
        (rank_r * rank_r + rank_i * rank_i, None),
    ]
    alphas = [
        decay * v_r if v_i is None else decay * v_r - rate * v_i for v_r, v_i in pairs
    ]
    cols[0] = packed(alphas + [v_r for v_r, v_i in pairs])
    cols[1] = packed([decay * decay + rate * rate, 2.0 * decay])
    own_vectors = own_lanes(vectors[...])
    diagonal = lax.broadcasted_iota(jnp.int32, (ch, LANES), 0) == lax.broadcasted_iota(
        jnp.int32, (ch, LANES), 1
    )

    def upright(row):
        column = jnp.sum(jnp.where(diagonal, row, 0.0), axis=1, keepdims=True)
        return jnp.broadcast_to(column, (ch, LANES))

    rise_s[...] = 2.0 * jnp.exp(-upright(own_vectors[2:3]))
    skip[...] = upright(own_vectors[3:4])
    cosine, sine = angles[0:1, :], angles[1:2, :]
    padded = angles.shape[1]

    def column_of(k, h):
        return pltpu.roll(cols[k], lax.rem(LANES - h, LANES), 1)

    def modes_at(h):
        two = column_of(1, h)
        square, double = two[:, 0:1], two[:, ch : ch + 1]
        y = rise_s[pl.ds(h, 1), 0:1] * sine
        cy = cosine * y
        den_r = square * (cosine * cosine) - y * y
        den_i = double * cy
        inverse = 1.0 / (den_r * den_r + den_i * den_i)
        return double, y, cy, den_r * inverse, den_i * inverse

    def cauchy_one(h):
        _, _, _, u, w = modes_at(h)
        column = column_of(0, h)
        for v in range(4):
            a = column[:, v * ch : v * ch + 1]
            b = column[:, (4 + v) * ch : (4 + v) * ch + 1]
            sums_s[v, pl.ds(h, 1), :] = jnp.sum(a * u, axis=0, keepdims=True)
            sums_s[4 + v, pl.ds(h, 1), :] = jnp.sum(a * w, axis=0, keepdims=True)
            sums_s[8 + v, pl.ds(h, 1), :] = jnp.sum(b * u, axis=0, keepdims=True)
            sums_s[12 + v, pl.ds(h, 1), :] = jnp.sum(b * w, axis=0, keepdims=True)

    def each_channel(one, unroll):
        def step(i, carry):
            for u in range(unroll):
                one(i * unroll + u)
            return carry

        if unroll == ch:
            step(0, 0)
        else:
            lax.fori_loop(0, ch // unroll, step, 0)

    def times(a, b):
        return a[0] * b[0] - a[1] * b[1], a[0] * b[1] + a[1] * b[0]

    def conj(a):
        return a[0], -a[1]

    def moments():
        y_all = rise_s[:, 0:1] * sine
        ms = [
            (
                2.0 * (cosine * sums_s[v] + y_all * sums_s[12 + v]),
                2.0 * (y_all * sums_s[8 + v] - cosine * sums_s[4 + v]),
            )
            for v in range(4)
        ]
        low_r, low_i = 1.0 + cosine * ms[3][0], cosine * ms[3][1]
        size = 1.0 / (low_r * low_r + low_i * low_i)
        return y_all, ms, times(ms[1], ms[2]), (low_r * size, -low_i * size)

    def high_low(x):
        high_part = x.astype(bf16)
        low_part = (x - high_part.astype(f32)).astype(bf16)
        return jnp.concatenate([high_part, low_part], axis=0)

    each_channel(cauchy_one, 4)
    pad_rows = (z.blocks - 1) * z.gr * z.ch
    data_rows = z.blocks * z.gr * z.ch
    xs[0:pad_rows, :] = jnp.zeros((pad_rows, LANES), f32)
    xs[pad_rows + data_rows : z.stack, :] = jnp.zeros(
        (z.stack - pad_rows - data_rows, LANES), f32
    )
    gs[data_rows : z.stack, :] = jnp.zeros((z.stack - data_rows, LANES), f32)
    masks[z.blocks * z.gr :, :] = jnp.zeros((masks.shape[0] - z.blocks * z.gr, LANES), f32)
    for m in range(z.micros):
        first_len, second_len = lengths[m, 0], lengths[m, 1]
        for i in range(z.blocks):
            at = i * z.gr + m * z.segments
            where = spot + i * LANES
            masks[at : at + 1, :] = jnp.where(where < first_len, 1.0, 0.0)
            inside = jnp.where(where < first_len + second_len, 1.0, 0.0)
            masks[at + 1 : at + 2, :] = jnp.where(where >= first_len, inside, 0.0)

    pl.semaphore_wait(
        barrier,
        z.members - 1 + z.members * (jnp.minimum(pipe, 1) + jnp.minimum(last - pipe, 1)),
    )

    @pl.when(pipe == 0)
    def _():
        to_peers(lambda c: tok_tx.at[c], tok_rx, TOK)

    to_peers(lambda c: vec_tx, vec_all, VEC)
    weights_ring(GLU)

    @pl.when(pipe > 0)
    def _():
        to_section_peers(lambda c: vec_tx, vec_next, VECN, pipe - 1)

    @pl.when(pipe == last)
    def _():
        to_peers(lambda c: cot_tx.at[c], cot_rx, COT)

    weights_ring(UP)
    weights_ring(DOWN)

    y_all, ms, cross, over = moments()
    fix = times(cross, over)
    spec = jnp.concatenate([ms[0][0] - cosine * fix[0], ms[0][1] - cosine * fix[1]], axis=1)
    wait_bytes(table, recv.at[TABLE])
    both = dot(high_low(spec), table[...])
    wide = (z.blocks + 1) * LANES
    kern_s[:, 0 : z.length] = both[0:ch] + both[ch : 2 * ch]
    kern_s[:, z.length : wide] = jnp.zeros((ch, wide - z.length), f32)

    def norm_stats(v):
        mean = jnp.sum(v, axis=1, keepdims=True) * (1.0 / width)
        spread = jnp.sum(v * v, axis=1, keepdims=True) * (1.0 / width) - mean * mean
        inv = lax.rsqrt(spread + norm_eps)
        return (v - mean) * inv, inv

    def norm_back(e, hat, inv, gain):
        dh = e * gain
        first = jnp.sum(dh, axis=1, keepdims=True) * (1.0 / width)
        second = jnp.sum(dh * hat, axis=1, keepdims=True) * (1.0 / width)
        return inv * (dh - first - hat * second)

    def turn_out(v, ref):
        tall = jnp.concatenate([v, jnp.zeros((LANES - rows, width), f32)], axis=0)
        ref[...] = tall.T.astype(bf16).reshape(ref.shape)

    def turn_in(ref):
        return ref[...].reshape(width, LANES).astype(f32).T[:rows]

    def full_row(source, r):
        tiles = [
            jnp.where(first_half, source[2 * j, r : r + 1, :], source[2 * j + 1, r : r + 1, :])
            for j in range(z.peers // 2)
        ]
        return jnp.concatenate(tiles, axis=1)

    wait_bytes(vec_all, recv.at[VEC])

    @pl.when(pipe == 0)
    def _():
        wait_bytes(tok_rx, recv.at[TOK])
        x = turn_in(tok_rx)
        res[...] = x.astype(bf16)
        hat1, inv1 = norm_stats(x)
        hat1_s[...] = hat1
        inv1_s[...] = jnp.broadcast_to(inv1, (rows, LANES))
        turn_out(hat1 * full_row(vec_all, 0) + full_row(vec_all, 1), tx1)
        to_members(lambda p: tx1.at[p], rx1, slot_me, A1)

    weights_across(GLU)

    def toeplitz_one(h):
        full = jnp.broadcast_to(kern_s[pl.ds(h, 1), :], (LANES, wide))
        full = pltpu.roll(full, 0, 1, stride=1, stride_axis=0).astype(bf16)
        far[h] = full[:, : z.length]
        for d in range(z.blocks):
            near[h, d * LANES : (d + 1) * LANES, :] = full[:, d * LANES : (d + 1) * LANES]

    each_channel(toeplitz_one, 2)
    weights_across(UP)
    weights_beside(GLU)
    weights_across(DOWN)
    weights_core(GLU)
    weights_beside(UP)

    def lane_tiles(ref, m):
        tiles = []
        for i in range(z.blocks):
            lo, hi = i * LANES, (i + 1) * LANES
            tile = None
            for k in range(lo // tok, -(-hi // tok)):
                piece = shifted(ref[m * z.slots + k].astype(f32), k * tok - lo)
                first = max(0, k * tok - lo)
                if tile is None:
                    tile = piece
                else:
                    tile = jnp.where(spot >= first, piece, tile)
            tiles.append(tile)
        return tiles

    def lane_pieces(tiles, m, ref):
        for k in range(z.slots):
            i, off = divmod(k * tok, LANES)
            piece = shifted(tiles[i], LANES - off)
            if off + tok > LANES:
                piece = jnp.where(spot < LANES - off, piece, shifted(tiles[i + 1], LANES - off))
            ref[m * z.slots + k] = piece.astype(bf16)

    def row_at(i, g):
        return (i * z.gr + g) * z.ch

    def masked_store(ref, base, m, i, tile):
        for q in range(z.segments):
            g = m * z.segments + q
            at = base + row_at(i, g)
            ref[at : at + z.ch, :] = tile * masks[i * z.gr + g : i * z.gr + g + 1, :]

    def masked_sum(m, i):
        total = None
        for q in range(z.segments):
            g = m * z.segments + q
            at = row_at(i, g)
            part = ys[at : at + z.ch, :] * masks[i * z.gr + g : i * z.gr + g + 1, :]
            total = part if total is None else total + part
        return total

    conv_rows = -(-(z.blocks * z.gr) // 8) * 8

    wait_bytes(rx1, recv.at[A1])
    for m in range(z.micros):
        for i, tile in enumerate(lane_tiles(rx1, m)):
            masked_store(xs, pad_rows, m, i, tile)

    def conv_one(h):
        parts = [
            xs[pl.ds((z.blocks - 1 - d) * z.gr * z.ch + h, conv_rows, stride=z.ch), :]
            for d in range(z.blocks)
        ]
        windows = jnp.concatenate(parts, axis=1).astype(bf16)
        ys[pl.ds(h, conv_rows, stride=z.ch), :] = dot(windows, near[h])

    each_channel(conv_one, ch)
    for m in range(z.micros):
        tiles = []
        for i in range(z.blocks):
            own = None
            for q in range(z.segments):
                at = pad_rows + row_at(i, m * z.segments + q)
                own = xs[at : at + z.ch, :] if own is None else own + xs[at : at + z.ch, :]
            tile = masked_sum(m, i) + skip[...] * own
            conv_out[m * z.blocks + i] = tile
            tiles.append(gelu(tile))
        lane_pieces(tiles, m, tx2)
    to_members(lambda p: tx2.at[slot_of(p)], rx2, me, A2)
    weights_beside(DOWN)
    weights_core(UP)
    weights_core(DOWN)
    wait_bytes(rx2, recv.at[A2])
    gated_s[...] = turn_in(rx2).astype(bf16)
    weights_here(GLU)
    gated = gated_s[...]
    value = dot_nt(gated, glu_all[0].reshape(width, width)) + full_row(vec_all, 5)
    sig = jax.nn.sigmoid(
        dot_nt(gated, glu_all[1].reshape(width, width)) + full_row(vec_all, 6)
    )
    val_s[...] = value
    sig_s[...] = sig
    pl.when(pipe > 0)(lambda: wait_bytes(res, recv.at[RES]))
    mid = res[...].astype(f32) + value * sig
    hat2, inv2 = norm_stats(mid)
    hat2_s[...] = hat2
    inv2_s[...] = jnp.broadcast_to(inv2, (rows, LANES))
    ffn_s[...] = (hat2 * full_row(vec_all, 2) + full_row(vec_all, 3)).astype(bf16)
    weights_here(UP)
    weights_here(DOWN)
    ffn_in = ffn_s[...]
    total = mid + full_row(vec_all, 4)
    for c in range(z.peers):
        offset = jnp.concatenate([vec_all[c, 7 + r : 8 + r, :] for r in range(per)], axis=1)
        hidden = dot(ffn_in, up_all[c]) + offset
        hidden_s[c] = hidden
        active = gelu(hidden).astype(bf16)
        act_s[c] = active
        total = total + dot(active, down_all[c])
    layer_out = jnp.where(row_ok, total, 0.0).astype(bf16)
    lay_s[...] = layer_out

    @pl.when(pipe < last)
    def _():
        wait_bytes(vec_next, recv.at[VECN])
        hat, inv = norm_stats(lay_s[...].astype(f32))
        hatn_s[...] = hat
        invn_s[...] = jnp.broadcast_to(inv, (rows, LANES))
        turn_out(hat * full_row(vec_next, 0) + full_row(vec_next, 1), tx1n)
        to_section(lambda p: tx1n.at[p], rx1, slot_me, A1, pipe + 1)
        remote(lay_s, res, RES, place(chan, data, pipe + 1)).start()

    def forward_rows():
        to_peers(lambda c: gated_s, ga, GA)
        to_peers(lambda c: ffn_s, fi, FI)
        to_peers(lambda c: act_s.at[c], ac, AC)

    def backward_rows():
        to_peers(lambda c: gtop, bg, BG)
        to_peers(lambda c: gh_s.at[c], gh, GH)
        to_peers(lambda c: gp_s.at[c], gp, GP)

    turn_out(lay_s[...].astype(f32), lay_t)

    @pl.when(pipe < last)
    def _():
        to_peers(lambda c: lay_t.at[c], hid_rx, HID)
        forward_rows()

    @pl.when(pipe == last)
    def _():
        wait_bytes(cot_rx, recv.at[COT])
        gtop[...] = jnp.where(row_ok, turn_in(cot_rx), 0.0).astype(bf16)

    @pl.when(pipe < last)
    def _():
        wait_bytes(mid_rx, recv.at[MID])
        wait_bytes(rx4n, recv.at[A4N])
        grad_in = jnp.where(row_ok, turn_in(rx4n), 0.0)
        hat = hatn_s[...]
        grad_res = mid_rx[...] + norm_back(
            grad_in, hat, invn_s[:, 0:1], full_row(vec_next, 0)
        )
        gtop[...] = grad_res.astype(bf16)
        pair = (
            jnp.sum(grad_in * hat, axis=0, keepdims=True),
            jnp.sum(grad_in, axis=0, keepdims=True),
        )
        for c in range(z.peers):
            for r, row in enumerate(pair):
                vgn_s[c, r : r + 1, :] = row[:, (c // 2) * LANES : (c // 2 + 1) * LANES]

    grad_low = gtop[...]
    grad_top = grad_low.astype(f32)
    grad_ffn = None
    for c in range(z.peers):
        grad_active = dot_nt(grad_low, down_all[c])
        grad_hidden = (grad_active * gelu_slope(hidden_s[c])).astype(bf16)
        gh_s[c] = grad_hidden
        part = dot_nt(grad_hidden, up_all[c])
        grad_ffn = part if grad_ffn is None else grad_ffn + part
    hat2 = hat2_s[...]
    grad_mid = grad_top + norm_back(grad_ffn, hat2, inv2_s[:, 0:1], full_row(vec_all, 2))
    mid_s[...] = grad_mid
    sig = sig_s[...]
    grad_value = grad_mid * sig
    grad_gate = grad_value * val_s[...] * (1.0 - sig)
    grad_gated = dot(grad_value.astype(bf16), glu_all[0].reshape(width, width)) + dot(
        grad_gate.astype(bf16), glu_all[1].reshape(width, width)
    )
    turn_out(grad_gated, tx3)
    to_members(lambda p: tx3.at[p], rx3, slot_me, A3)
    for j in range(z.peers // 2):
        gv = grad_value[:, j * LANES : (j + 1) * LANES]
        gg = shifted(grad_gate[:, j * LANES : (j + 1) * LANES], LANES // 2)
        gp_s[2 * j] = jnp.where(first_half, gv, gg).astype(bf16)
        gp_s[2 * j + 1] = jnp.where(first_half, gg, gv).astype(bf16)
    pl.when(pipe > 0)(lambda: remote(mid_s, mid_rx, MID, place(chan, data, pipe - 1)).start())
    pl.when(pipe == 0)(backward_rows)

    @pl.when(pipe < last)
    def _():
        turn_out(gtop[...].astype(f32), ign_t)
        to_section_peers(lambda c: ign_t.at[c], ig_rx, IG, pipe + 1)
        to_section(lambda p: vgn_s.at[p // z.groups], vnrx, me, VGN, pipe + 1)

    wait_bytes(rx3, recv.at[A3])
    for m in range(z.micros):
        for i, tile in enumerate(lane_tiles(rx3, m)):
            masked_store(gs, 0, m, i, tile * gelu_slope(conv_out[m * z.blocks + i]))

    def back_one(h):
        parts = [
            gs[pl.ds(d * z.gr * z.ch + h, conv_rows, stride=z.ch), :] for d in range(z.blocks)
        ]
        windows = jnp.concatenate(parts, axis=1).astype(bf16)
        ys[pl.ds(h, conv_rows, stride=z.ch), :] = dot_nt(windows, far[h])

    each_channel(back_one, ch)
    for m in range(z.micros):
        tiles = []
        for i in range(z.blocks):
            own = None
            for q in range(z.segments):
                at = row_at(i, m * z.segments + q)
                own = gs[at : at + z.ch, :] if own is None else own + gs[at : at + z.ch, :]
            tiles.append(masked_sum(m, i) + skip[...] * own)
        lane_pieces(tiles, m, tx4)

    @pl.when(pipe == 0)
    def _():
        to_members(lambda p: tx4.at[slot_of(p)], rx4, me, A4)

    @pl.when(pipe > 0)
    def _():
        to_section(lambda p: tx4.at[slot_of(p)], rx4n, me, A4N, pipe - 1)
        backward_rows()

    @pl.when(pipe == last)
    def _():
        to_peers(lambda c: lay_t.at[c], hid_rx, HID)
        forward_rows()

    def lag_one(h):
        x = xs[pl.ds(pad_rows + h, conv_rows, stride=z.ch), :]
        parts = [
            gs[pl.ds(d * z.gr * z.ch + h, conv_rows, stride=z.ch), :] for d in range(z.blocks)
        ]
        prod = dot_tn(x.astype(bf16), jnp.concatenate(parts, axis=1).astype(bf16))
        prod = jnp.concatenate([prod, jnp.zeros((LANES, LANES), f32)], axis=1)
        size = LANES // 2
        while size >= 8:
            prod = prod[:size] + shifted(prod[size:], wide - size)
            size //= 2
        row = prod[0:1]
        for a in range(1, 8):
            row = row + shifted(prod[a : a + 1], wide - a)
        lag_s[pl.ds(h, 1), :] = row

    each_channel(lag_one, 4)

    @pl.when(pipe == 0)
    def _():
        wait_bytes(rx4, recv.at[A4])
        grad_in = jnp.where(row_ok, turn_in(rx4), 0.0)
        hat = hat1_s[...]
        grad_res = mid_s[...] + norm_back(grad_in, hat, inv1_s[:, 0:1], full_row(vec_all, 0))
        turn_out(grad_res, ig_t)
        to_peers(lambda c: ig_t.at[c], ig_rx, IG)
        pair = (
            jnp.sum(grad_in * hat, axis=0, keepdims=True),
            jnp.sum(grad_in, axis=0, keepdims=True),
        )
        for c in range(z.peers):
            for r, row in enumerate(pair):
                vg0_s[c, r : r + 1, :] = row[:, (c // 2) * LANES : (c // 2 + 1) * LANES]
        to_members(lambda p: vg0_s.at[p // z.groups], vnrx, me, VGN)

    rows_of = [
        jnp.sum(grad_ffn * hat2, axis=0, keepdims=True),
        jnp.sum(grad_ffn, axis=0, keepdims=True),
        jnp.sum(grad_top, axis=0, keepdims=True),
    ]
    for c in range(z.peers):
        j = c // 2
        for r, row in enumerate(rows_of):
            vg_s[c, r : r + 1, :] = row[:, j * LANES : (j + 1) * LANES]
        vg_s[c, 3:4, :] = jnp.sum(gp_s[c].astype(f32), axis=0, keepdims=True)
        up_row = jnp.sum(gh_s[c].astype(f32), axis=0, keepdims=True)
        for r in range(per):
            vg_s[c, 4 + r : 5 + r, :] = up_row[:, r * LANES : (r + 1) * LANES]
    to_members(lambda p: vg_s.at[p // z.groups], vrx, me, VG)
    many = z.peers * rows
    grads = (
        (ac, AC, bg, BG, z.hid, width, pdown, kdown, sdown, ldown, ddown),
        (fi, FI, gh, GH, width, z.hid, pup, kup, sup, lup, dup),
        (gp, GP, ga, GA, 2 * z.cw, width, pglu, kglu, sglu, lglu, dglu),
    )
    for t, (left, lp, right, rp, n_left, n_right, part, krx, *_) in enumerate(grads):
        wait_bytes(left, recv.at[lp])
        wait_bytes(right, recv.at[rp])
        part[...] = dot_tn(left[...].reshape(many, n_left), right[...].reshape(many, n_right))
        half = n_left // 2
        other = pl.ds(pl.multiple_of((1 - core) * half, half), half)
        remote(part.at[other], krx, GRADS + 3 * t, sibling).start()
    for t, (_, _, _, _, n_left, _, part, krx, lsend, lrx, _) in enumerate(grads):
        half = n_left // 2
        own = pl.ds(pl.multiple_of(core * half, half), half)
        wait_bytes(krx, recv.at[GRADS + 3 * t])
        lsend[...] = (part[own, :] + krx[...]).astype(bf16)
        remote(lsend, lrx, GRADS + 3 * t + 1, across).start()

    both = dot_nt(high_low(lag_s[:, 0 : z.length]), table[...])
    grad_spec = both[0:ch] + both[ch : 2 * ch]
    gk = (grad_spec[:, 0:padded], grad_spec[:, padded : 2 * padded])
    y_all, ms, cross, over = moments()
    g_top = times(conj(over), gk)
    g_top = (-cosine * g_top[0], -cosine * g_top[1])
    g_low = times(conj(times(times(cross, over), over)), gk)
    g_three = (cosine * cosine * g_low[0], cosine * cosine * g_low[1])
    g_ms = [gk, times(conj(ms[2]), g_top), times(conj(ms[1]), g_top), g_three]
    g_rise = None
    for v, (g_r, g_i) in enumerate(g_ms):
        gsum_s[v] = 2.0 * cosine * g_r
        gsum_s[4 + v] = -2.0 * cosine * g_i
        gsum_s[8 + v] = 2.0 * y_all * g_i
        gsum_s[12 + v] = 2.0 * y_all * g_r
        part = 2.0 * (sums_s[12 + v] * g_r + sums_s[8 + v] * g_i)
        g_rise = part if g_rise is None else g_rise + part
    slope_s[...] = g_rise
    gcol_s[...] = jnp.zeros(gcol_s.shape, f32)
    gstep_s[...] = jnp.zeros(gstep_s.shape, f32)

    def mode_one(h):
        double, y, cy, u, w = modes_at(h)
        column = column_of(0, h)
        gu, gw = 0.0, 0.0
        acc = gcol_s[0]
        for v in range(4):
            a = column[:, v * ch : v * ch + 1]
            b = column[:, (4 + v) * ch : (4 + v) * ch + 1]
            au, aw = gsum_s[v, pl.ds(h, 1), :], gsum_s[4 + v, pl.ds(h, 1), :]
            bu, bw = gsum_s[8 + v, pl.ds(h, 1), :], gsum_s[12 + v, pl.ds(h, 1), :]
            gu = gu + a * au + b * bu
            gw = gw + a * aw + b * bw
            ga_col = jnp.sum(u * au + w * aw, axis=1, keepdims=True)
            gb_col = jnp.sum(u * bu + w * bw, axis=1, keepdims=True)
            acc = jnp.where(spot == v * ch + h, ga_col, acc)
            acc = jnp.where(spot == (4 + v) * ch + h, gb_col, acc)
        gcol_s[0] = acc
        even, cross_uw = u * u - w * w, 2.0 * u * w
        g_den_r = -(even * gu + cross_uw * gw)
        g_den_i = even * gw - cross_uw * gu
        ge = jnp.sum(cosine * cosine * g_den_r, axis=1, keepdims=True)
        gf = jnp.sum(cy * g_den_i, axis=1, keepdims=True)
        acc = jnp.where(spot == h, ge, gcol_s[1])
        gcol_s[1] = jnp.where(spot == ch + h, gf, acc)
        gy = slope_s[pl.ds(h, 1), :] + jnp.sum(
            double * cosine * g_den_i - 2.0 * y * g_den_r, axis=0, keepdims=True
        )
        total_y = jnp.sum(y * gy, axis=1, keepdims=True)
        gstep_s[0:1, :] = jnp.where(spot == h, -total_y, gstep_s[0:1, :])

    each_channel(mode_one, 2)

    def unpacked(k, i):
        return shifted(gcol_s[k], LANES - i * ch)

    g_square, g_double = unpacked(1, 0), unpacked(1, 1)
    g_decay = 2.0 * decay * g_square + 2.0 * g_double
    g_rate = 2.0 * rate * g_square
    g_pairs = []
    for v, (v_r, v_i) in enumerate(pairs):
        g_alpha, g_beta = unpacked(0, v), unpacked(0, 4 + v)
        g_decay = g_decay + g_alpha * v_r
        if v_i is not None:
            g_rate = g_rate - g_alpha * v_i
        g_pairs.append((decay * g_alpha + g_beta, -rate * g_alpha))
    c_b, c_p, p_b = g_pairs[0], g_pairs[1], g_pairs[2]
    p_p = g_pairs[3][0]
    rank, into, out = (rank_r, rank_i), (in_r, in_i), (out_r, out_i)

    def plus(*terms):
        return sum(t[0] for t in terms), sum(t[1] for t in terms)

    g_out = plus(times(conj(into), c_b), times(conj(rank), c_p))
    g_in = plus(times(conj(out), c_b), times(rank, p_b))
    g_rank = plus(
        times(conj(out), c_p),
        times(into, conj(p_b)),
        (2.0 * rank_r * p_p, 2.0 * rank_i * p_p),
    )
    modes_tx[0:nh, :] = packed([g_decay, g_rate, *g_rank, *g_in, *g_out])
    modes_tx[nh : nh + 8, :] = gstep_s[...]
    skip_row = jnp.sum(jnp.where(diagonal, lag_s[:, 0:1], 0.0), axis=0, keepdims=True)
    modes_tx[nh + 1 : nh + 2, :] = skip_row
    for k in range(1, z.groups):
        remote(modes_tx, modes_rx.at[data], MODES, place(chan, lax.rem(data + k, z.groups))).start()
    pltpu.make_async_copy(modes_tx, modes_rx.at[data], recv.at[MODES]).start()

    for t, (_, _, _, _, n_left, _, _, _, lsend, lrx, final) in enumerate(grads):
        half = n_left // 2
        own = pl.ds(pl.multiple_of(core * half, half), half)
        wait_bytes(lrx, recv.at[GRADS + 3 * t + 1])
        final[own, :] = lsend[...].astype(f32) + lrx[...].astype(f32)
        remote(final.at[own], final.at[own], GRADS + 3 * t + 2, sibling).start()

    def collect(source, target):
        count = tok * z.quarters
        for m in range(z.micros):
            tiles = []
            for i in range(-(-count // LANES)):
                lo, hi = i * LANES, min((i + 1) * LANES, count)
                tile = None
                for q in range(lo // tok, -(-hi // tok)):
                    piece = shifted(source[m * z.quarters + q].astype(f32), q * tok - lo)
                    first = max(0, q * tok - lo)
                    tile = piece if tile is None else jnp.where(spot >= first, piece, tile)
                tiles.append(tile)
            target[m] = jnp.concatenate(tiles, axis=1)[:, 0:count].astype(bf16)

    wait_bytes(hid_rx, recv.at[HID])
    collect(hid_rx, hid_out)
    wait_bytes(ig_rx, recv.at[IG])
    collect(ig_rx, ig_out)
    wait_bytes(vrx, recv.at[VG])
    wait_bytes(vnrx, recv.at[VGN])
    summed, summed_one = vrx[0], vnrx[0]
    for p in range(1, z.members):
        summed = summed + vrx[p]
        summed_one = summed_one + vnrx[p]
    upb_out[...] = jnp.concatenate([summed[4 + r : 5 + r, :] for r in range(per)], axis=1)
    summed, summed_one = own_half(summed), own_half(summed_one)
    for r in range(3):
        ffn_out[r] = summed[r : r + 1, 0 : z.cw]
    glub_out[0:1, :] = summed[3:4, 0 : z.cw]
    glub_out[1:2, :] = shifted(summed[3:4], LANES // 2)[:, 0 : z.cw]
    vec_out[0:2, :] = summed_one[0:2, 0 : z.cw]
    wait_bytes(modes_rx, recv.at[MODES])

    def over_groups(take):
        total = take(0)
        for d in range(1, z.groups):
            total = jnp.where(spot // ch == d, take(d), total)
        return total[:, 0 : z.cw]

    for p in range(8):
        modes_out[p] = over_groups(
            lambda d: shifted(modes_rx[d, 0:nh, :], (d - p) * ch)
        )
    for r in range(2):
        vec_out[2 + r : 3 + r, :] = over_groups(
            lambda d: shifted(modes_rx[d, nh + r : nh + r + 1, :], d * ch)
        )
    for t, (_, _, _, _, n_left, _, _, _, _, _, final) in enumerate(grads):
        half = n_left // 2
        other = pl.ds(pl.multiple_of((1 - core) * half, half), half)
        wait_bytes(final.at[other], recv.at[GRADS + 3 * t + 2])
    glu_out[0] = dglu[pl.ds(pl.multiple_of(odd * z.cw, z.cw), z.cw), :]
    glu_out[1] = dglu[pl.ds(pl.multiple_of((1 - odd) * z.cw, z.cw), z.cw), :]

    for t in (GLU, UP, DOWN):
        weights_sent(t)
    for ref, phase in (
        (vec_all, VEC), (hid_rx, HID), (ga, GA), (fi, FI), (ac, AC), (bg, BG), (gh, GH), (gp, GP),
    ):
        wait_bytes(ref.at[pl.ds(0, z.peers - 1)], send.at[phase])
    for ref, phase in ((rx2, A2), (rx3, A3), (vrx, VG)):
        wait_bytes(ref.at[pl.ds(0, z.members - 1)], send.at[phase])
    wait_bytes(modes_rx.at[pl.ds(0, z.groups - 1)], send.at[MODES])
    for t, (_, _, _, _, n_left, _, _, krx, lsend, _, final) in enumerate(grads):
        wait_bytes(krx, send.at[GRADS + 3 * t])
        wait_bytes(lsend, send.at[GRADS + 3 * t + 1])
        wait_bytes(final.at[pl.ds(0, n_left // 2)], send.at[GRADS + 3 * t + 2])

    @pl.when(pipe == 0)
    def _():
        wait_bytes(tok_rx.at[pl.ds(0, z.peers - 1)], send.at[TOK])
        wait_bytes(ig_rx.at[pl.ds(0, z.peers - 1)], send.at[IG])
        for ref, phase in ((rx1, A1), (rx4, A4), (vnrx, VGN)):
            wait_bytes(ref.at[pl.ds(0, z.members - 1)], send.at[phase])

    @pl.when(pipe == last)
    def _():
        wait_bytes(cot_rx.at[pl.ds(0, z.peers - 1)], send.at[COT])

    @pl.when(pipe < last)
    def _():
        for ref, phase in ((rx1, A1), (lay_s, RES), (ig_rx, IG), (vnrx, VGN)):
            wait_bytes(ref, send.at[phase])

    @pl.when(pipe > 0)
    def _():
        for ref, phase in ((vec_all, VECN), (mid_s, MID), (rx4, A4N)):
            wait_bytes(ref, send.at[phase])


def finish_kernel(*refs):
    count = (len(refs) - 1) // 3
    sems = refs[-1]
    sources, targets, held = refs[:count], refs[count : 2 * count], refs[2 * count : -1]
    loads = [pltpu.make_async_copy(sources[i], held[i], sems.at[i]) for i in range(count)]
    stores = [
        pltpu.make_async_copy(held[i], targets[i], sems.at[count + i]) for i in range(count)
    ]
    for load in loads:
        load.start()
    for load, store in zip(loads, stores):
        load.wait()
        store.start()
    for store in stores:
        store.wait()


def body(
    tokens,
    seq_lengths,
    out_cot,
    s4_vectors,
    s4_modes,
    glu_weight,
    glu_bias,
    ffn_vectors,
    up_weight,
    up_bias,
    down_weight,
):
    micros, tok_rows, chan_width = tokens.shape
    width = glu_weight.shape[1]
    hidden = up_weight.shape[2]
    z = Sizes(
        lax.axis_size("pipe"), lax.axis_size("chan"), lax.axis_size("dp"),
        tok_rows, chan_width, width, hidden,
    )
    length = z.length
    padded = -(-(length // 2 + 1) // LANES) * LANES
    nh = s4_modes.shape[3]
    table = jnp.asarray(fourier_table(length, padded).astype(ml_dtypes.bfloat16))
    angles = jnp.asarray(half_angles(length, padded))

    vmem = pl.BlockSpec(memory_space=pltpu.VMEM)
    smem = pl.BlockSpec(memory_space=pltpu.SMEM)
    anywhere = pl.BlockSpec(memory_space=pl.ANY)
    n, r, w, ch = z.peers, z.rows, width, z.ch

    def s(shape, kind=f32):
        return jax.ShapeDtypeStruct(shape, kind)

    def v(shape, kind=bf16):
        return pltpu.VMEM(shape, kind)

    conv_rows = -(-(z.blocks * z.gr) // 8) * 8
    wide = (z.blocks + 1) * LANES
    rows_full, rows_wide, side = v((r, w)), v((r, w), f32), v((r, LANES), f32)
    peer_tiles, exchange = v((n, chan_width, LANES)), v((z.members, z.ch, LANES))
    small = v((n, 8, LANES), f32)
    results = (
        s((micros, chan_width, tok_rows), bf16), s((micros, chan_width, tok_rows), bf16),
        s((4, chan_width)), s((8, nh, chan_width)), s((2, chan_width, w)),
        s((2, chan_width)), s((3, 1, chan_width)), s((w, hidden)), s((1, hidden)),
        s((hidden, w)),
    )
    raw = pl.pallas_call(
        lambda *refs: main_kernel(z, *refs),
        out_shape=results,
        in_specs=[smem] + [vmem] * 11 + [anywhere],
        out_specs=[vmem] * 10,
        scratch_shapes=[
            peer_tiles, peer_tiles, v((16, LANES), f32), v((ch, length, LANES)),
            v((ch, LANES, length)), v((ch, LANES), f32), v((conv_rows, LANES), f32),
            peer_tiles, peer_tiles, v((z.stack, LANES), f32), v((z.stack, LANES), f32),
            v((2 * padded, length)), v((2, nh, LANES), f32),
            v((ch, LANES), f32), v((16, ch, padded), f32), v((16, ch, padded), f32),
            v((ch, padded), f32), v((ch, wide), f32), v((ch, wide), f32),
            v((2, nh, LANES), f32), v((8, LANES), f32),
            v((nh + 8, LANES), f32), v((z.groups, nh + 8, LANES), f32),
            v((2 * chan_width, w), f32), v((w, hidden), f32), v((hidden, w), f32),
            v((chan_width, w), f32), v((w // 2, hidden), f32), v((hidden // 2, w), f32),
            v((chan_width, w)), v((w // 2, hidden)), v((hidden // 2, w)),
            v((chan_width, w)), v((w // 2, hidden)), v((hidden // 2, w)),
            v((2 * chan_width, w), f32),
            v((n, 16, LANES), f32), v((n, 16, LANES), f32),
            v((2, n, chan_width, w)), v((n, w, hidden)),
            v((n, hidden, w)), peer_tiles, peer_tiles, rows_full, rows_full,
        ]
        + [exchange] * 10
        + [
            v((z.micros * z.blocks, z.ch, LANES), f32), v((conv_rows * z.ch, LANES), f32),
            rows_wide, side, rows_wide, side, rows_wide, side,
            rows_wide, rows_wide, v((n, r, hidden), f32),
            rows_full, rows_full, v((n, r, hidden)), v((n, r, hidden)), v((n, r, LANES)),
            rows_full, peer_tiles, peer_tiles, peer_tiles, rows_wide, rows_wide,
            small, small, small,
            v((n, r, w)), v((n, r, w)), v((n, r, hidden)), v((n, r, w)), v((n, r, hidden)),
            v((n, r, LANES)), v((z.members, 8, LANES), f32), v((z.members, 8, LANES), f32),
            pltpu.SemaphoreType.DMA((50,)), pltpu.SemaphoreType.DMA((50,)),
        ],
        compiler_params=pltpu.CompilerParams(
            collective_id=0, has_side_effects=True, vmem_limit_bytes=60 * 2**20
        ),
        name="layers",
    )(
        seq_lengths, tokens.transpose(0, 2, 1), out_cot.transpose(0, 2, 1), s4_vectors[0],
        s4_modes[0].transpose(0, 2, 1), glu_weight[0].transpose(1, 2, 0), glu_bias[0],
        ffn_vectors.transpose(1, 0, 2), up_weight[0], up_bias, down_weight[0], angles, table,
    )
    hid, ig, vec, modes, dglu, glub, ffn, dup, upb, ddown = pl.pallas_call(
        finish_kernel,
        out_shape=results,
        in_specs=[anywhere] * 10,
        out_specs=[anywhere] * 10,
        scratch_shapes=[pltpu.VMEM(x.shape, x.dtype) for x in results]
        + [pltpu.SemaphoreType.DMA((20,))],
        compiler_params=pltpu.CompilerParams(vmem_limit_bytes=60 * 2**20),
        name="finish",
    )(*raw)
    return (
        hid.transpose(0, 2, 1)[None], ig.transpose(0, 2, 1)[None], vec[None],
        modes.transpose(0, 2, 1)[None], dglu.transpose(2, 0, 1)[None], glub[None],
        ffn.transpose(1, 0, 2), dup[None], upb, ddown[None],
    )


def solution(mesh):
    placed = (
        P(None, "dp", "chan"),
        P(),
        P(None, "dp", "chan"),
        P("pipe", None, "chan"),
        P("pipe", None, "chan", None),
        P("pipe", None, None, "chan"),
        P("pipe", None, "chan"),
        P("pipe", None, "chan"),
        P("pipe", None, "chan"),
        P("pipe", "chan"),
        P("pipe", "chan", None),
    )
    return jax.shard_map(
        body,
        mesh=mesh,
        in_specs=placed,
        out_specs=(
            P("pipe", None, "dp", "chan"),
            P("pipe", None, "dp", "chan"),
            P("pipe", None, "chan"),
            P("pipe", None, "chan", None),
            P("pipe", None, None, "chan"),
            P("pipe", None, "chan"),
            P("pipe", None, "chan"),
            P("pipe", None, "chan"),
            P("pipe", "chan"),
            P("pipe", "chan", None),
        ),
        check_vma=False,
    )
```

time: 246 us -> 208 us (0.85); the launches traced: 242 us -> 207 us
  local copies, waits for them, and re-layouts: 18.1 us -> 0 us
  Pallas kernels: 221 us -> 207 us
    unnamed x26 -> x0, local copies, waits for them, and re-layouts: 17.2 us -> none
    pallas_call x1 -> x2, Pallas kernels: 221 us -> 207 us  [the longest x1 204 us: body(): pl.pallas_call(lambda *refs: main_kernel(z, *refs), out_shape=results, in...]
where the time goes in v3:
time: 208 us; the launch traced here: 207 us
  Pallas kernels  207 us (100%)
    pallas_call x1, Pallas kernels, body(): pl.pallas_call(lambda *refs: main_kernel(z, *refs), out_shape=results, in...  204 us

profile of v3, /device:TPU:1, one launch (start us, length us, event | category | flops | bytes accessed | tf_op | source)
XLA Modules:
  0.0 207.5 jit_solution(802370877819479641)
XLA Ops:
  0.6 204.2 %layers.1 = (bf16[2,64,288]{2,1,0:T(8,128)(2,1)}, bf16[2,64,288]{2,1,0:T(8,128)(2,1)}, f32[4,64]{1,0:T(4,128)}, f32[8,32,64]{2,1,0:T(8,128)}, f32[2,64,512]{2,1,...) custom-call(s32[2,2]{1,0:T(2,128)} %refs_0_.1, ...), custom_call_target="tpu_custom_call" | custom-call | tf_op jit(solution)/shard_map/layers/pallas_call | solution.py:1042
  204.9 2.5 %finish.1 = (bf16[2,64,288]{2,1,0:T(8,128)(2,1)}, bf16[2,64,288]{2,1,0:T(8,128)(2,1)}, f32[4,64]{1,0:T(4,128)}, f32[8,32,64]{2,1,0:T(8,128)}, f32[2,64,512]{2,1,...) custom-call(bf16[2,64,288]{2,1,0:T(8,128)(2,1)} %get-tuple-element.3, ...), custom_call_target="tpu_custom_call" | custom-call | tf_op jit(solution)/shard_map/finish/pallas_call | solution.py:1086

commit v4 on v3

--- a/solution.py
+++ b/solution.py
@@ -79,8 +79,9 @@
         self.members = peers * groups
         self.ch = model_width // self.members
         self.slots = self.quarters * groups
-        self.gr = self.micros * self.segments
-        self.stack = (2 * self.blocks) * self.gr * self.ch
+        self.conv_rows = -(-(self.blocks * self.segments) // 8) * 8
+        spare = -(-(self.conv_rows - self.blocks * self.segments) // self.segments)
+        self.stack = (2 * self.blocks - 1 + spare) * self.segments * self.ch
 
 
 def main_kernel(z, *refs):
@@ -93,7 +94,7 @@
     ) = refs[13:23]
     (
         tok_tx, cot_tx, vec_tx, near, far, skip, masks, hid_rx, ig_rx, xs, gs,
-        table, cols, rise_s, sums_s, gsum_s, slope_s, kern_s, lag_s, gcol_s, gstep_s,
+        table, cols, rise_s, sums_s, uw_s, guw_s, rest_s, gsum_s, slope_s, kern_s, lag_s, gcol_s, gstep_s,
         modes_tx, modes_rx, pglu, pup, pdown, kglu, kup, kdown, sglu, sup, sdown,
         lglu, lup, ldown, dglu,
         vec_all, vec_next, glu_all, up_all, down_all, tok_rx, cot_rx, res, gtop,
@@ -115,6 +116,10 @@
     odd = lax.rem(chan, 2)
     per = z.hid // LANES
 
+    high, deep = chan // z.quarters, lax.rem(chan, z.quarters)
+    side, core = data // 2, lax.rem(data, 2)
+    height = 2 * high + side
+
     def slot_of(p):
         c, d = p // z.groups, lax.rem(p, z.groups)
         return (c // z.quarters) * z.slots + d * z.quarters + lax.rem(c, z.quarters)
@@ -147,22 +152,67 @@
         lax.fori_loop(1, z.peers, step, 0)
         pltpu.make_async_copy(src_of(chan), dst.at[chan], recv.at[phase]).start()
 
+    def far_first(i):
+        return lax.rem(2 + i + (i // 2) * (2 * i - 3), 4)
+
+    def number(y, depth, core_there):
+        return ((y // 2) * z.quarters + depth) * z.groups + lax.rem(y, 2) * 2 + core_there
+
+    def to_all(src_of, dst, slot, phase, section=None):
+        def chip(k):
+            y = lax.rem(height + far_first(k // 4), 4)
+            return y, lax.rem(deep + far_first(lax.rem(k, 4)), 4)
+
+        def step(k, carry):
+            y, depth = chip(k)
+            for c in range(2):
+                p = number(y, depth, c)
+                remote(src_of(p), dst.at[slot], phase, member(p, section)).start()
+            return carry
+
+        chips = z.members // 2
+        lax.fori_loop(0, chips if section is not None else chips - 1, step, 0)
+        if section is None:
+            p = number(height, deep, 1 - core)
+            remote(src_of(p), dst.at[slot], phase, member(p)).start()
+            pltpu.make_async_copy(src_of(me), dst.at[slot], recv.at[phase]).start()
+
     def to_members(src_of, dst, slot, phase):
+        to_all(src_of, dst, slot, phase)
+
+    def to_section(src_of, dst, slot, phase, section):
+        to_all(src_of, dst, slot, phase, section)
+
+    def to_micro(m, source, dst, phase, section=None):
+        near_by = jnp.where(own_micro == m, 1, 0)
+
+        def send_to(p):
+            remote(source.at[slot_of(p)], dst.at[me], phase, member(p, section)).start()
+
+        def chip(k):
+            y = 2 * m + lax.rem(side + near_by + k // 4, 2)
+            return y, lax.rem(deep + far_first(lax.rem(k, 4)), 4)
+
         def step(k, carry):
-            p = lax.rem(me + k, z.members)
-            remote(src_of(p), dst.at[slot], phase, member(p)).start()
+            y, depth = chip(k)
+            for c in range(2):
+                send_to(number(y, depth, c))
             return carry
 
-        lax.fori_loop(1, z.members, step, 0)
-        pltpu.make_async_copy(src_of(me), dst.at[slot], recv.at[phase]).start()
-
-    def to_section(src_of, dst, slot, phase, section):
-        def step(k, carry):
-            p = lax.rem(me + k, z.members)
-            remote(src_of(p), dst.at[slot], phase, member(p, section)).start()
-            return carry
-
-        lax.fori_loop(0, z.members, step, 0)
+        lax.fori_loop(0, z.slots // 2 - 1, step, 0)
+        if section is not None:
+            step(z.slots // 2 - 1, 0)
+            return
+
+        @pl.when(own_micro == m)
+        def _():
+            send_to(number(height, deep, 1 - core))
+            block = source.at[slot_of(me)]
+            pltpu.make_async_copy(block, dst.at[me], recv.at[phase]).start()
+
+        @pl.when(own_micro != m)
+        def _():
+            step(z.slots // 2 - 1, 0)
 
     def to_section_peers(src_of, dst, phase, section):
         def step(k, carry):
@@ -173,13 +223,12 @@
         lax.fori_loop(0, z.peers, step, 0)
 
     (
-        VEC, VECN, TOK, COT, A1, A2, A3, A4, A4N, RES, MID, HID, IG, GA, FI, AC, BG, GH, GP, VG,
+        VEC, VECN, TOK, COT, A2, A4, A4N, RES, MID, HID, IG, GA, FI, AC, BG, GH, GP, VG,
         VGN, TABLE, MODES,
-    ) = range(23)
-    GLU, UP, DOWN, GRADS = 23, 29, 35, 41
-
-    high, deep = chan // z.quarters, lax.rem(chan, z.quarters)
-    side, core = data // 2, lax.rem(data, 2)
+    ) = range(21)
+    A1, A3, GLU, UP, DOWN, GRADS = 21, 23, 25, 31, 37, 43
+    own_micro = chan // z.quarters
+
     own_side, far_side = high * z.quarters, (1 - high) * z.quarters
     sibling, across = place(chan, side * 2 + 1 - core), place(chan, (1 - side) * 2 + core)
 
@@ -198,41 +247,46 @@
         start = pl.multiple_of(core * half + part * fourth, fourth)
         return whole.at[pl.ds(c, count), pl.ds(start, fourth)]
 
-    def weights_ring(t):
+    def weights_out(t):
         if t == GLU:
-            loc, whole, mine = glu_loc, glu_all.at[:, chan], glu_loc.at[core]
+            loc, whole, half = glu_loc, glu_all.at[:, chan], glu_loc.at[core]
+            fourth = z.cw // 2
+            quarter = half.at[pl.ds(pl.multiple_of(side * fourth, fourth), fourth)]
         else:
             loc, whole = (up_loc, up_all) if t == UP else (down_loc, down_all)
-            half = loc.shape[0] // 2
-            whole, mine = whole.at[chan], loc.at[pl.ds(pl.multiple_of(core * half, half), half)]
+            size = loc.shape[0] // 2
+            fourth = size // 2
+            whole, half = whole.at[chan], loc.at[pl.ds(pl.multiple_of(core * size, size), size)]
+            start = pl.multiple_of(core * size + side * fourth, fourth)
+            quarter = loc.at[pl.ds(start, fourth)]
         pltpu.make_async_copy(loc, whole, recv.at[t + 5]).start()
+        there = piece_of(t, chan, 1, side).at[0]
+        for k in range(z.quarters):
+            c = far_side + lax.rem(deep + k, z.quarters)
+            remote(quarter, there, t + 1, place(c, (1 - side) * 2 + core)).start()
+        there = piece_of(t, chan, 1).at[0]
         for k in range(1, z.quarters):
             c = own_side + lax.rem(deep + k, z.quarters)
-            there = piece_of(t, chan, 1).at[0]
-            remote(mine, there, t, place(c, data)).start()
-
-    def weights_across(t):
-        loc = {GLU: glu_loc, UP: up_loc, DOWN: down_loc}[t]
-        wait_bytes(piece_of(t, 0, z.quarters - 1), recv.at[t])
-        wait_bytes(loc, recv.at[t + 5])
-        piece = piece_of(t, own_side, z.quarters, side)
-        where = place(far_side + deep, (1 - side) * 2 + core)
-        remote(piece, piece, t + 1, where).start()
-        for k in range(1, z.quarters):
-            piece = piece_of(t, own_side + lax.rem(deep + k, z.quarters), 1)
-            remote(piece, piece, t + 3, sibling).start()
+            remote(half, there, t, place(c, data)).start()
 
     def weights_beside(t):
         wait_bytes(piece_of(t, 0, z.quarters, 0), recv.at[t + 1])
         piece = piece_of(t, far_side, z.quarters, 1 - side)
         remote(piece, piece, t + 2, across).start()
 
+    def weights_near(t):
+        wait_bytes(piece_of(t, 0, z.quarters - 1), recv.at[t])
+        for k in range(1, z.quarters):
+            piece = piece_of(t, own_side + lax.rem(deep + k, z.quarters), 1)
+            remote(piece, piece, t + 3, sibling).start()
+
     def weights_core(t):
         wait_bytes(piece_of(t, 0, z.quarters, 0), recv.at[t + 2])
         piece = piece_of(t, far_side, z.quarters)
         remote(piece, piece, t + 4, sibling).start()
 
     def weights_here(t):
+        wait_bytes({GLU: glu_loc, UP: up_loc, DOWN: down_loc}[t], recv.at[t + 5])
         wait_bytes(piece_of(t, 0, z.quarters - 1), recv.at[t + 3])
         wait_bytes(piece_of(t, 0, z.quarters), recv.at[t + 4])
 
@@ -348,6 +402,9 @@
 
     def cauchy_one(h):
         _, _, _, u, w = modes_at(h)
+        at = pl.ds(pl.multiple_of(h * nh, nh), nh)
+        uw_s[at, 0:padded] = u
+        uw_s[at, padded : 2 * padded] = w
         column = column_of(0, h)
         for v in range(4):
             a = column[:, v * ch : v * ch + 1]
@@ -393,18 +450,19 @@
         return jnp.concatenate([high_part, low_part], axis=0)
 
     each_channel(cauchy_one, 4)
-    pad_rows = (z.blocks - 1) * z.gr * z.ch
-    data_rows = z.blocks * z.gr * z.ch
-    xs[0:pad_rows, :] = jnp.zeros((pad_rows, LANES), f32)
-    xs[pad_rows + data_rows : z.stack, :] = jnp.zeros(
-        (z.stack - pad_rows - data_rows, LANES), f32
-    )
-    gs[data_rows : z.stack, :] = jnp.zeros((z.stack - data_rows, LANES), f32)
-    masks[z.blocks * z.gr :, :] = jnp.zeros((masks.shape[0] - z.blocks * z.gr, LANES), f32)
+    pad_rows = (z.blocks - 1) * z.segments * z.ch
+    data_rows = z.blocks * z.segments * z.ch
+    for m in range(z.micros):
+        at = m * z.stack
+        xs[at : at + pad_rows, :] = jnp.zeros((pad_rows, LANES), f32)
+        rest = z.stack - pad_rows - data_rows
+        xs[at + z.stack - rest : at + z.stack, :] = jnp.zeros((rest, LANES), f32)
+        rest = z.stack - data_rows
+        gs[at + data_rows : at + z.stack, :] = jnp.zeros((rest, LANES), f32)
     for m in range(z.micros):
         first_len, second_len = lengths[m, 0], lengths[m, 1]
         for i in range(z.blocks):
-            at = i * z.gr + m * z.segments
+            at = (m * z.blocks + i) * z.segments
             where = spot + i * LANES
             masks[at : at + 1, :] = jnp.where(where < first_len, 1.0, 0.0)
             inside = jnp.where(where < first_len + second_len, 1.0, 0.0)
@@ -420,7 +478,7 @@
         to_peers(lambda c: tok_tx.at[c], tok_rx, TOK)
 
     to_peers(lambda c: vec_tx, vec_all, VEC)
-    weights_ring(GLU)
+    weights_out(GLU)
 
     @pl.when(pipe > 0)
     def _():
@@ -430,8 +488,6 @@
     def _():
         to_peers(lambda c: cot_tx.at[c], cot_rx, COT)
 
-    weights_ring(UP)
-    weights_ring(DOWN)
 
     y_all, ms, cross, over = moments()
     fix = times(cross, over)
@@ -479,9 +535,10 @@
         hat1_s[...] = hat1
         inv1_s[...] = jnp.broadcast_to(inv1, (rows, LANES))
         turn_out(hat1 * full_row(vec_all, 0) + full_row(vec_all, 1), tx1)
-        to_members(lambda p: tx1.at[p], rx1, slot_me, A1)
-
-    weights_across(GLU)
+        to_members(lambda p: tx1.at[p], rx1, slot_me, A1 + own_micro)
+
+    weights_out(UP)
+    pl.when(pipe > 0)(lambda: weights_out(DOWN))
 
     def toeplitz_one(h):
         full = jnp.broadcast_to(kern_s[pl.ds(h, 1), :], (LANES, wide))
@@ -491,11 +548,25 @@
             near[h, d * LANES : (d + 1) * LANES, :] = full[:, d * LANES : (d + 1) * LANES]
 
     each_channel(toeplitz_one, 2)
-    weights_across(UP)
     weights_beside(GLU)
-    weights_across(DOWN)
+    weights_near(GLU)
+
+    def weights_up():
+        weights_beside(UP)
+        weights_near(UP)
+        weights_core(UP)
+
+    def weights_down():
+        weights_beside(DOWN)
+        weights_near(DOWN)
+        weights_core(DOWN)
+
+    @pl.when(pipe > 0)
+    def _():
+        weights_up()
+        weights_down()
+
     weights_core(GLU)
-    weights_beside(UP)
 
     def lane_tiles(ref, m):
         tiles = []
@@ -520,55 +591,63 @@
                 piece = jnp.where(spot < LANES - off, piece, shifted(tiles[i + 1], LANES - off))
             ref[m * z.slots + k] = piece.astype(bf16)
 
-    def row_at(i, g):
-        return (i * z.gr + g) * z.ch
+    def row_at(m, i, q):
+        return m * z.stack + (i * z.segments + q) * z.ch
+
+    def mask_of(m, i, q):
+        at = (m * z.blocks + i) * z.segments + q
+        return masks[at : at + 1, :]
 
     def masked_store(ref, base, m, i, tile):
         for q in range(z.segments):
-            g = m * z.segments + q
-            at = base + row_at(i, g)
-            ref[at : at + z.ch, :] = tile * masks[i * z.gr + g : i * z.gr + g + 1, :]
+            at = base + row_at(m, i, q)
+            ref[at : at + z.ch, :] = tile * mask_of(m, i, q)
 
     def masked_sum(m, i):
         total = None
         for q in range(z.segments):
-            g = m * z.segments + q
-            at = row_at(i, g)
-            part = ys[at : at + z.ch, :] * masks[i * z.gr + g : i * z.gr + g + 1, :]
+            at = row_at(0, i, q)
+            part = ys[at : at + z.ch, :] * mask_of(m, i, q)
             total = part if total is None else total + part
         return total
 
-    conv_rows = -(-(z.blocks * z.gr) // 8) * 8
-
-    wait_bytes(rx1, recv.at[A1])
+    def whole_tile(ref, base, m, i):
+        total = None
+        for q in range(z.segments):
+            at = base + row_at(m, i, q)
+            total = ref[at : at + z.ch, :] if total is None else total + ref[at : at + z.ch, :]
+        return total
+
+    def windows(ref, m, h, back):
+        parts = []
+        for d in range(z.blocks):
+            first = (z.blocks - 1 - d) if back else d
+            start = m * z.stack + first * z.segments * z.ch + h
+            parts.append(ref[pl.ds(start, z.conv_rows, stride=z.ch), :])
+        return jnp.concatenate(parts, axis=1).astype(bf16)
+
     for m in range(z.micros):
+        wait_bytes(rx1.at[pl.ds(m * z.slots, z.slots)], recv.at[A1 + m])
         for i, tile in enumerate(lane_tiles(rx1, m)):
             masked_store(xs, pad_rows, m, i, tile)
 
-    def conv_one(h):
-        parts = [
-            xs[pl.ds((z.blocks - 1 - d) * z.gr * z.ch + h, conv_rows, stride=z.ch), :]
-            for d in range(z.blocks)
-        ]
-        windows = jnp.concatenate(parts, axis=1).astype(bf16)
-        ys[pl.ds(h, conv_rows, stride=z.ch), :] = dot(windows, near[h])
-
-    each_channel(conv_one, ch)
-    for m in range(z.micros):
+        def conv_one(h):
+            ys[pl.ds(h, z.conv_rows, stride=z.ch), :] = dot(windows(xs, m, h, True), near[h])
+
+        each_channel(conv_one, ch)
         tiles = []
         for i in range(z.blocks):
-            own = None
-            for q in range(z.segments):
-                at = pad_rows + row_at(i, m * z.segments + q)
-                own = xs[at : at + z.ch, :] if own is None else own + xs[at : at + z.ch, :]
-            tile = masked_sum(m, i) + skip[...] * own
+            tile = masked_sum(m, i) + skip[...] * whole_tile(xs, pad_rows, m, i)
             conv_out[m * z.blocks + i] = tile
             tiles.append(gelu(tile))
         lane_pieces(tiles, m, tx2)
-    to_members(lambda p: tx2.at[slot_of(p)], rx2, me, A2)
-    weights_beside(DOWN)
-    weights_core(UP)
-    weights_core(DOWN)
+        to_micro(m, tx2, rx2, A2)
+
+    @pl.when(pipe == 0)
+    def _():
+        weights_out(DOWN)
+        weights_up()
+
     wait_bytes(rx2, recv.at[A2])
     gated_s[...] = turn_in(rx2).astype(bf16)
     weights_here(GLU)
@@ -586,16 +665,17 @@
     inv2_s[...] = jnp.broadcast_to(inv2, (rows, LANES))
     ffn_s[...] = (hat2 * full_row(vec_all, 2) + full_row(vec_all, 3)).astype(bf16)
     weights_here(UP)
-    weights_here(DOWN)
     ffn_in = ffn_s[...]
-    total = mid + full_row(vec_all, 4)
     for c in range(z.peers):
         offset = jnp.concatenate([vec_all[c, 7 + r : 8 + r, :] for r in range(per)], axis=1)
         hidden = dot(ffn_in, up_all[c]) + offset
         hidden_s[c] = hidden
-        active = gelu(hidden).astype(bf16)
-        act_s[c] = active
-        total = total + dot(active, down_all[c])
+        act_s[c] = gelu(hidden).astype(bf16)
+    pl.when(pipe == 0)(weights_down)
+    weights_here(DOWN)
+    total = mid + full_row(vec_all, 4)
+    for c in range(z.peers):
+        total = total + dot(act_s[c], down_all[c])
     layer_out = jnp.where(row_ok, total, 0.0).astype(bf16)
     lay_s[...] = layer_out
 
@@ -606,7 +686,7 @@
         hatn_s[...] = hat
         invn_s[...] = jnp.broadcast_to(inv, (rows, LANES))
         turn_out(hat * full_row(vec_next, 0) + full_row(vec_next, 1), tx1n)
-        to_section(lambda p: tx1n.at[p], rx1, slot_me, A1, pipe + 1)
+        to_section(lambda p: tx1n.at[p], rx1, slot_me, A1 + own_micro, pipe + 1)
         remote(lay_s, res, RES, place(chan, data, pipe + 1)).start()
 
     def forward_rows():
@@ -668,7 +748,7 @@
         grad_gate.astype(bf16), glu_all[1].reshape(width, width)
     )
     turn_out(grad_gated, tx3)
-    to_members(lambda p: tx3.at[p], rx3, slot_me, A3)
+    to_members(lambda p: tx3.at[p], rx3, slot_me, A3 + own_micro)
     for j in range(z.peers // 2):
         gv = grad_value[:, j * LANES : (j + 1) * LANES]
         gg = shifted(grad_gate[:, j * LANES : (j + 1) * LANES], LANES // 2)
@@ -683,37 +763,23 @@
         to_section_peers(lambda c: ign_t.at[c], ig_rx, IG, pipe + 1)
         to_section(lambda p: vgn_s.at[p // z.groups], vnrx, me, VGN, pipe + 1)
 
-    wait_bytes(rx3, recv.at[A3])
     for m in range(z.micros):
+        wait_bytes(rx3.at[pl.ds(m * z.slots, z.slots)], recv.at[A3 + m])
         for i, tile in enumerate(lane_tiles(rx3, m)):
             masked_store(gs, 0, m, i, tile * gelu_slope(conv_out[m * z.blocks + i]))
 
-    def back_one(h):
-        parts = [
-            gs[pl.ds(d * z.gr * z.ch + h, conv_rows, stride=z.ch), :] for d in range(z.blocks)
+        def back_one(h):
+            ys[pl.ds(h, z.conv_rows, stride=z.ch), :] = dot_nt(windows(gs, m, h, False), far[h])
+
+        each_channel(back_one, ch)
+        tiles = [
+            masked_sum(m, i) + skip[...] * whole_tile(gs, 0, m, i) for i in range(z.blocks)
         ]
-        windows = jnp.concatenate(parts, axis=1).astype(bf16)
-        ys[pl.ds(h, conv_rows, stride=z.ch), :] = dot_nt(windows, far[h])
-
-    each_channel(back_one, ch)
-    for m in range(z.micros):
-        tiles = []
-        for i in range(z.blocks):
-            own = None
-            for q in range(z.segments):
-                at = row_at(i, m * z.segments + q)
-                own = gs[at : at + z.ch, :] if own is None else own + gs[at : at + z.ch, :]
-            tiles.append(masked_sum(m, i) + skip[...] * own)
         lane_pieces(tiles, m, tx4)
-
-    @pl.when(pipe == 0)
-    def _():
-        to_members(lambda p: tx4.at[slot_of(p)], rx4, me, A4)
-
-    @pl.when(pipe > 0)
-    def _():
-        to_section(lambda p: tx4.at[slot_of(p)], rx4n, me, A4N, pipe - 1)
-        backward_rows()
+        pl.when(pipe == 0)(lambda: to_micro(m, tx4, rx4, A4))
+        pl.when(pipe > 0)(lambda: to_micro(m, tx4, rx4n, A4N, pipe - 1))
+
+    pl.when(pipe > 0)(backward_rows)
 
     @pl.when(pipe == last)
     def _():
@@ -721,23 +787,44 @@
         forward_rows()
 
     def lag_one(h):
-        x = xs[pl.ds(pad_rows + h, conv_rows, stride=z.ch), :]
-        parts = [
-            gs[pl.ds(d * z.gr * z.ch + h, conv_rows, stride=z.ch), :] for d in range(z.blocks)
+        x = [
+            xs[pl.ds(m * z.stack + pad_rows + h, z.conv_rows, stride=z.ch), :]
+            for m in range(z.micros)
         ]
-        prod = dot_tn(x.astype(bf16), jnp.concatenate(parts, axis=1).astype(bf16))
+        g = jnp.concatenate([windows(gs, m, h, False) for m in range(z.micros)], axis=0)
+        prod = dot_tn(jnp.concatenate(x, axis=0).astype(bf16), g)
         prod = jnp.concatenate([prod, jnp.zeros((LANES, LANES), f32)], axis=1)
         size = LANES // 2
         while size >= 8:
             prod = prod[:size] + shifted(prod[size:], wide - size)
             size //= 2
-        row = prod[0:1]
-        for a in range(1, 8):
-            row = row + shifted(prod[a : a + 1], wide - a)
-        lag_s[pl.ds(h, 1), :] = row
+        for t in range(z.blocks + 1):
+            rest_s[t, pl.ds(pl.multiple_of(h * 8, 8), 8), :] = prod[:, t * LANES : (t + 1) * LANES]
+
+    def lag_rest():
+        total = None
+        for a in range(8):
+            tiles = [rest_s[t, pl.ds(a, ch, stride=8), :] for t in range(z.blocks + 1)]
+            part = shifted(jnp.concatenate(tiles, axis=1), wide - a)
+            total = part if total is None else total + part
+        lag_s[...] = total
 
     each_channel(lag_one, 4)
-
+    lag_rest()
+
+    many = z.peers * rows
+    grads = (
+        (ac, AC, bg, BG, z.hid, width, pdown, kdown, sdown, ldown, ddown),
+        (fi, FI, gh, GH, width, z.hid, pup, kup, sup, lup, dup),
+        (gp, GP, ga, GA, 2 * z.cw, width, pglu, kglu, sglu, lglu, dglu),
+    )
+    for t, (left, lp, right, rp, n_left, n_right, part, krx, *_) in enumerate(grads):
+        wait_bytes(left, recv.at[lp])
+        wait_bytes(right, recv.at[rp])
+        part[...] = dot_tn(left[...].reshape(many, n_left), right[...].reshape(many, n_right))
+        half = n_left // 2
+        other = pl.ds(pl.multiple_of((1 - core) * half, half), half)
+        remote(part.at[other], krx, GRADS + 3 * t, sibling).start()
     @pl.when(pipe == 0)
     def _():
         wait_bytes(rx4, recv.at[A4])
@@ -755,6 +842,13 @@
                 vg0_s[c, r : r + 1, :] = row[:, (c // 2) * LANES : (c // 2 + 1) * LANES]
         to_members(lambda p: vg0_s.at[p // z.groups], vnrx, me, VGN)
 
+    for t, (_, _, _, _, n_left, _, part, krx, lsend, lrx, _) in enumerate(grads):
+        half = n_left // 2
+        own = pl.ds(pl.multiple_of(core * half, half), half)
+        wait_bytes(krx, recv.at[GRADS + 3 * t])
+        lsend[...] = (part[own, :] + krx[...]).astype(bf16)
+        remote(lsend, lrx, GRADS + 3 * t + 1, across).start()
+
     rows_of = [
         jnp.sum(grad_ffn * hat2, axis=0, keepdims=True),
         jnp.sum(grad_ffn, axis=0, keepdims=True),
@@ -769,26 +863,6 @@
         for r in range(per):
             vg_s[c, 4 + r : 5 + r, :] = up_row[:, r * LANES : (r + 1) * LANES]
     to_members(lambda p: vg_s.at[p // z.groups], vrx, me, VG)
-    many = z.peers * rows
-    grads = (
-        (ac, AC, bg, BG, z.hid, width, pdown, kdown, sdown, ldown, ddown),
-        (fi, FI, gh, GH, width, z.hid, pup, kup, sup, lup, dup),
-        (gp, GP, ga, GA, 2 * z.cw, width, pglu, kglu, sglu, lglu, dglu),
-    )
-    for t, (left, lp, right, rp, n_left, n_right, part, krx, *_) in enumerate(grads):
-        wait_bytes(left, recv.at[lp])
-        wait_bytes(right, recv.at[rp])
-        part[...] = dot_tn(left[...].reshape(many, n_left), right[...].reshape(many, n_right))
-        half = n_left // 2
-        other = pl.ds(pl.multiple_of((1 - core) * half, half), half)
-        remote(part.at[other], krx, GRADS + 3 * t, sibling).start()
-    for t, (_, _, _, _, n_left, _, part, krx, lsend, lrx, _) in enumerate(grads):
-        half = n_left // 2
-        own = pl.ds(pl.multiple_of(core * half, half), half)
-        wait_bytes(krx, recv.at[GRADS + 3 * t])
-        lsend[...] = (part[own, :] + krx[...]).astype(bf16)
-        remote(lsend, lrx, GRADS + 3 * t + 1, across).start()
-
     both = dot_nt(high_low(lag_s[:, 0 : z.length]), table[...])
     grad_spec = both[0:ch] + both[ch : 2 * ch]
     gk = (grad_spec[:, 0:padded], grad_spec[:, padded : 2 * padded])
@@ -800,38 +874,42 @@
     g_ms = [gk, times(conj(ms[2]), g_top), times(conj(ms[1]), g_top), g_three]
     g_rise = None
     for v, (g_r, g_i) in enumerate(g_ms):
-        gsum_s[v] = 2.0 * cosine * g_r
-        gsum_s[4 + v] = -2.0 * cosine * g_i
-        gsum_s[8 + v] = 2.0 * y_all * g_i
-        gsum_s[12 + v] = 2.0 * y_all * g_r
+        gsum_s[v, :, 0:padded] = 2.0 * cosine * g_r
+        gsum_s[v, :, padded : 2 * padded] = -2.0 * cosine * g_i
+        gsum_s[4 + v, :, 0:padded] = 2.0 * y_all * g_i
+        gsum_s[4 + v, :, padded : 2 * padded] = 2.0 * y_all * g_r
         part = 2.0 * (sums_s[12 + v] * g_r + sums_s[8 + v] * g_i)
         g_rise = part if g_rise is None else g_rise + part
     slope_s[...] = g_rise
     gcol_s[...] = jnp.zeros(gcol_s.shape, f32)
     gstep_s[...] = jnp.zeros(gstep_s.shape, f32)
 
+    def split(x):
+        high_part = x.astype(bf16)
+        return high_part, (x - high_part.astype(f32)).astype(bf16)
+
+    g_high, g_low = split(gsum_s[...].reshape(8 * ch, 2 * padded))
+    own = [jnp.where(lax.rem(spot, ch) == h, cols[0], 0.0) for h in range(ch)]
+    c_high, c_low = split(jnp.concatenate(own, axis=0))
+    guw_s[...] = dot(c_high, g_high) + dot(c_high, g_low) + dot(c_low, g_high)
+    uw_high, uw_low = split(uw_s[...])
+    g_cols = dot_nt(uw_high, g_high) + dot_nt(uw_high, g_low) + dot_nt(uw_low, g_high)
+    total = g_cols[0:nh]
+    for h in range(1, ch):
+        total = jnp.where(lax.rem(spot, ch) == h, g_cols[h * nh : (h + 1) * nh], total)
+    gcol_s[0] = total
+
     def mode_one(h):
-        double, y, cy, u, w = modes_at(h)
-        column = column_of(0, h)
-        gu, gw = 0.0, 0.0
-        acc = gcol_s[0]
-        for v in range(4):
-            a = column[:, v * ch : v * ch + 1]
-            b = column[:, (4 + v) * ch : (4 + v) * ch + 1]
-            au, aw = gsum_s[v, pl.ds(h, 1), :], gsum_s[4 + v, pl.ds(h, 1), :]
-            bu, bw = gsum_s[8 + v, pl.ds(h, 1), :], gsum_s[12 + v, pl.ds(h, 1), :]
-            gu = gu + a * au + b * bu
-            gw = gw + a * aw + b * bw
-            ga_col = jnp.sum(u * au + w * aw, axis=1, keepdims=True)
-            gb_col = jnp.sum(u * bu + w * bw, axis=1, keepdims=True)
-            acc = jnp.where(spot == v * ch + h, ga_col, acc)
-            acc = jnp.where(spot == (4 + v) * ch + h, gb_col, acc)
-        gcol_s[0] = acc
+        at = pl.ds(pl.multiple_of(h * nh, nh), nh)
+        u, w = uw_s[at, 0:padded], uw_s[at, padded : 2 * padded]
+        gu, gw = guw_s[at, 0:padded], guw_s[at, padded : 2 * padded]
+        double = column_of(1, h)[:, ch : ch + 1]
+        y = rise_s[pl.ds(h, 1), 0:1] * sine
         even, cross_uw = u * u - w * w, 2.0 * u * w
         g_den_r = -(even * gu + cross_uw * gw)
         g_den_i = even * gw - cross_uw * gu
         ge = jnp.sum(cosine * cosine * g_den_r, axis=1, keepdims=True)
-        gf = jnp.sum(cy * g_den_i, axis=1, keepdims=True)
+        gf = jnp.sum(cosine * y * g_den_i, axis=1, keepdims=True)
         acc = jnp.where(spot == h, ge, gcol_s[1])
         gcol_s[1] = jnp.where(spot == ch + h, gf, acc)
         gy = slope_s[pl.ds(h, 1), :] + jnp.sum(
@@ -840,7 +918,7 @@
         total_y = jnp.sum(y * gy, axis=1, keepdims=True)
         gstep_s[0:1, :] = jnp.where(spot == h, -total_y, gstep_s[0:1, :])
 
-    each_channel(mode_one, 2)
+    each_channel(mode_one, 4)
 
     def unpacked(k, i):
         return shifted(gcol_s[k], LANES - i * ch)
@@ -944,7 +1022,7 @@
         (vec_all, VEC), (hid_rx, HID), (ga, GA), (fi, FI), (ac, AC), (bg, BG), (gh, GH), (gp, GP),
     ):
         wait_bytes(ref.at[pl.ds(0, z.peers - 1)], send.at[phase])
-    for ref, phase in ((rx2, A2), (rx3, A3), (vrx, VG)):
+    for ref, phase in ((rx2, A2), (rx3, A3 + own_micro), (vrx, VG)):
         wait_bytes(ref.at[pl.ds(0, z.members - 1)], send.at[phase])
     wait_bytes(modes_rx.at[pl.ds(0, z.groups - 1)], send.at[MODES])
     for t, (_, _, _, _, n_left, _, _, krx, lsend, _, final) in enumerate(grads):
@@ -956,7 +1034,7 @@
     def _():
         wait_bytes(tok_rx.at[pl.ds(0, z.peers - 1)], send.at[TOK])
         wait_bytes(ig_rx.at[pl.ds(0, z.peers - 1)], send.at[IG])
-        for ref, phase in ((rx1, A1), (rx4, A4), (vnrx, VGN)):
+        for ref, phase in ((rx1, A1 + own_micro), (rx4, A4), (vnrx, VGN)):
             wait_bytes(ref.at[pl.ds(0, z.members - 1)], send.at[phase])
 
     @pl.when(pipe == last)
@@ -965,7 +1043,7 @@
 
     @pl.when(pipe < last)
     def _():
-        for ref, phase in ((rx1, A1), (lay_s, RES), (ig_rx, IG), (vnrx, VGN)):
+        for ref, phase in ((rx1, A1 + own_micro), (lay_s, RES), (ig_rx, IG), (vnrx, VGN)):
             wait_bytes(ref, send.at[phase])
 
     @pl.when(pipe > 0)
@@ -1028,7 +1106,6 @@
     def v(shape, kind=bf16):
         return pltpu.VMEM(shape, kind)
 
-    conv_rows = -(-(z.blocks * z.gr) // 8) * 8
     wide = (z.blocks + 1) * LANES
     rows_full, rows_wide, side = v((r, w)), v((r, w), f32), v((r, LANES), f32)
     peer_tiles, exchange = v((n, chan_width, LANES)), v((z.members, z.ch, LANES))
@@ -1046,10 +1123,13 @@
         out_specs=[vmem] * 10,
         scratch_shapes=[
             peer_tiles, peer_tiles, v((16, LANES), f32), v((ch, length, LANES)),
-            v((ch, LANES, length)), v((ch, LANES), f32), v((conv_rows, LANES), f32),
-            peer_tiles, peer_tiles, v((z.stack, LANES), f32), v((z.stack, LANES), f32),
+            v((ch, LANES, length)), v((ch, LANES), f32), v((40, LANES), f32),
+            peer_tiles, peer_tiles, v((micros * z.stack, LANES), f32),
+            v((micros * z.stack, LANES), f32),
             v((2 * padded, length)), v((2, nh, LANES), f32),
-            v((ch, LANES), f32), v((16, ch, padded), f32), v((16, ch, padded), f32),
+            v((ch, LANES), f32), v((16, ch, padded), f32), v((ch * nh, 2 * padded), f32),
+            v((ch * nh, 2 * padded), f32), v((z.blocks + 1, 8 * ch, LANES), f32),
+            v((8, ch, 2 * padded), f32),
             v((ch, padded), f32), v((ch, wide), f32), v((ch, wide), f32),
             v((2, nh, LANES), f32), v((8, LANES), f32),
             v((nh + 8, LANES), f32), v((z.groups, nh + 8, LANES), f32),
@@ -1064,7 +1144,7 @@
         ]
         + [exchange] * 10
         + [
-            v((z.micros * z.blocks, z.ch, LANES), f32), v((conv_rows * z.ch, LANES), f32),
+            v((z.micros * z.blocks, z.ch, LANES), f32), v((z.conv_rows * z.ch, LANES), f32),
             rows_wide, side, rows_wide, side, rows_wide, side,
             rows_wide, rows_wide, v((n, r, hidden), f32),
             rows_full, rows_full, v((n, r, hidden)), v((n, r, hidden)), v((n, r, LANES)),
@@ -1072,7 +1152,7 @@
             small, small, small,
             v((n, r, w)), v((n, r, w)), v((n, r, hidden)), v((n, r, w)), v((n, r, hidden)),
             v((n, r, LANES)), v((z.members, 8, LANES), f32), v((z.members, 8, LANES), f32),
-            pltpu.SemaphoreType.DMA((50,)), pltpu.SemaphoreType.DMA((50,)),
+            pltpu.SemaphoreType.DMA((52,)), pltpu.SemaphoreType.DMA((52,)),
         ],
         compiler_params=pltpu.CompilerParams(
             collective_id=0, has_side_effects=True, vmem_limit_bytes=60 * 2**20

time: 208 us -> 185 us (0.89)
  Pallas kernels: 207 us -> 184 us
    pallas_call x1, Pallas kernels: 204 us -> 181 us  [body(): pl.pallas_call(lambda *refs: main_kernel(z, *refs), out_shape=results, in...]
where the time goes in v4:
time: 185 us
  Pallas kernels  184 us (99%)
    pallas_call x1, Pallas kernels, body(): pl.pallas_call(lambda *refs: main_kernel(z, *refs), out_shape=results, in...  181 us

profile of v4, /device:TPU:1, one launch (start us, length us, event | category | flops | bytes accessed | tf_op | source)
XLA Modules:
  0.0 184.7 jit_solution(8443524691887171416)
XLA Ops:
  0.6 181.4 %layers.1 = (bf16[2,64,288]{2,1,0:T(8,128)(2,1)}, bf16[2,64,288]{2,1,0:T(8,128)(2,1)}, f32[4,64]{1,0:T(4,128)}, f32[8,32,64]{2,1,0:T(8,128)}, f32[2,64,512]{2,1,...) custom-call(s32[2,2]{1,0:T(2,128)} %refs_0_.1, ...), custom_call_target="tpu_custom_call" | custom-call | tf_op jit(solution)/shard_map/layers/pallas_call | solution.py:1119
  182.1 2.5 %finish.1 = (bf16[2,64,288]{2,1,0:T(8,128)(2,1)}, bf16[2,64,288]{2,1,0:T(8,128)(2,1)}, f32[4,64]{1,0:T(4,128)}, f32[8,32,64]{2,1,0:T(8,128)}, f32[2,64,512]{2,1,...) custom-call(bf16[2,64,288]{2,1,0:T(8,128)(2,1)} %get-tuple-element.3, ...), custom_call_target="tpu_custom_call" | custom-call | tf_op jit(solution)/shard_map/finish/pallas_call | solution.py:1166

commit v5 on v4

--- a/solution.py
+++ b/solution.py
@@ -226,20 +226,41 @@
         VEC, VECN, TOK, COT, A2, A4, A4N, RES, MID, HID, IG, GA, FI, AC, BG, GH, GP, VG,
         VGN, TABLE, MODES,
     ) = range(21)
-    A1, A3, GLU, UP, DOWN, GRADS = 21, 23, 25, 31, 37, 43
+    A1, A3, GLU, UPA, UPB, DNA, DNB, GRADS = 21, 23, 25, 31, 37, 43, 49, 55
+    direct = (DNB,)
     own_micro = chan // z.quarters
 
     own_side, far_side = high * z.quarters, (1 - high) * z.quarters
     sibling, across = place(chan, side * 2 + 1 - core), place(chan, (1 - side) * 2 + core)
 
+    def columns(t):
+        if t == GLU:
+            return glu_loc, glu_all
+        loc, whole = (up_loc, up_all) if t in (UPA, UPB) else (down_loc, down_all)
+        count = loc.shape[1] // 2
+        where = pl.ds(count if t in (UPB, DNB) else 0, count)
+        return loc.at[:, where], whole.at[:, :, where]
+
+    def own_rows(t, part=None):
+        loc, _ = columns(t)
+        if t == GLU:
+            fourth = z.cw // 2
+            half = loc.at[core]
+            return half if part is None else half.at[pl.ds(pl.multiple_of(part * fourth, fourth), fourth)]
+        half = loc.shape[0] // 2
+        if part is None:
+            return loc.at[pl.ds(pl.multiple_of(core * half, half), half)]
+        fourth = half // 2
+        return loc.at[pl.ds(pl.multiple_of(core * half + part * fourth, fourth), fourth)]
+
     def piece_of(t, c, count, part=None):
+        loc, whole = columns(t)
         if t == GLU:
+            fourth = z.cw // 2
             if part is None:
-                return glu_all.at[core, pl.ds(c, count)]
-            fourth = z.cw // 2
+                return whole.at[core, pl.ds(c, count)]
             start = pl.multiple_of(part * fourth, fourth)
-            return glu_all.at[core, pl.ds(c, count), pl.ds(start, fourth)]
-        loc, whole = (up_loc, up_all) if t == UP else (down_loc, down_all)
+            return whole.at[core, pl.ds(c, count), pl.ds(start, fourth)]
         half = loc.shape[0] // 2
         fourth = half // 2
         if part is None:
@@ -248,28 +269,22 @@
         return whole.at[pl.ds(c, count), pl.ds(start, fourth)]
 
     def weights_out(t):
-        if t == GLU:
-            loc, whole, half = glu_loc, glu_all.at[:, chan], glu_loc.at[core]
-            fourth = z.cw // 2
-            quarter = half.at[pl.ds(pl.multiple_of(side * fourth, fourth), fourth)]
-        else:
-            loc, whole = (up_loc, up_all) if t == UP else (down_loc, down_all)
-            size = loc.shape[0] // 2
-            fourth = size // 2
-            whole, half = whole.at[chan], loc.at[pl.ds(pl.multiple_of(core * size, size), size)]
-            start = pl.multiple_of(core * size + side * fourth, fourth)
-            quarter = loc.at[pl.ds(start, fourth)]
+        loc, whole = columns(t)
+        whole = whole.at[:, chan] if t == GLU else whole.at[chan]
         pltpu.make_async_copy(loc, whole, recv.at[t + 5]).start()
-        there = piece_of(t, chan, 1, side).at[0]
-        for k in range(z.quarters):
+        part = None if t in direct else side
+        payload, there = own_rows(t, part), piece_of(t, chan, 1, part).at[0]
+        for k in (2, 3, 1, 0):
             c = far_side + lax.rem(deep + k, z.quarters)
-            remote(quarter, there, t + 1, place(c, (1 - side) * 2 + core)).start()
-        there = piece_of(t, chan, 1).at[0]
-        for k in range(1, z.quarters):
+            remote(payload, there, t + 1, place(c, (1 - side) * 2 + core)).start()
+        payload, there = own_rows(t), piece_of(t, chan, 1).at[0]
+        for k in (2, 3, 1):
             c = own_side + lax.rem(deep + k, z.quarters)
-            remote(half, there, t, place(c, data)).start()
+            remote(payload, there, t, place(c, data)).start()
 
     def weights_beside(t):
+        if t in direct:
+            return
         wait_bytes(piece_of(t, 0, z.quarters, 0), recv.at[t + 1])
         piece = piece_of(t, far_side, z.quarters, 1 - side)
         remote(piece, piece, t + 2, across).start()
@@ -281,51 +296,46 @@
             remote(piece, piece, t + 3, sibling).start()
 
     def weights_core(t):
-        wait_bytes(piece_of(t, 0, z.quarters, 0), recv.at[t + 2])
+        if t in direct:
+            wait_bytes(piece_of(t, 0, z.quarters), recv.at[t + 1])
+        else:
+            wait_bytes(piece_of(t, 0, z.quarters, 0), recv.at[t + 2])
         piece = piece_of(t, far_side, z.quarters)
         remote(piece, piece, t + 4, sibling).start()
 
     def weights_here(t):
-        wait_bytes({GLU: glu_loc, UP: up_loc, DOWN: down_loc}[t], recv.at[t + 5])
+        wait_bytes(columns(t)[0], recv.at[t + 5])
         wait_bytes(piece_of(t, 0, z.quarters - 1), recv.at[t + 3])
         wait_bytes(piece_of(t, 0, z.quarters), recv.at[t + 4])
 
     def weights_sent(t):
-        for stage, count, part in (
-            (0, z.quarters - 1, None), (1, z.quarters, 0), (2, z.quarters, 0),
-            (3, z.quarters - 1, None), (4, z.quarters, None),
-        ):
+        far_part = None if t in direct else 0
+        stages = [(0, z.quarters - 1, None), (1, z.quarters, far_part)]
+        if t not in direct:
+            stages.append((2, z.quarters, 0))
+        stages += [(3, z.quarters - 1, None), (4, z.quarters, None)]
+        for stage, count, part in stages:
             wait_bytes(piece_of(t, 0, count, part), send.at[t + stage])
 
+    def weights_all(steps, *which):
+        for t in which:
+            for step in steps:
+                step(t)
+
+    forward_steps = (weights_beside, weights_near)
+
     barrier = pltpu.get_barrier_semaphore()
 
-    def greet(p, section):
-        pl.semaphore_signal(
-            barrier, inc=1, device_id=member(p, section), device_id_type=pl.DeviceIdType.MESH
-        )
+    def greet(where):
+        pl.semaphore_signal(barrier, inc=1, device_id=where, device_id_type=pl.DeviceIdType.MESH)
 
     def greet_own(k, carry):
-        greet(lax.rem(me + k, z.members), None)
+        greet(member(lax.rem(me + k, z.members)))
         return carry
 
-    def greet_next(k, carry):
-        greet(lax.rem(me + k, z.members), pipe + 1)
-        return carry
-
-    def greet_before(k, carry):
-        greet(lax.rem(me + k, z.members), pipe - 1)
-        return carry
-
+    pl.when(pipe < last)(lambda: greet(place(chan, data, pipe + 1)))
+    pl.when(pipe > 0)(lambda: greet(place(chan, data, pipe - 1)))
     lax.fori_loop(1, z.members, greet_own, 0)
-
-    @pl.when(pipe < last)
-    def _():
-        lax.fori_loop(0, z.members, greet_next, 0)
-
-    @pl.when(pipe > 0)
-    def _():
-        lax.fori_loop(0, z.members, greet_before, 0)
-
     pltpu.make_async_copy(table_in, table, recv.at[TABLE]).start()
 
     def own_half(x):
@@ -414,7 +424,7 @@
             sums_s[8 + v, pl.ds(h, 1), :] = jnp.sum(b * u, axis=0, keepdims=True)
             sums_s[12 + v, pl.ds(h, 1), :] = jnp.sum(b * w, axis=0, keepdims=True)
 
-    def each_channel(one, unroll):
+    def each_channel(one, unroll, first=0, end=None):
         def step(i, carry):
             for u in range(unroll):
                 one(i * unroll + u)
@@ -423,7 +433,7 @@
         if unroll == ch:
             step(0, 0)
         else:
-            lax.fori_loop(0, ch // unroll, step, 0)
+            lax.fori_loop(first // unroll, (ch if end is None else end) // unroll, step, 0)
 
     def times(a, b):
         return a[0] * b[0] - a[1] * b[1], a[0] * b[1] + a[1] * b[0]
@@ -470,7 +480,7 @@
 
     pl.semaphore_wait(
         barrier,
-        z.members - 1 + z.members * (jnp.minimum(pipe, 1) + jnp.minimum(last - pipe, 1)),
+        z.members - 1 + jnp.minimum(pipe, 1) + jnp.minimum(last - pipe, 1),
     )
 
     @pl.when(pipe == 0)
@@ -479,10 +489,6 @@
 
     to_peers(lambda c: vec_tx, vec_all, VEC)
     weights_out(GLU)
-
-    @pl.when(pipe > 0)
-    def _():
-        to_section_peers(lambda c: vec_tx, vec_next, VECN, pipe - 1)
 
     @pl.when(pipe == last)
     def _():
@@ -526,6 +532,10 @@
 
     wait_bytes(vec_all, recv.at[VEC])
 
+    @pl.when(pipe > 0)
+    def _():
+        remote(vec_all, vec_next, VECN, place(chan, data, pipe - 1)).start()
+
     @pl.when(pipe == 0)
     def _():
         wait_bytes(tok_rx, recv.at[TOK])
@@ -537,8 +547,12 @@
         turn_out(hat1 * full_row(vec_all, 0) + full_row(vec_all, 1), tx1)
         to_members(lambda p: tx1.at[p], rx1, slot_me, A1 + own_micro)
 
-    weights_out(UP)
-    pl.when(pipe > 0)(lambda: weights_out(DOWN))
+    weights_out(UPA)
+    pl.when(pipe == 0)(lambda: weights_out(UPB))
+
+    @pl.when(pipe > 0)
+    def _():
+        weights_all((weights_out,), UPB, DNA, DNB)
 
     def toeplitz_one(h):
         full = jnp.broadcast_to(kern_s[pl.ds(h, 1), :], (LANES, wide))
@@ -548,23 +562,12 @@
             near[h, d * LANES : (d + 1) * LANES, :] = full[:, d * LANES : (d + 1) * LANES]
 
     each_channel(toeplitz_one, 2)
-    weights_beside(GLU)
-    weights_near(GLU)
-
-    def weights_up():
-        weights_beside(UP)
-        weights_near(UP)
-        weights_core(UP)
-
-    def weights_down():
-        weights_beside(DOWN)
-        weights_near(DOWN)
-        weights_core(DOWN)
+    weights_all(forward_steps, GLU)
 
     @pl.when(pipe > 0)
     def _():
-        weights_up()
-        weights_down()
+        weights_all(forward_steps, UPA, UPB, DNA, DNB)
+        weights_all((weights_core,), UPA, UPB, DNA, DNB)
 
     weights_core(GLU)
 
@@ -645,8 +648,10 @@
 
     @pl.when(pipe == 0)
     def _():
-        weights_out(DOWN)
-        weights_up()
+        weights_out(DNA)
+        weights_out(DNB)
+        weights_all(forward_steps, UPA, UPB)
+        weights_all((weights_core,), UPA)
 
     wait_bytes(rx2, recv.at[A2])
     gated_s[...] = turn_in(rx2).astype(bf16)
@@ -664,15 +669,27 @@
     hat2_s[...] = hat2
     inv2_s[...] = jnp.broadcast_to(inv2, (rows, LANES))
     ffn_s[...] = (hat2 * full_row(vec_all, 2) + full_row(vec_all, 3)).astype(bf16)
-    weights_here(UP)
+
+    @pl.when(pipe == 0)
+    def _():
+        weights_core(UPB)
+        weights_all(forward_steps, DNA)
+
+    weights_all((weights_here,), UPA, UPB)
     ffn_in = ffn_s[...]
     for c in range(z.peers):
         offset = jnp.concatenate([vec_all[c, 7 + r : 8 + r, :] for r in range(per)], axis=1)
         hidden = dot(ffn_in, up_all[c]) + offset
         hidden_s[c] = hidden
         act_s[c] = gelu(hidden).astype(bf16)
-    pl.when(pipe == 0)(weights_down)
-    weights_here(DOWN)
+
+    @pl.when(pipe == 0)
+    def _():
+        weights_core(DNA)
+        weights_all(forward_steps, DNB)
+        weights_core(DNB)
+
+    weights_all((weights_here,), DNA, DNB)
     total = mid + full_row(vec_all, 4)
     for c in range(z.peers):
         total = total + dot(act_s[c], down_all[c])
@@ -694,8 +711,10 @@
         to_peers(lambda c: ffn_s, fi, FI)
         to_peers(lambda c: act_s.at[c], ac, AC)
 
-    def backward_rows():
+    def top_rows():
         to_peers(lambda c: gtop, bg, BG)
+
+    def hidden_rows():
         to_peers(lambda c: gh_s.at[c], gh, GH)
         to_peers(lambda c: gp_s.at[c], gp, GP)
 
@@ -755,7 +774,7 @@
         gp_s[2 * j] = jnp.where(first_half, gv, gg).astype(bf16)
         gp_s[2 * j + 1] = jnp.where(first_half, gg, gv).astype(bf16)
     pl.when(pipe > 0)(lambda: remote(mid_s, mid_rx, MID, place(chan, data, pipe - 1)).start())
-    pl.when(pipe == 0)(backward_rows)
+    pl.when(pipe == 0)(top_rows)
 
     @pl.when(pipe < last)
     def _():
@@ -779,12 +798,47 @@
         pl.when(pipe == 0)(lambda: to_micro(m, tx4, rx4, A4))
         pl.when(pipe > 0)(lambda: to_micro(m, tx4, rx4n, A4N, pipe - 1))
 
-    pl.when(pipe > 0)(backward_rows)
+    pl.when(pipe > 0)(top_rows)
+    hidden_rows()
 
     @pl.when(pipe == last)
     def _():
         to_peers(lambda c: lay_t.at[c], hid_rx, HID)
         forward_rows()
+
+    many = z.peers * rows
+    grads = (
+        (ac, AC, bg, BG, z.hid, width, pdown, kdown, sdown, ldown, ddown),
+        (fi, FI, gh, GH, width, z.hid, pup, kup, sup, lup, dup),
+        (gp, GP, ga, GA, 2 * z.cw, width, pglu, kglu, sglu, lglu, dglu),
+    )
+
+    def product(t):
+        left, lp, right, rp, n_left, n_right, part, krx, *_ = grads[t]
+        wait_bytes(left, recv.at[lp])
+        wait_bytes(right, recv.at[rp])
+        part[...] = dot_tn(left[...].reshape(many, n_left), right[...].reshape(many, n_right))
+        half = n_left // 2
+        other = pl.ds(pl.multiple_of((1 - core) * half, half), half)
+        remote(part.at[other], krx, GRADS + 3 * t, sibling).start()
+
+    def chip_sum(t):
+        _, _, _, _, n_left, _, part, krx, lsend, lrx, _ = grads[t]
+        half = n_left // 2
+        own = pl.ds(pl.multiple_of(core * half, half), half)
+        wait_bytes(krx, recv.at[GRADS + 3 * t])
+        lsend[...] = (part[own, :] + krx[...]).astype(bf16)
+        remote(lsend, lrx, GRADS + 3 * t + 1, across).start()
+
+    def both_chips(t):
+        _, _, _, _, n_left, _, _, _, lsend, lrx, final = grads[t]
+        half = n_left // 2
+        own = pl.ds(pl.multiple_of(core * half, half), half)
+        wait_bytes(lrx, recv.at[GRADS + 3 * t + 1])
+        final[own, :] = lsend[...].astype(f32) + lrx[...].astype(f32)
+        remote(final.at[own], final.at[own], GRADS + 3 * t + 2, sibling).start()
+
+    product(0)
 
     def lag_one(h):
         x = [
@@ -809,22 +863,14 @@
             total = part if total is None else total + part
         lag_s[...] = total
 
-    each_channel(lag_one, 4)
+    each_channel(lag_one, 4, 0, ch // 2)
+    chip_sum(0)
+    each_channel(lag_one, 4, ch // 2, ch)
     lag_rest()
-
-    many = z.peers * rows
-    grads = (
-        (ac, AC, bg, BG, z.hid, width, pdown, kdown, sdown, ldown, ddown),
-        (fi, FI, gh, GH, width, z.hid, pup, kup, sup, lup, dup),
-        (gp, GP, ga, GA, 2 * z.cw, width, pglu, kglu, sglu, lglu, dglu),
-    )
-    for t, (left, lp, right, rp, n_left, n_right, part, krx, *_) in enumerate(grads):
-        wait_bytes(left, recv.at[lp])
-        wait_bytes(right, recv.at[rp])
-        part[...] = dot_tn(left[...].reshape(many, n_left), right[...].reshape(many, n_right))
-        half = n_left // 2
-        other = pl.ds(pl.multiple_of((1 - core) * half, half), half)
-        remote(part.at[other], krx, GRADS + 3 * t, sibling).start()
+    product(1)
+    product(2)
+
+
     @pl.when(pipe == 0)
     def _():
         wait_bytes(rx4, recv.at[A4])
@@ -842,12 +888,8 @@
                 vg0_s[c, r : r + 1, :] = row[:, (c // 2) * LANES : (c // 2 + 1) * LANES]
         to_members(lambda p: vg0_s.at[p // z.groups], vnrx, me, VGN)
 
-    for t, (_, _, _, _, n_left, _, part, krx, lsend, lrx, _) in enumerate(grads):
-        half = n_left // 2
-        own = pl.ds(pl.multiple_of(core * half, half), half)
-        wait_bytes(krx, recv.at[GRADS + 3 * t])
-        lsend[...] = (part[own, :] + krx[...]).astype(bf16)
-        remote(lsend, lrx, GRADS + 3 * t + 1, across).start()
+    chip_sum(1)
+    chip_sum(2)
 
     rows_of = [
         jnp.sum(grad_ffn * hat2, axis=0, keepdims=True),
@@ -955,12 +997,8 @@
         remote(modes_tx, modes_rx.at[data], MODES, place(chan, lax.rem(data + k, z.groups))).start()
     pltpu.make_async_copy(modes_tx, modes_rx.at[data], recv.at[MODES]).start()
 
-    for t, (_, _, _, _, n_left, _, _, _, lsend, lrx, final) in enumerate(grads):
-        half = n_left // 2
-        own = pl.ds(pl.multiple_of(core * half, half), half)
-        wait_bytes(lrx, recv.at[GRADS + 3 * t + 1])
-        final[own, :] = lsend[...].astype(f32) + lrx[...].astype(f32)
-        remote(final.at[own], final.at[own], GRADS + 3 * t + 2, sibling).start()
+    for t in range(3):
+        both_chips(t)
 
     def collect(source, target):
         count = tok * z.quarters
@@ -1016,8 +1054,7 @@
     glu_out[0] = dglu[pl.ds(pl.multiple_of(odd * z.cw, z.cw), z.cw), :]
     glu_out[1] = dglu[pl.ds(pl.multiple_of((1 - odd) * z.cw, z.cw), z.cw), :]
 
-    for t in (GLU, UP, DOWN):
-        weights_sent(t)
+    weights_all((weights_sent,), GLU, UPA, UPB, DNA, DNB)
     for ref, phase in (
         (vec_all, VEC), (hid_rx, HID), (ga, GA), (fi, FI), (ac, AC), (bg, BG), (gh, GH), (gp, GP),
     ):
@@ -1152,7 +1189,7 @@
             small, small, small,
             v((n, r, w)), v((n, r, w)), v((n, r, hidden)), v((n, r, w)), v((n, r, hidden)),
             v((n, r, LANES)), v((z.members, 8, LANES), f32), v((z.members, 8, LANES), f32),
-            pltpu.SemaphoreType.DMA((52,)), pltpu.SemaphoreType.DMA((52,)),
+            pltpu.SemaphoreType.DMA((64,)), pltpu.SemaphoreType.DMA((64,)),
         ],
         compiler_params=pltpu.CompilerParams(
             collective_id=0, has_side_effects=True, vmem_limit_bytes=60 * 2**20

time: 185 us -> 177 us (0.957)
  Pallas kernels: 184 us -> 176 us
    pallas_call x1, Pallas kernels: 181 us -> 173 us  [body(): pl.pallas_call(lambda *refs: main_kernel(z, *refs), out_shape=results, in...]
where the time goes in v5:
time: 177 us
  Pallas kernels  176 us (99%)
    pallas_call x1, Pallas kernels, body(): pl.pallas_call(lambda *refs: main_kernel(z, *refs), out_shape=results, in...  173 us

profile of v5, /device:TPU:1, one launch (start us, length us, event | category | flops | bytes accessed | tf_op | source)
XLA Modules:
  0.0 176.6 jit_solution(4776104562054026949)
XLA Ops:
  0.6 173.3 %layers.1 = (bf16[2,64,288]{2,1,0:T(8,128)(2,1)}, bf16[2,64,288]{2,1,0:T(8,128)(2,1)}, f32[4,64]{1,0:T(4,128)}, f32[8,32,64]{2,1,0:T(8,128)}, f32[2,64,512]{2,1,...) custom-call(s32[2,2]{1,0:T(2,128)} %refs_0_.1, ...), custom_call_target="tpu_custom_call" | custom-call | tf_op jit(solution)/shard_map/layers/pallas_call | solution.py:1156
  174.0 2.5 %finish.1 = (bf16[2,64,288]{2,1,0:T(8,128)(2,1)}, bf16[2,64,288]{2,1,0:T(8,128)(2,1)}, f32[4,64]{1,0:T(4,128)}, f32[8,32,64]{2,1,0:T(8,128)}, f32[2,64,512]{2,1,...) custom-call(bf16[2,64,288]{2,1,0:T(8,128)(2,1)} %get-tuple-element.3, ...), custom_call_target="tpu_custom_call" | custom-call | tf_op jit(solution)/shard_map/finish/pallas_call | solution.py:1203

commit v6 on v5

--- a/solution.py
+++ b/solution.py
@@ -73,6 +73,8 @@
         self.rows = -(-self.tok // 16) * 16
         self.length = tok_rows * groups
         self.blocks = self.length // LANES
+        self.local = tok_rows
+        self.over = -(-tok_rows // LANES) * LANES
         self.width = model_width
         self.cw = chan_width
         self.hid = hidden
@@ -98,10 +100,10 @@
         modes_tx, modes_rx, pglu, pup, pdown, kglu, kup, kdown, sglu, sup, sdown,
         lglu, lup, ldown, dglu,
         vec_all, vec_next, glu_all, up_all, down_all, tok_rx, cot_rx, res, gtop,
-        tx1, tx1n, rx1, tx2, rx2, tx3, rx3, tx4, rx4, rx4n,
-        conv_out, ys, hat1_s, inv1_s, hatn_s, invn_s, hat2_s, inv2_s, val_s, sig_s, hidden_s,
+        tx1n, rx1, tx2, rx2, tx3, rx3, tx4, rx4, rx4n,
+        conv_out, ys, hatn_s, invn_s, hat2_s, inv2_s, val_s, sig_s, hidden_s,
         gated_s, ffn_s, act_s, gh_s, gp_s, lay_s, lay_t, ig_t, ign_t, mid_s, mid_rx,
-        vg_s, vgn_s, vg0_s, ga, fi, ac, bg, gh, gp, vrx, vnrx, send, recv,
+        stat_tx, stat_rx, entry_tx, entry_rx, vg_s, vgn_s, vg0_s, ga, fi, ac, bg, gh, gp, vrx, vnrx, send, recv,
     ) = refs[23:]
     pipe = lax.axis_index("pipe")
     chan = lax.axis_index("chan")
@@ -223,10 +225,11 @@
         lax.fori_loop(0, z.peers, step, 0)
 
     (
-        VEC, VECN, TOK, COT, A2, A4, A4N, RES, MID, HID, IG, GA, FI, AC, BG, GH, GP, VG,
+        VEC, VECN, TOK, COT, A2, A4, A4N, RES, MID, HID, IG, GA, FI, AC, GH, GP, VG,
         VGN, TABLE, MODES,
-    ) = range(21)
-    A1, A3, GLU, UPA, UPB, DNA, DNB, GRADS = 21, 23, 25, 31, 37, 43, 49, 55
+    ) = range(20)
+    STAT, ENTRY = 66, 67
+    A1, A3, GLU, UPA, UPB, DNA, DNB, GRADS, BG = 21, 23, 25, 31, 37, 43, 49, 55, 64
     direct = (DNB,)
     own_micro = chan // z.quarters
 
@@ -340,6 +343,8 @@
 
     def own_half(x):
         return pltpu.roll(x, odd * (LANES // 2), x.ndim - 1)
+
+    stat_tx[...] = jnp.zeros(stat_tx.shape, f32)
 
     def fill_blocks(source, target):
         count = z.tok * z.quarters
@@ -485,10 +490,16 @@
 
     @pl.when(pipe == 0)
     def _():
+        for m in range(z.micros):
+            x = tokens[m].astype(f32)
+            stat_tx[2 * m : 2 * m + 1, 0 : z.local] = jnp.sum(x, axis=0, keepdims=True)
+            stat_tx[2 * m + 1 : 2 * m + 2, 0 : z.local] = jnp.sum(x * x, axis=0, keepdims=True)
+        to_peers(lambda c: stat_tx, stat_rx, STAT)
         to_peers(lambda c: tok_tx.at[c], tok_rx, TOK)
 
     to_peers(lambda c: vec_tx, vec_all, VEC)
     weights_out(GLU)
+    pl.when(pipe == 0)(lambda: weights_all((weights_out,), UPA, UPB))
 
     @pl.when(pipe == last)
     def _():
@@ -530,38 +541,70 @@
         ]
         return jnp.concatenate(tiles, axis=1)
 
+    @pl.when(pipe == 0)
+    def _():
+        tall = lax.broadcasted_iota(jnp.int32, (z.cw, LANES), 0) == spot
+
+        def upright_all(r):
+            row = jnp.concatenate([vectors[r : r + 1, :], jnp.zeros((1, LANES - z.cw), f32)], axis=1)
+            return jnp.sum(jnp.where(tall, row, 0.0), axis=1, keepdims=True)
+
+        gain, bias = upright_all(0), upright_all(1)
+        wait_bytes(stat_rx, recv.at[STAT])
+        total = stat_rx[0]
+        for c in range(1, z.peers):
+            total = total + stat_rx[c]
+        total = total * (1.0 / width)
+        for m in range(z.micros):
+            mean = total[2 * m : 2 * m + 1, 0 : z.local]
+            spread = total[2 * m + 1 : 2 * m + 2, 0 : z.local] - mean * mean
+            hat = (tokens[m].astype(f32) - mean) * lax.rsqrt(spread + norm_eps)
+            normed = (hat * gain + bias).astype(bf16)
+            for d in range(z.groups):
+                entry_tx[d, m, :, 0 : z.local] = normed[d * ch : (d + 1) * ch, :]
+        for k in range(1, z.groups):
+            d = lax.rem(data + k, z.groups)
+            remote(entry_tx.at[d], entry_rx.at[data], ENTRY, place(chan, d)).start()
+        pltpu.make_async_copy(entry_tx.at[data], entry_rx.at[data], recv.at[ENTRY]).start()
+
+    pl.when(pipe == 0)(lambda: weights_out(DNA))
     wait_bytes(vec_all, recv.at[VEC])
 
     @pl.when(pipe > 0)
     def _():
         remote(vec_all, vec_next, VECN, place(chan, data, pipe - 1)).start()
 
-    @pl.when(pipe == 0)
-    def _():
-        wait_bytes(tok_rx, recv.at[TOK])
-        x = turn_in(tok_rx)
-        res[...] = x.astype(bf16)
-        hat1, inv1 = norm_stats(x)
-        hat1_s[...] = hat1
-        inv1_s[...] = jnp.broadcast_to(inv1, (rows, LANES))
-        turn_out(hat1 * full_row(vec_all, 0) + full_row(vec_all, 1), tx1)
-        to_members(lambda p: tx1.at[p], rx1, slot_me, A1 + own_micro)
-
-    weights_out(UPA)
-    pl.when(pipe == 0)(lambda: weights_out(UPB))
 
     @pl.when(pipe > 0)
     def _():
-        weights_all((weights_out,), UPB, DNA, DNB)
+        weights_all((weights_out,), UPA, UPB, DNA, DNB)
 
     def toeplitz_one(h):
         full = jnp.broadcast_to(kern_s[pl.ds(h, 1), :], (LANES, wide))
         full = pltpu.roll(full, 0, 1, stride=1, stride_axis=0).astype(bf16)
-        far[h] = full[:, : z.length]
         for d in range(z.blocks):
             near[h, d * LANES : (d + 1) * LANES, :] = full[:, d * LANES : (d + 1) * LANES]
 
     each_channel(toeplitz_one, 2)
+
+    def reversed_one(h):
+        full = jnp.broadcast_to(lag_s[pl.ds(h, 1), :], (LANES, wide))
+        full = pltpu.roll(full, 0, 1, stride=1, stride_axis=0).astype(bf16)
+        for d in range(z.blocks):
+            at = (z.blocks - 1 - d) * LANES
+            far[h, d * LANES : (d + 1) * LANES, :] = full[:, at : at + LANES]
+
+    def reversed_kernel():
+        down = lax.broadcasted_iota(jnp.int32, (LANES, LANES), 0)
+        along = lax.broadcasted_iota(jnp.int32, (LANES, LANES), 1)
+        flip = jnp.where(down + along == LANES - 1, 1.0, 0.0).astype(bf16)
+        tiles = [
+            dot(kern_s[:, t * LANES : (t + 1) * LANES].astype(bf16), flip)
+            for t in reversed(range(z.blocks + 1))
+        ]
+        lag_s[...] = shifted(jnp.concatenate(tiles, axis=1), wide - (2 * LANES - 1))
+        each_channel(reversed_one, 2)
+
     weights_all(forward_steps, GLU)
 
     @pl.when(pipe > 0)
@@ -571,14 +614,14 @@
 
     weights_core(GLU)
 
-    def lane_tiles(ref, m):
+    def lane_tiles(pieces, size):
         tiles = []
         for i in range(z.blocks):
             lo, hi = i * LANES, (i + 1) * LANES
             tile = None
-            for k in range(lo // tok, -(-hi // tok)):
-                piece = shifted(ref[m * z.slots + k].astype(f32), k * tok - lo)
-                first = max(0, k * tok - lo)
+            for k in range(lo // size, -(-hi // size)):
+                piece = shifted(pieces(k).astype(f32), k * size - lo)[:, 0:LANES]
+                first = max(0, k * size - lo)
                 if tile is None:
                     tile = piece
                 else:
@@ -630,9 +673,18 @@
         return jnp.concatenate(parts, axis=1).astype(bf16)
 
     for m in range(z.micros):
-        wait_bytes(rx1.at[pl.ds(m * z.slots, z.slots)], recv.at[A1 + m])
-        for i, tile in enumerate(lane_tiles(rx1, m)):
-            masked_store(xs, pad_rows, m, i, tile)
+        @pl.when(pipe == 0)
+        def _():
+            if m == 0:
+                wait_bytes(entry_rx, recv.at[ENTRY])
+            for i, tile in enumerate(lane_tiles(lambda k: entry_rx[k, m], z.local)):
+                masked_store(xs, pad_rows, m, i, tile)
+
+        @pl.when(pipe > 0)
+        def _():
+            wait_bytes(rx1.at[pl.ds(m * z.slots, z.slots)], recv.at[A1 + m])
+            for i, tile in enumerate(lane_tiles(lambda k: rx1[m * z.slots + k], tok)):
+                masked_store(xs, pad_rows, m, i, tile)
 
         def conv_one(h):
             ys[pl.ds(h, z.conv_rows, stride=z.ch), :] = dot(windows(xs, m, h, True), near[h])
@@ -646,12 +698,17 @@
         lane_pieces(tiles, m, tx2)
         to_micro(m, tx2, rx2, A2)
 
+    pl.when(pipe == last)(reversed_kernel)
+
     @pl.when(pipe == 0)
     def _():
-        weights_out(DNA)
+        wait_bytes(tok_rx, recv.at[TOK])
+        res[...] = turn_in(tok_rx).astype(bf16)
         weights_out(DNB)
         weights_all(forward_steps, UPA, UPB)
         weights_all((weights_core,), UPA)
+        weights_all(forward_steps, DNA)
+        weights_all((weights_core,), UPB)
 
     wait_bytes(rx2, recv.at[A2])
     gated_s[...] = turn_in(rx2).astype(bf16)
@@ -663,18 +720,16 @@
     )
     val_s[...] = value
     sig_s[...] = sig
-    pl.when(pipe > 0)(lambda: wait_bytes(res, recv.at[RES]))
+
+    @pl.when(pipe > 0)
+    def _():
+        wait_bytes(res, recv.at[RES])
+
     mid = res[...].astype(f32) + value * sig
     hat2, inv2 = norm_stats(mid)
     hat2_s[...] = hat2
     inv2_s[...] = jnp.broadcast_to(inv2, (rows, LANES))
     ffn_s[...] = (hat2 * full_row(vec_all, 2) + full_row(vec_all, 3)).astype(bf16)
-
-    @pl.when(pipe == 0)
-    def _():
-        weights_core(UPB)
-        weights_all(forward_steps, DNA)
-
     weights_all((weights_here,), UPA, UPB)
     ffn_in = ffn_s[...]
     for c in range(z.peers):
@@ -685,8 +740,8 @@
 
     @pl.when(pipe == 0)
     def _():
+        weights_all(forward_steps, DNB)
         weights_core(DNA)
-        weights_all(forward_steps, DNB)
         weights_core(DNB)
 
     weights_all((weights_here,), DNA, DNB)
@@ -711,8 +766,10 @@
         to_peers(lambda c: ffn_s, fi, FI)
         to_peers(lambda c: act_s.at[c], ac, AC)
 
-    def top_rows():
-        to_peers(lambda c: gtop, bg, BG)
+    def top_rows(part):
+        count = width // 2
+        where = pl.ds(part * count, count)
+        to_peers(lambda c: gtop.at[:, where], bg.at[:, :, where], BG + part)
 
     def hidden_rows():
         to_peers(lambda c: gh_s.at[c], gh, GH)
@@ -723,6 +780,8 @@
     @pl.when(pipe < last)
     def _():
         to_peers(lambda c: lay_t.at[c], hid_rx, HID)
+        reversed_kernel()
+        wait_bytes(hid_rx, recv.at[HID])
         forward_rows()
 
     @pl.when(pipe == last)
@@ -748,6 +807,7 @@
             for r, row in enumerate(pair):
                 vgn_s[c, r : r + 1, :] = row[:, (c // 2) * LANES : (c // 2 + 1) * LANES]
 
+    pl.when(pipe == 0)(lambda: top_rows(0))
     grad_low = gtop[...]
     grad_top = grad_low.astype(f32)
     grad_ffn = None
@@ -774,7 +834,7 @@
         gp_s[2 * j] = jnp.where(first_half, gv, gg).astype(bf16)
         gp_s[2 * j + 1] = jnp.where(first_half, gg, gv).astype(bf16)
     pl.when(pipe > 0)(lambda: remote(mid_s, mid_rx, MID, place(chan, data, pipe - 1)).start())
-    pl.when(pipe == 0)(top_rows)
+    pl.when(pipe == 0)(lambda: top_rows(1))
 
     @pl.when(pipe < last)
     def _():
@@ -784,11 +844,13 @@
 
     for m in range(z.micros):
         wait_bytes(rx3.at[pl.ds(m * z.slots, z.slots)], recv.at[A3 + m])
-        for i, tile in enumerate(lane_tiles(rx3, m)):
+        if m == 0:
+            pl.when(pipe == 0)(hidden_rows)
+        for i, tile in enumerate(lane_tiles(lambda k: rx3[m * z.slots + k], tok)):
             masked_store(gs, 0, m, i, tile * gelu_slope(conv_out[m * z.blocks + i]))
 
         def back_one(h):
-            ys[pl.ds(h, z.conv_rows, stride=z.ch), :] = dot_nt(windows(gs, m, h, False), far[h])
+            ys[pl.ds(h, z.conv_rows, stride=z.ch), :] = dot(windows(gs, m, h, False), far[h])
 
         each_channel(back_one, ch)
         tiles = [
@@ -798,8 +860,13 @@
         pl.when(pipe == 0)(lambda: to_micro(m, tx4, rx4, A4))
         pl.when(pipe > 0)(lambda: to_micro(m, tx4, rx4n, A4N, pipe - 1))
 
-    pl.when(pipe > 0)(top_rows)
-    hidden_rows()
+
+    @pl.when(pipe > 0)
+    def _():
+        top_rows(0)
+        top_rows(1)
+        hidden_rows()
+
 
     @pl.when(pipe == last)
     def _():
@@ -814,13 +881,17 @@
     )
 
     def product(t):
-        left, lp, right, rp, n_left, n_right, part, krx, *_ = grads[t]
+        left, lp, right, rp, n_left, n_right, local, krx, *_ = grads[t]
         wait_bytes(left, recv.at[lp])
-        wait_bytes(right, recv.at[rp])
-        part[...] = dot_tn(left[...].reshape(many, n_left), right[...].reshape(many, n_right))
+        if rp == BG:
+            for part in range(2):
+                wait_bytes(bg.at[:, :, pl.ds(0, width // 2)], recv.at[BG + part])
+        else:
+            wait_bytes(right, recv.at[rp])
+        local[...] = dot_tn(left[...].reshape(many, n_left), right[...].reshape(many, n_right))
         half = n_left // 2
         other = pl.ds(pl.multiple_of((1 - core) * half, half), half)
-        remote(part.at[other], krx, GRADS + 3 * t, sibling).start()
+        remote(local.at[other], krx, GRADS + 3 * t, sibling).start()
 
     def chip_sum(t):
         _, _, _, _, n_left, _, part, krx, lsend, lrx, _ = grads[t]
@@ -873,10 +944,10 @@
 
     @pl.when(pipe == 0)
     def _():
+        hat, inv = norm_stats(res[...].astype(f32))
         wait_bytes(rx4, recv.at[A4])
         grad_in = jnp.where(row_ok, turn_in(rx4), 0.0)
-        hat = hat1_s[...]
-        grad_res = mid_s[...] + norm_back(grad_in, hat, inv1_s[:, 0:1], full_row(vec_all, 0))
+        grad_res = mid_s[...] + norm_back(grad_in, hat, inv, full_row(vec_all, 0))
         turn_out(grad_res, ig_t)
         to_peers(lambda c: ig_t.at[c], ig_rx, IG)
         pair = (
@@ -1014,7 +1085,7 @@
                 tiles.append(tile)
             target[m] = jnp.concatenate(tiles, axis=1)[:, 0:count].astype(bf16)
 
-    wait_bytes(hid_rx, recv.at[HID])
+    pl.when(pipe == last)(lambda: wait_bytes(hid_rx, recv.at[HID]))
     collect(hid_rx, hid_out)
     wait_bytes(ig_rx, recv.at[IG])
     collect(ig_rx, ig_out)
@@ -1056,9 +1127,12 @@
 
     weights_all((weights_sent,), GLU, UPA, UPB, DNA, DNB)
     for ref, phase in (
-        (vec_all, VEC), (hid_rx, HID), (ga, GA), (fi, FI), (ac, AC), (bg, BG), (gh, GH), (gp, GP),
+        (vec_all, VEC), (hid_rx, HID), (ga, GA), (fi, FI), (ac, AC), (gh, GH), (gp, GP),
     ):
         wait_bytes(ref.at[pl.ds(0, z.peers - 1)], send.at[phase])
+    for part in range(2):
+        sent = bg.at[pl.ds(0, z.peers - 1), :, pl.ds(0, width // 2)]
+        wait_bytes(sent, send.at[BG + part])
     for ref, phase in ((rx2, A2), (rx3, A3 + own_micro), (vrx, VG)):
         wait_bytes(ref.at[pl.ds(0, z.members - 1)], send.at[phase])
     wait_bytes(modes_rx.at[pl.ds(0, z.groups - 1)], send.at[MODES])
@@ -1071,7 +1145,9 @@
     def _():
         wait_bytes(tok_rx.at[pl.ds(0, z.peers - 1)], send.at[TOK])
         wait_bytes(ig_rx.at[pl.ds(0, z.peers - 1)], send.at[IG])
-        for ref, phase in ((rx1, A1 + own_micro), (rx4, A4), (vnrx, VGN)):
+        wait_bytes(stat_rx.at[pl.ds(0, z.peers - 1)], send.at[STAT])
+        wait_bytes(entry_rx.at[pl.ds(0, z.groups - 1)], send.at[ENTRY])
+        for ref, phase in ((rx4, A4), (vnrx, VGN)):
             wait_bytes(ref.at[pl.ds(0, z.members - 1)], send.at[phase])
 
     @pl.when(pipe == last)
@@ -1160,7 +1236,7 @@
         out_specs=[vmem] * 10,
         scratch_shapes=[
             peer_tiles, peer_tiles, v((16, LANES), f32), v((ch, length, LANES)),
-            v((ch, LANES, length)), v((ch, LANES), f32), v((40, LANES), f32),
+            v((ch, length, LANES)), v((ch, LANES), f32), v((40, LANES), f32),
             peer_tiles, peer_tiles, v((micros * z.stack, LANES), f32),
             v((micros * z.stack, LANES), f32),
             v((2 * padded, length)), v((2, nh, LANES), f32),
@@ -1179,17 +1255,19 @@
             v((2, n, chan_width, w)), v((n, w, hidden)),
             v((n, hidden, w)), peer_tiles, peer_tiles, rows_full, rows_full,
         ]
-        + [exchange] * 10
+        + [exchange] * 9
         + [
             v((z.micros * z.blocks, z.ch, LANES), f32), v((z.conv_rows * z.ch, LANES), f32),
-            rows_wide, side, rows_wide, side, rows_wide, side,
+            rows_wide, side, rows_wide, side,
             rows_wide, rows_wide, v((n, r, hidden), f32),
             rows_full, rows_full, v((n, r, hidden)), v((n, r, hidden)), v((n, r, LANES)),
             rows_full, peer_tiles, peer_tiles, peer_tiles, rows_wide, rows_wide,
+            v((8, z.over), f32), v((n, 8, z.over), f32),
+            v((z.groups, micros, ch, z.over)), v((z.groups, micros, ch, z.over)),
             small, small, small,
             v((n, r, w)), v((n, r, w)), v((n, r, hidden)), v((n, r, w)), v((n, r, hidden)),
             v((n, r, LANES)), v((z.members, 8, LANES), f32), v((z.members, 8, LANES), f32),
-            pltpu.SemaphoreType.DMA((64,)), pltpu.SemaphoreType.DMA((64,)),
+            pltpu.SemaphoreType.DMA((68,)), pltpu.SemaphoreType.DMA((68,)),
         ],
         compiler_params=pltpu.CompilerParams(
             collective_id=0, has_side_effects=True, vmem_limit_bytes=60 * 2**20

time: 177 us -> 169 us (0.955)
  Pallas kernels: 176 us -> 168 us
    pallas_call x1, Pallas kernels: 173 us -> 166 us  [body(): pl.pallas_call(lambda *refs: main_kernel(z, *refs), out_shape=results, in...]
where the time goes in v6:
time: 169 us
  Pallas kernels  168 us (99%)
    pallas_call x1, Pallas kernels, body(): pl.pallas_call(lambda *refs: main_kernel(z, *refs), out_shape=results, in...  166 us

profile of v6, /device:TPU:1, one launch (start us, length us, event | category | flops | bytes accessed | tf_op | source)
XLA Modules:
  0.0 169.2 jit_solution(3476163422923755400)
XLA Ops:
  0.6 165.9 %layers.1 = (bf16[2,64,288]{2,1,0:T(8,128)(2,1)}, bf16[2,64,288]{2,1,0:T(8,128)(2,1)}, f32[4,64]{1,0:T(4,128)}, f32[8,32,64]{2,1,0:T(8,128)}, f32[2,64,512]{2,1,...) custom-call(s32[2,2]{1,0:T(2,128)} %refs_0_.1, ...), custom_call_target="tpu_custom_call" | custom-call | tf_op jit(solution)/shard_map/layers/pallas_call | solution.py:1232
  166.6 2.5 %finish.1 = (bf16[2,64,288]{2,1,0:T(8,128)(2,1)}, bf16[2,64,288]{2,1,0:T(8,128)(2,1)}, f32[4,64]{1,0:T(4,128)}, f32[8,32,64]{2,1,0:T(8,128)}, f32[2,64,512]{2,1,...) custom-call(bf16[2,64,288]{2,1,0:T(8,128)(2,1)} %get-tuple-element.3, ...), custom_call_target="tpu_custom_call" | custom-call | tf_op jit(solution)/shard_map/finish/pallas_call | solution.py:1281

commit v7 on v6

--- a/solution.py
+++ b/solution.py
@@ -761,6 +761,20 @@
         to_section(lambda p: tx1n.at[p], rx1, slot_me, A1 + own_micro, pipe + 1)
         remote(lay_s, res, RES, place(chan, data, pipe + 1)).start()
 
+    def collect(source, target):
+        count = tok * z.quarters
+        for m in range(z.micros):
+            tiles = []
+            for i in range(-(-count // LANES)):
+                lo, hi = i * LANES, min((i + 1) * LANES, count)
+                tile = None
+                for q in range(lo // tok, -(-hi // tok)):
+                    piece = shifted(source[m * z.quarters + q].astype(f32), q * tok - lo)
+                    first = max(0, q * tok - lo)
+                    tile = piece if tile is None else jnp.where(spot >= first, piece, tile)
+                tiles.append(tile)
+            target[m] = jnp.concatenate(tiles, axis=1)[:, 0:count].astype(bf16)
+
     def forward_rows():
         to_peers(lambda c: gated_s, ga, GA)
         to_peers(lambda c: ffn_s, fi, FI)
@@ -783,6 +797,7 @@
         reversed_kernel()
         wait_bytes(hid_rx, recv.at[HID])
         forward_rows()
+        collect(hid_rx, hid_out)
 
     @pl.when(pipe == last)
     def _():
@@ -842,6 +857,19 @@
         to_section_peers(lambda c: ign_t.at[c], ig_rx, IG, pipe + 1)
         to_section(lambda p: vgn_s.at[p // z.groups], vnrx, me, VGN, pipe + 1)
 
+    rows_of = [
+        jnp.sum(grad_ffn * hat2, axis=0, keepdims=True),
+        jnp.sum(grad_ffn, axis=0, keepdims=True),
+        jnp.sum(grad_top, axis=0, keepdims=True),
+    ]
+    for c in range(z.peers):
+        j = c // 2
+        for r, row in enumerate(rows_of):
+            vg_s[c, r : r + 1, :] = row[:, j * LANES : (j + 1) * LANES]
+        vg_s[c, 3:4, :] = jnp.sum(gp_s[c].astype(f32), axis=0, keepdims=True)
+        up_row = jnp.sum(gh_s[c].astype(f32), axis=0, keepdims=True)
+        for r in range(per):
+            vg_s[c, 4 + r : 5 + r, :] = up_row[:, r * LANES : (r + 1) * LANES]
     for m in range(z.micros):
         wait_bytes(rx3.at[pl.ds(m * z.slots, z.slots)], recv.at[A3 + m])
         if m == 0:
@@ -909,6 +937,7 @@
         final[own, :] = lsend[...].astype(f32) + lrx[...].astype(f32)
         remote(final.at[own], final.at[own], GRADS + 3 * t + 2, sibling).start()
 
+    to_members(lambda p: vg_s.at[p // z.groups], vrx, me, VG)
     product(0)
 
     def lag_one(h):
@@ -962,20 +991,6 @@
     chip_sum(1)
     chip_sum(2)
 
-    rows_of = [
-        jnp.sum(grad_ffn * hat2, axis=0, keepdims=True),
-        jnp.sum(grad_ffn, axis=0, keepdims=True),
-        jnp.sum(grad_top, axis=0, keepdims=True),
-    ]
-    for c in range(z.peers):
-        j = c // 2
-        for r, row in enumerate(rows_of):
-            vg_s[c, r : r + 1, :] = row[:, j * LANES : (j + 1) * LANES]
-        vg_s[c, 3:4, :] = jnp.sum(gp_s[c].astype(f32), axis=0, keepdims=True)
-        up_row = jnp.sum(gh_s[c].astype(f32), axis=0, keepdims=True)
-        for r in range(per):
-            vg_s[c, 4 + r : 5 + r, :] = up_row[:, r * LANES : (r + 1) * LANES]
-    to_members(lambda p: vg_s.at[p // z.groups], vrx, me, VG)
     both = dot_nt(high_low(lag_s[:, 0 : z.length]), table[...])
     grad_spec = both[0:ch] + both[ch : 2 * ch]
     gk = (grad_spec[:, 0:padded], grad_spec[:, padded : 2 * padded])
@@ -1071,22 +1086,12 @@
     for t in range(3):
         both_chips(t)
 
-    def collect(source, target):
-        count = tok * z.quarters
-        for m in range(z.micros):
-            tiles = []
-            for i in range(-(-count // LANES)):
-                lo, hi = i * LANES, min((i + 1) * LANES, count)
-                tile = None
-                for q in range(lo // tok, -(-hi // tok)):
-                    piece = shifted(source[m * z.quarters + q].astype(f32), q * tok - lo)
-                    first = max(0, q * tok - lo)
-                    tile = piece if tile is None else jnp.where(spot >= first, piece, tile)
-                tiles.append(tile)
-            target[m] = jnp.concatenate(tiles, axis=1)[:, 0:count].astype(bf16)
-
-    pl.when(pipe == last)(lambda: wait_bytes(hid_rx, recv.at[HID]))
-    collect(hid_rx, hid_out)
+
+    @pl.when(pipe == last)
+    def _():
+        wait_bytes(hid_rx, recv.at[HID])
+        collect(hid_rx, hid_out)
+
     wait_bytes(ig_rx, recv.at[IG])
     collect(ig_rx, ig_out)
     wait_bytes(vrx, recv.at[VG])

time: 169 us -> 168 us (level)
  no operation moved by 1% of the time
where the time goes in v7:
time: 168 us
  Pallas kernels  167 us (99%)
    pallas_call x1, Pallas kernels, body(): pl.pallas_call(lambda *refs: main_kernel(z, *refs), out_shape=results, in...  164 us

profile of v7, /device:TPU:1, one launch (start us, length us, event | category | flops | bytes accessed | tf_op | source)
XLA Modules:
  0.0 167.7 jit_solution(5416708430534993804)
XLA Ops:
  0.6 164.4 %layers.1 = (bf16[2,64,288]{2,1,0:T(8,128)(2,1)}, bf16[2,64,288]{2,1,0:T(8,128)(2,1)}, f32[4,64]{1,0:T(4,128)}, f32[8,32,64]{2,1,0:T(8,128)}, f32[2,64,512]{2,1,...) custom-call(s32[2,2]{1,0:T(2,128)} %refs_0_.1, ...), custom_call_target="tpu_custom_call" | custom-call | tf_op jit(solution)/shard_map/layers/pallas_call | solution.py:1237
  165.1 2.5 %finish.1 = (bf16[2,64,288]{2,1,0:T(8,128)(2,1)}, bf16[2,64,288]{2,1,0:T(8,128)(2,1)}, f32[4,64]{1,0:T(4,128)}, f32[8,32,64]{2,1,0:T(8,128)}, f32[2,64,512]{2,1,...) custom-call(bf16[2,64,288]{2,1,0:T(8,128)(2,1)} %get-tuple-element.3, ...), custom_call_target="tpu_custom_call" | custom-call | tf_op jit(solution)/shard_map/finish/pallas_call | solution.py:1286
